TPU v7x, 128 devices: a whole 4x4x4 slice. The times are simulated.
128 devices in a mesh: ctx: 32 (over z, x, core), kvh: 4 (over y).
Axes of the slice: x: 4, y: 4, z: 4, core: 2. Of those that a mesh axis runs over, the one named last changes fastest.
Arguments:
- queries: bfloat16 [256, 16384], P('ctx', 'kvh'), may hold values from -96 to 96
- cache: bfloat16 [8, 65536, 8, 256], P(None, 'ctx', 'kvh'), may hold values from -6 to 6, as said below
- new_kv: bfloat16 [8, 32, 8, 256], P(None, None, 'kvh'), may hold values from -6 to 6
- lengths: int32 [8], replicated, may hold values from 26625 to 65536, as said below
- out_weight: bfloat16 [16384, 16384], P('kvh', 'ctx'), may hold values from -3 to 3
Outputs:
- projected: bfloat16 [256, 16384], P('kvh', 'ctx')
Inputs may be any that keep to these rules, and one draw needn't show every extreme that they name: `lengths`: the longest request's length equals 65536. `cache`: entries at positions at or beyond a request's length are never read.
All inputs are finite; a program needn't handle non-finite values.
Results may differ from a plain program's by a relative error of at most 0.0063.
Values may be sent and summed in bfloat16 or wider, within the bound.
No kernel may reach another device: no remote copies, remote signals or barrier semaphores. Data moves between devices by JAX's collectives and lax.ppermute only.
A program may use at most 320 MiB of HBM per device.

v0:
```python
import jax
import jax.numpy as jnp
from jax import lax
from jax.sharding import PartitionSpec as P

QH = 128
KV_HEADS = 8
HD = 128
REQS = 8
NEW = 32


def partial_scores(qblock, keys, values, valid):
    scores = jnp.dot(qblock, keys.T, preferred_element_type=jnp.float32) * HD ** (-0.5)
    scores = jnp.where(valid, scores, -1e30)
    top = jnp.max(scores, axis=1)
    weights = jnp.where(valid, jnp.exp(scores - top[:, None]), 0.0)
    total = jnp.sum(weights, axis=1)
    summed = jnp.dot(weights.astype(jnp.bfloat16), values, preferred_element_type=jnp.float32)
    return (top, total, summed)


def cache_partials(gathered, cache, lengths, offset):
    slot = cache.shape[1]
    kv_local = cache.shape[2]
    group = QH // KV_HEADS
    grouped = gathered.reshape(REQS, NEW, kv_local, group * HD)
    positions = offset + jnp.arange(slot, dtype=jnp.int32)

    def one(pair):
        req = pair // kv_local
        head = pair % kv_local
        qblock = grouped[req, :, head].reshape(NEW * group, HD)
        valid = (positions < lengths[req])[None, :]
        top, total, summed = partial_scores(
            qblock, cache[req, :, head, :HD], cache[req, :, head, HD:], valid
        )
        normal = (summed / jnp.maximum(total, 1.0)[:, None]).astype(jnp.bfloat16)
        return (top, total, normal)

    tops, totals, normals = lax.map(one, jnp.arange(REQS * kv_local, dtype=jnp.int32))
    tops = (
        tops.reshape(REQS, kv_local, NEW, group)
        .transpose(0, 2, 1, 3)
        .reshape(REQS * NEW, kv_local * group)
    )
    totals = (
        totals.reshape(REQS, kv_local, NEW, group)
        .transpose(0, 2, 1, 3)
        .reshape(REQS * NEW, kv_local * group)
    )
    normals = (
        normals.reshape(REQS, kv_local, NEW, group, HD)
        .transpose(0, 2, 1, 3, 4)
        .reshape(REQS * NEW, kv_local * group, HD)
    )
    return (tops, totals, normals)


def new_partials(q_rows, row_start, new_kv):
    count = q_rows.shape[0]
    kv_local = new_kv.shape[2]
    group = QH // KV_HEADS
    row_ids = row_start + jnp.arange(count, dtype=jnp.int32)
    request = row_ids // NEW
    token = row_ids % NEW
    grouped = q_rows.reshape(count, kv_local, group, HD)
    picked = new_kv[request]
    scores = jnp.einsum(
        "rkgd,rnkd->rkgn", grouped, picked[..., :HD], preferred_element_type=jnp.float32
    ) * HD ** (-0.5)
    valid = (jnp.arange(NEW, dtype=jnp.int32)[None, :] <= token[:, None])[:, None, None, :]
    scores = jnp.where(valid, scores, -1e30)
    top = jnp.max(scores, axis=3)
    weights = jnp.where(valid, jnp.exp(scores - top[..., None]), 0.0)
    total = jnp.sum(weights, axis=3)
    summed = jnp.einsum(
        "rkgn,rnkd->rkgd",
        weights.astype(jnp.bfloat16),
        picked[..., HD:],
        preferred_element_type=jnp.float32,
    )
    return (
        top.reshape(count, kv_local * group),
        total.reshape(count, kv_local * group),
        summed.reshape(count, kv_local * group, HD),
    )


def combine_stacked(tops, totals, sums):
    best = jnp.max(tops, axis=0)
    factor = jnp.exp(tops - best[None])
    total = jnp.sum(factor * totals, axis=0)
    summed = jnp.sum(factor[..., None] * sums, axis=0)
    return (summed / total[..., None]).astype(jnp.bfloat16).reshape(summed.shape[0], -1)


def on_device(queries, cache, new_kv, lengths, out_weight):
    per_rows = queries.shape[0]
    offset = lax.axis_index("ctx") * cache.shape[1]
    gathered = lax.all_gather(queries, "ctx", axis=0, tiled=True)
    tops, totals, normals = cache_partials(gathered, cache, lengths, offset)
    got_normals = lax.all_to_all(normals, "ctx", split_axis=0, concat_axis=0, tiled=True)
    got_tops, got_totals = (
        lax.all_to_all(tops, "ctx", split_axis=0, concat_axis=0, tiled=True),
        lax.all_to_all(totals, "ctx", split_axis=0, concat_axis=0, tiled=True),
    )
    sources = lax.axis_size("ctx")
    got_tops = got_tops.reshape(sources, per_rows, -1)
    got_totals = got_totals.reshape(sources, per_rows, -1)
    got_normals = got_normals.reshape(sources, per_rows, got_normals.shape[1], HD)
    got_sums = got_totals[..., None] * got_normals.astype(jnp.float32)
    own_top, own_total, own_sum = new_partials(queries, lax.axis_index("ctx") * per_rows, new_kv)
    own_rows = combine_stacked(
        jnp.concatenate([got_tops, own_top[None]], axis=0),
        jnp.concatenate([got_totals, own_total[None]], axis=0),
        jnp.concatenate([got_sums, own_sum[None]], axis=0),
    )
    attended = lax.all_gather(own_rows, "ctx", axis=0, tiled=True)
    result = lax.psum_scatter(
        jnp.dot(attended, out_weight, preferred_element_type=jnp.float32),
        "kvh",
        scatter_dimension=0,
        tiled=True,
    )
    return result.astype(jnp.bfloat16)


def solution(mesh):
    placed = (
        P("ctx", "kvh"),
        P(None, "ctx", "kvh", None),
        P(None, None, "kvh", None),
        P(),
        P("kvh", "ctx"),
    )
    return jax.shard_map(
        on_device, mesh=mesh, in_specs=placed, out_specs=P("kvh", "ctx"), check_vma=False
    )
```

profile of v0, /device:TPU:0, one launch (start us, length us, event | category | flops | bytes accessed | tf_op | source)
XLA Modules:
  0.0 377.3 jit_solution(1028680727790954980)
XLA Ops:
  7.3 15.3 %copy.14 = bf16[8,2048,2,256]{3,1,2,0:T(8,128)(2,1)} copy(bf16[8,2048,2,256]{3,2,1,0:T(2,128)(2,1)} %param.8) | data formatting | bytes 33554432
  22.6 33.4 %all-gather.3.cloned.1.call-done = bf16[256,4096]{1,0:T(8,128)(2,1)} async-done(((bf16[8,4096]{1,0:T(8,128)(2,1)}), bf16[256,4096]{1,0:T(8,128)(2,1)}) %all-gather.3.cloned.1.call-update) | async-done | bytes 2097168 | tf_op jit(solution)/shard_map/all_gather | solution.py:101
  56.1 3.3 reshape.169
  59.4 2.2 copy.13
  61.6 178.1 %while.17 = (s32[]{:T(128)}, f32[16,512]{1,0:T(8,128)S(1)}, f32[16,512]{1,0:T(8,128)S(1)}, bf16[16,512,128]{2,1,0:T(8,128)(2,1)}, s32[16]{0:T(128)S(1)}, /*index...) while((s32[]{:T(128)}, f32[16,512]{1,0:T(8,128)S(1)}, ...), condition=%wide.region_3.4_spmd.clone, body=%wide.region_0.3_spmd.clone.sunk | while | flops 550637056 | bytes 14449104 | solution.py:41
  69.9 2.7 fusion.68
  78.1 1.9 fusion.66
  81.1 2.7 fusion.68
  89.2 1.9 fusion.66
  92.2 2.7 fusion.68
  103.3 2.7 fusion.68
  114.5 2.7 fusion.68
  125.6 2.7 fusion.68
  136.7 2.7 fusion.68
  147.9 2.7 fusion.68
  159.0 2.7 fusion.68
  170.2 2.7 fusion.68
  181.3 2.7 fusion.68
  192.4 2.7 fusion.68
  203.6 2.7 fusion.68
  214.7 2.7 fusion.68
  225.8 2.7 fusion.68
  236.9 2.7 fusion.68
  241.0 5.2 %all-to-all-start = ((f32[32,1,256]{2,1,0:T(1,128)}), f32[32,1,256]{2,1,0:T(1,128)S(1)}, u32[]{:S(2)}, u32[]{:S(2)}) async-start(f32[32,1,256]{2,1,0:T(1,128)} %reshape.186), calls=%async_computation | async-start | bytes 65536 | tf_op jit(solution)/shard_map/all_to_all | solution.py:105
  247.5 6.1 %all-to-all-done = f32[32,1,256]{2,1,0:T(1,128)S(1)} async-done(((f32[32,1,256]{2,1,0:T(1,128)}), f32[32,1,256]{2,1,0:T(1,128)S(1)}, u32[]{:S(2)}, u32[]{:S(2)}) %all-to-all-start) | async-done | bytes 32800 | tf_op jit(solution)/shard_map/all_to_all | solution.py:105
  253.7 3.9 %all-to-all-start.1 = ((f32[32,1,256]{2,1,0:T(1,128)}), f32[32,1,256]{2,1,0:T(1,128)S(1)}, u32[]{:S(2)}, u32[]{:S(2)}) async-start(f32[32,1,256]{2,1,0:T(1,128)} %reshape.184), calls=%async_computation.1 | async-start | bytes 65536 | tf_op jit(solution)/shard_map/all_to_all | solution.py:106
  259.3 5.6 %all-to-all-done.1 = f32[32,1,256]{2,1,0:T(1,128)S(1)} async-done(((f32[32,1,256]{2,1,0:T(1,128)}), f32[32,1,256]{2,1,0:T(1,128)S(1)}, u32[]{:S(2)}, u32[]{:S(2)}) %all-to-all-start.1) | async-done | bytes 32800 | tf_op jit(solution)/shard_map/all_to_all | solution.py:106
  264.9 4.0 %all-to-all-start.2 = ((bf16[256,32,128]{2,1,0:T(8,128)(2,1)}), bf16[256,32,128]{2,1,0:T(8,128)(2,1)S(1)}, u32[]{:S(2)}, u32[]{:S(2)}) async-start(bf16[256,32,128]{2,1,0:T(8,128)(2,1)} %bitcast.59), calls=%async_computation.2 | async-start | bytes 4194304 | tf_op jit(solution)/shard_map/all_to_all | solution.py:103
  273.7 25.3 %all-to-all-done.2 = bf16[256,32,128]{2,1,0:T(8,128)(2,1)S(1)} async-done(((bf16[256,32,128]{2,1,0:T(8,128)(2,1)}), bf16[256,32,128]{2,1,0:T(8,128)(2,1)S(1)}, u32[]{:S(2)}, u32[]{:S(2)}) %all-to-all-start.2) | async-done | bytes 2097184 | tf_op jit(solution)/shard_map/all_to_all | solution.py:103
  302.4 41.1 %all-gather.5.cloned.1.call-done = bf16[256,4096]{1,0:T(8,128)(2,1)} async-done(((bf16[8,4096]{1,0:T(8,128)(2,1)}), bf16[256,4096]{1,0:T(8,128)(2,1)}) %all-gather.5.cloned.1.call-update) | async-done | bytes 2097168 | tf_op jit(solution)/shard_map/all_gather | solution.py:119
  343.5 4.9 %fusion.53 = f32[256,512]{1,0:T(8,128)} fusion(bf16[256,4096]{1,0:T(8,128)(2,1)} %all-gather.5.cloned.1.call-done, bf16[4096,512]{1,0:T(8,128)(2,1)} %param.11), kind=kOutput, calls=%fused_computation.65 | convolution fusion | flops 1073741824 | bytes 6815744 | tf_op jit(solution)/shard_map/dot_general | solution.py:121
  348.4 20.8 %reduce-scatter.2.cloned.1.call-done = f32[64,512]{1,0:T(8,128)} async-done(((f32[256,512]{1,0:T(8,128)}), f32[64,512]{1,0:T(8,128)}) %reduce-scatter.2.cloned.1.call-update) | async-done | bytes 131088 | tf_op jit(solution)/shard_map/reduce_scatter | solution.py:120
  (210 shorter events, 104.8 us)
Async XLA Ops:
  6.5 262.5 %copy-start = (bf16[8,32,2,256]{3,2,1,0:T(2,128)(2,1)S(1)}, bf16[8,32,2,256]{3,2,1,0:T(2,128)(2,1)}, u32[]{:S(2)}) copy-start(bf16[8,32,2,256]{3,2,1,0:T(2,128)(2,1)} %param.9) | copy-start | bytes 786436
  6.5 49.5 %all-gather.3.cloned.1.call-start = ((), (), s32[]{:S(2)}) async-start(), calls=%async_computation.4 | async-start | bytes 2162688 | tf_op jit(solution)/shard_map/all_gather | solution.py:101
  22.6 39.0 %copy-start.3 = (s32[8]{0:T(128)S(1)}, s32[8]{0:T(128)}, u32[]{:S(2)}) copy-start(s32[8]{0:T(128)} %param.10) | copy-start | bytes 100
  239.8 17.8 %copy-start.1 = (bf16[16,512,128]{2,1,0:T(8,128)(2,1)S(1)}, bf16[16,512,128]{2,1,0:T(8,128)(2,1)}, u32[]{:S(2)}) copy-start(bf16[16,512,128]{2,1,0:T(8,128)(2,1)} %get-tuple-element.125) | copy-start | bytes 6291460
  241.0 12.6 %all-to-all-start = ((f32[32,1,256]{2,1,0:T(1,128)}), f32[32,1,256]{2,1,0:T(1,128)S(1)}, u32[]{:S(2)}, u32[]{:S(2)}) async-start(f32[32,1,256]{2,1,0:T(1,128)} %reshape.186), calls=%async_computation | async-start | bytes 65536 | tf_op jit(solution)/shard_map/all_to_all | solution.py:105
  253.7 11.3 %all-to-all-start.1 = ((f32[32,1,256]{2,1,0:T(1,128)}), f32[32,1,256]{2,1,0:T(1,128)S(1)}, u32[]{:S(2)}, u32[]{:S(2)}) async-start(f32[32,1,256]{2,1,0:T(1,128)} %reshape.184), calls=%async_computation.1 | async-start | bytes 65536 | tf_op jit(solution)/shard_map/all_to_all | solution.py:106
  257.5 12.9 %copy-start.2 = (bf16[8,4096]{1,0:T(8,128)(2,1)S(1)}, bf16[8,4096]{1,0:T(8,128)(2,1)}, u32[]{:S(2)}) copy-start(bf16[8,4096]{1,0:T(8,128)(2,1)} %param.7) | copy-start | bytes 196612
  264.9 34.0 %all-to-all-start.2 = ((bf16[256,32,128]{2,1,0:T(8,128)(2,1)}), bf16[256,32,128]{2,1,0:T(8,128)(2,1)S(1)}, u32[]{:S(2)}, u32[]{:S(2)}) async-start(bf16[256,32,128]{2,1,0:T(8,128)(2,1)} %bitcast.59), calls=%async_computation.2 | async-start | bytes 4194304 | tf_op jit(solution)/shard_map/all_to_all | solution.py:103
  269.0 74.5 %all-gather.5.cloned.1.call-start = ((), (), s32[]{:S(2)}) async-start(), calls=%async_computation.5 | async-start | bytes 2162688 | tf_op jit(solution)/shard_map/all_gather | solution.py:119
  302.4 66.8 %reduce-scatter.2.cloned.1.call-start = ((), (), s32[]{:S(2)}) async-start(), calls=%async_computation.6 | async-start | bytes 655360 | tf_op jit(solution)/shard_map/reduce_scatter | solution.py:120
Sparse Core Ops, SparseCore 0:
  9.6 46.4 all-gather.2
  302.5 40.9 all-gather.4
  348.5 20.6 reduce-scatter.1
where the time goes:
time: 380 us; the launch traced here: 377 us
  waiting for transfers between devices  133 us (35%)
  matrix products  79 us (21%)
  local copies, waits for them, and re-layouts  64.2 us (17%)
  loops' own time  40.7 us (11%)
  other arithmetic  33.7 us (9%)
  between operations  13.4 us (4%)
  starting transfers between devices  13.2 us (3%)
    dot_general x16, matrix products, partial_scores(): jnp.dot(weights.astype(jnp.bfloat16), values, preferred_element_type=jnp....  43.3 us
    all_gather x1, waiting for transfers between devices, on_device(): attended = lax.all_gather(own_rows, 'ctx', axis=0, tiled=True)  41.1 us
    another operation x1, loops' own time, cache_partials(): lax.map(one, jnp.arange(REQS * kv_local, dtype=jnp.int32))  40.7 us
    all_gather x1, waiting for transfers between devices, on_device(): gathered = lax.all_gather(queries, 'ctx', axis=0, tiled=True)  33.4 us
    dot_general x16, matrix products, partial_scores(): jnp.dot(qblock, keys.T, preferred_element_type=jnp.float32) * HD ** (-0.5)  30.3 us
    all_to_all x1, waiting for transfers between devices, on_device(): lax.all_to_all(normals, 'ctx', split_axis=0, concat_axis=0, tiled=True)  25.3 us
    reduce_scatter x1, waiting for transfers between devices, on_device(): lax.psum_scatter(jnp.dot(attended, out_weight, preferred_element_type=jnp...  20.8 us
    unnamed x15, local copies, waits for them, and re-layouts  19.9 us
  transfers between devices with their start and end apart: 6, of which 6 were waited for; matrix products, arithmetic and copies ran while one was open for 6% of the time, Pallas kernels for 0%

commit v1 on v0

v1 whole, which is shorter than its diff:
```python
import functools
import math

import jax
import jax.numpy as jnp
from jax import lax
from jax.experimental import pallas as pl
from jax.experimental.pallas import tpu as pltpu
from jax.sharding import PartitionSpec as P

KV_HEADS = 8
QH = 128
HD = 128
REQS = 8
NEW = 32
GROUP = QH // KV_HEADS
SIDE = 4
ROWS = 16
BLOCK = GROUP * ROWS
FEATS = GROUP * HD
WIDE = FEATS + HD
SCALE = HD ** (-0.5) * math.log2(math.e)
EMPTY = -1e30
F32, BF16 = jnp.float32, jnp.bfloat16
MIB = 2**20


def at(z, x, core):
    return ((z % SIDE) * SIDE + x % SIDE) * 2 + core


def places():
    return [(z, x, c) for z in range(SIDE) for x in range(SIDE) for c in range(2)]


def from_first(value, step):
    pairs = [(at(z, x + step, c) if c == 0 else at(z + step, x, c), at(z, x, c)) for z, x, c in places()]
    return lax.ppermute(value, "ctx", pairs)


def from_second(value, step):
    pairs = [(at(z + step, x, c) if c == 0 else at(z, x + step, c), at(z, x, c)) for z, x, c in places()]
    return lax.ppermute(value, "ctx", pairs)


def from_twin(value):
    return lax.ppermute(value, "ctx", [(at(z, x, 1 - c), at(z, x, c)) for z, x, c in places()])


def from_plane(value, step):
    return lax.ppermute(value, "kvh", [((s + step) % SIDE, s) for s in range(SIDE)])


def dot_nt(a, b):
    return lax.dot_general(a, b, (((1,), (1,)), ((), ())), preferred_element_type=F32)


def weigh(s):
    top = (jnp.max(s, axis=1, keepdims=True) * SCALE).astype(BF16).astype(F32)
    w = jnp.exp2(s * SCALE - top)
    return top, jnp.sum(w, axis=1, keepdims=True), w.astype(BF16)


def put_partial(out, index, top, total, summed):
    lane = lax.broadcasted_iota(jnp.int32, (ROWS, HD), 1)
    high = total.astype(BF16).astype(F32)
    low = total - high
    stats = jnp.zeros((ROWS, HD), F32)
    for g in range(GROUP):
        rows = slice(g * ROWS, (g + 1) * ROWS)
        out[index, :, g * HD : (g + 1) * HD] = summed[rows].astype(BF16)
        stats = jnp.where(lane == g, top[rows], stats)
        stats = jnp.where(lane == GROUP + g, high[rows], stats)
        stats = jnp.where(lane == 2 * GROUP + g, low[rows], stats)
    out[index, :, FEATS:] = stats.astype(BF16)


def assemble(info, own, other, held):
    z, x, core = info[0], info[1], info[2]
    for dz in range(SIDE):
        for dx in range(SIDE):
            chip = ((z + dz) % SIDE) * SIDE + (x + dx) % SIDE

            def place(zero, one, chip=chip):
                zero, one = zero.astype(F32), one.astype(F32)
                for g in range(GROUP):
                    cols = slice(g * HD, (g + 1) * HD)
                    pair = jnp.concatenate([zero[:, cols], one[:, cols]], axis=0)
                    held[chip, g * ROWS : (g + 1) * ROWS, :] = pair.astype(BF16)

            @pl.when(core == 0)
            def _():
                place(own[dz][dx], other[dx][dz])

            @pl.when(core == 1)
            def _():
                place(other[dz][dx], own[dx][dz])


def attend_kernel(with_new, info, valid, *refs):
    own, other, cache = refs[:SIDE], refs[SIDE : 2 * SIDE], refs[2 * SIDE]
    refs = refs[2 * SIDE + 1 :]
    if with_new:
        new, out, new_out, held = refs
    else:
        out, held = refs
    step = pl.program_id(0)

    @pl.when(step == 0)
    def _():
        assemble(info, own, other, held)

    first, second = valid[2 * step], valid[2 * step + 1]
    slot = cache.shape[2]
    full = jnp.logical_and(first == slot, second == slot)
    where = [(r, half) for r in range(2) for half in range(2)]

    def scores(r, half):
        return dot_nt(held[step * SIDE + 2 * r + half], cache[0, r, :, :HD])

    def finish(r, half, s):
        top, total, w = weigh(s)
        summed = jnp.dot(w, cache[0, r, :, HD:], preferred_element_type=F32)
        put_partial(out, 2 * r + half, top, total, summed)

    @pl.when(full)
    def _():
        s = scores(*where[0])
        for i, (r, half) in enumerate(where):
            later = scores(*where[i + 1]) if i + 1 < len(where) else None
            finish(r, half, s)
            s = later

    @pl.when(jnp.logical_not(full))
    def _():
        for r, count in ((0, first), (1, second)):

            @pl.when(count > 0)
            def _(r=r, count=count):
                for half in range(2):
                    s = scores(r, half)
                    position = lax.broadcasted_iota(jnp.int32, s.shape, 1)
                    finish(r, half, jnp.where(position < count, s, EMPTY))

            @pl.when(count <= 0)
            def _(r=r):
                lane = lax.broadcasted_iota(jnp.int32, (ROWS, WIDE), 1)
                tops = jnp.logical_and(lane >= FEATS, lane < FEATS + GROUP)
                none = jnp.where(tops, EMPTY, 0.0).astype(BF16)
                for half in range(2):
                    out[2 * r + half] = none

    if with_new:
        @pl.when(step == pl.num_programs(0) - 1)
        def _():
            z, x = info[0], info[1]
            s = dot_nt(held[z * SIDE + x], new[0, :, :HD])
            token = (x % 2) * ROWS + lax.broadcasted_iota(jnp.int32, s.shape, 0) % ROWS
            key = lax.broadcasted_iota(jnp.int32, s.shape, 1)
            top, total, w = weigh(jnp.where(key <= token, s, EMPTY))
            summed = jnp.dot(w, new[0, :, HD:], preferred_element_type=F32)
            put_partial(new_out, 0, top, total, summed)


def attend(info, valid, own, other, cache, new, head_of):
    per = cache.shape[2]
    queries = pl.BlockSpec((SIDE, ROWS // 2, FEATS), lambda i, info, valid: (0, 0, head_of(info[2])))
    in_specs = [queries] * (2 * SIDE) + [
        pl.BlockSpec((1, 2, per, 2 * HD), lambda i, info, valid: (head_of(info[2]), i, 0, 0))
    ]
    out_specs = [pl.BlockSpec((SIDE, ROWS, WIDE), lambda i, info, valid: (i, 0, 0))]
    out_shape = [jax.ShapeDtypeStruct((SIDE * SIDE, ROWS, WIDE), BF16)]
    args = [*own, *other, cache]
    if new is not None:
        in_specs.append(pl.BlockSpec((1, NEW, 2 * HD), lambda i, info, valid: (0, 0, 0)))
        out_specs.append(pl.BlockSpec((1, ROWS, WIDE), lambda i, info, valid: (0, 0, 0)))
        out_shape.append(jax.ShapeDtypeStruct((1, ROWS, WIDE), BF16))
        args.append(new)
    return pl.pallas_call(
        functools.partial(attend_kernel, new is not None),
        out_shape=out_shape,
        grid_spec=pltpu.PrefetchScalarGridSpec(
            num_scalar_prefetch=2,
            grid=(REQS // 2,),
            in_specs=in_specs,
            out_specs=out_specs,
            scratch_shapes=[pltpu.VMEM((SIDE * SIDE, BLOCK, HD), BF16)],
        ),
        compiler_params=pltpu.CompilerParams(vmem_limit_bytes=48 * MIB),
        cost_estimate=pl.CostEstimate(
            flops=4 * REQS * 2 * BLOCK * per * HD, bytes_accessed=REQS * per * 2 * HD * 2, transcendentals=0
        ),
        name="attend_new" if new is not None else "attend",
    )(info, valid, *args)


def merge(parts):
    parts = [p.astype(F32) for p in parts]
    tops = [p[:, FEATS : FEATS + GROUP] for p in parts]
    totals = [p[:, FEATS + GROUP : FEATS + 2 * GROUP] + p[:, FEATS + 2 * GROUP : FEATS + 3 * GROUP] for p in parts]
    best = functools.reduce(jnp.maximum, tops)
    factors = [jnp.exp2(t - best) for t in tops]
    total = sum(f * t for f, t in zip(factors, totals))
    summed = [
        sum(f[:, g : g + 1] * p[:, g * HD : (g + 1) * HD] for f, p in zip(factors, parts)) for g in range(GROUP)
    ]
    return best, total, summed


def put_merged(out, index, parts):
    best, total, summed = merge(parts)
    high = total.astype(BF16)
    low = (total - high.astype(F32)).astype(BF16)
    for g in range(GROUP):
        out[index, :, g * HD : (g + 1) * HD] = summed[g].astype(BF16)
    rest = jnp.zeros((ROWS, HD - 3 * GROUP), BF16)
    out[index, :, FEATS:] = jnp.concatenate([best.astype(BF16), high, low, rest], axis=1)


def twin_kernel(info, mine, got, new, *outs):
    z, x, core = info[0], info[1], info[2]
    for d in range(SIDE):
        for j in range(SIDE):
            chip = jnp.where(core == 0, ((z + d) % SIDE) * SIDE + j, j * SIDE + (x + d) % SIDE)
            if d == 0:
                own = chip == z * SIDE + x

                @pl.when(own)
                def _():
                    put_merged(outs[d], j, [mine[chip], got[chip], new[0]])

                @pl.when(jnp.logical_not(own))
                def _():
                    put_merged(outs[d], j, [mine[chip], got[chip]])
            else:
                put_merged(outs[d], j, [mine[chip], got[chip]])


def whole():
    return pl.BlockSpec(memory_space=pltpu.VMEM)


def merge_twins(info, mine, got, new):
    return pl.pallas_call(
        twin_kernel,
        out_shape=[jax.ShapeDtypeStruct((SIDE, ROWS, WIDE), BF16)] * SIDE,
        in_specs=[pl.BlockSpec(memory_space=pltpu.SMEM)] + [whole()] * 3,
        out_specs=[whole()] * SIDE,
        compiler_params=pltpu.CompilerParams(vmem_limit_bytes=24 * MIB),
        name="merge_twins",
    )(info, mine, got, new)


def four_kernel(a, b, c, d, out):
    @pl.loop(0, SIDE)
    def _(j):
        put_merged(out, j, [a[j], b[j], c[j], d[j]])


def merge_four(parts):
    return pl.pallas_call(
        four_kernel,
        out_shape=jax.ShapeDtypeStruct((SIDE, ROWS, WIDE), BF16),
        in_specs=[whole()] * SIDE,
        out_specs=whole(),
        compiler_params=pltpu.CompilerParams(vmem_limit_bytes=24 * MIB),
        name="merge_four",
    )(*parts)


def final_kernel(a, b, c, d, out):
    @pl.loop(0, SIDE)
    def _(j):
        _, total, summed = merge([a[j], b[j], c[j], d[j]])
        for g in range(GROUP):
            out[j, :, g * HD : (g + 1) * HD] = (summed[g] / total[:, g : g + 1]).astype(BF16)


def merge_final(parts):
    return pl.pallas_call(
        final_kernel,
        out_shape=jax.ShapeDtypeStruct((SIDE, ROWS, FEATS), BF16),
        in_specs=[whole()] * SIDE,
        out_specs=whole(),
        compiler_params=pltpu.CompilerParams(vmem_limit_bytes=24 * MIB),
        name="merge_final",
    )(*parts)


def project_kernel(info, *refs):
    own, other, weight = refs[:SIDE], refs[SIDE : 2 * SIDE], refs[2 * SIDE]
    keep, sends, held, acc = refs[2 * SIDE + 1], refs[2 * SIDE + 2 : 3 * SIDE + 1], refs[-2], refs[-1]
    step = pl.program_id(0)
    z, x, core, y = info[0], info[1], info[2], info[3]
    depth = weight.shape[0]
    per = FEATS // depth

    @pl.when(step == 0)
    def _():
        acc[...] = jnp.zeros_like(acc)

        def place(zero, one):
            for d in range(SIDE):
                for j in range(SIDE):
                    for half, values, chip in (
                        (0, zero, ((z + d) % SIDE) * SIDE + j),
                        (1, one, j * SIDE + (x + d) % SIDE),
                    ):
                        rows = pl.ds(pl.multiple_of(chip * ROWS, ROWS), ROWS)
                        for k in range(per):
                            held[half * per + k, rows, :] = values[d][j, :, k * depth : (k + 1) * depth]

        @pl.when(core == 0)
        def _():
            place(own, other)

        @pl.when(core == 1)
        def _():
            place(other, own)

    acc[...] += jnp.dot(held[step], weight[...], preferred_element_type=F32)

    @pl.when(step == pl.num_programs(0) - 1)
    def _():
        count = keep.shape[0]
        for d in range(SIDE):
            rows = acc[pl.ds(pl.multiple_of(((y + d) % SIDE) * count, count), count), :]
            if d == 0:
                keep[...] = rows
            else:
                sends[d - 1][...] = rows.astype(BF16)


def project(info, own, other, weight):
    depth = 1024
    cols = weight.shape[1]
    rows = SIDE * SIDE * ROWS
    return pl.pallas_call(
        project_kernel,
        out_shape=[jax.ShapeDtypeStruct((rows // SIDE, cols), F32)]
        + [jax.ShapeDtypeStruct((rows // SIDE, cols), BF16)] * (SIDE - 1),
        grid=(weight.shape[0] // depth,),
        in_specs=[pl.BlockSpec(memory_space=pltpu.SMEM)]
        + [whole()] * (2 * SIDE)
        + [pl.BlockSpec((depth, cols), lambda i: (i, 0))],
        out_specs=[whole()] * SIDE,
        scratch_shapes=[
            pltpu.VMEM((weight.shape[0] // depth, rows, depth), BF16),
            pltpu.VMEM((rows, cols), F32),
        ],
        compiler_params=pltpu.CompilerParams(vmem_limit_bytes=32 * MIB),
        name="project",
    )(info, *own, *other, weight)


def on_device(queries, cache, new_kv, lengths, out_weight):
    index = lax.axis_index("ctx")
    z, x, core = index // (2 * SIDE), (index // 2) % SIDE, index % 2
    info = jnp.stack([z, x, core, lax.axis_index("kvh")]).astype(jnp.int32)
    slot = cache.shape[1]
    valid = jnp.clip(lengths - index * slot, 0, slot).astype(jnp.int32)
    by_head = jnp.transpose(cache, (2, 0, 1, 3))

    line = jnp.stack([queries] + [from_first(queries, s) for s in (1, 2, 3)])
    own = [line] + [from_second(line, s) for s in (1, 2, 3)]
    other = [from_twin(part) for part in own]

    request = 2 * z + x // 2
    new = lax.dynamic_slice(new_kv, (request, 0, core, 0), (1, NEW, 1, 2 * HD)).reshape(1, NEW, 2 * HD)

    (sent,) = attend(info, valid, own, other, by_head, None, lambda c: 1 - c)
    got = from_twin(sent)
    mine, from_new = attend(info, valid, own, other, by_head, new, lambda c: c)
    parts = merge_twins(info, mine, got, from_new)
    zs = merge_four([parts[0]] + [from_second(parts[SIDE - s], s) for s in (1, 2, 3)])
    rows = merge_final([zs] + [from_first(zs, s) for s in (1, 2, 3)])

    own = [rows] + [from_second(rows, s) for s in (1, 2, 3)]
    other = [from_twin(part) for part in own]
    keep, *sends = project(info, own, other, out_weight)
    total = keep
    for d in (1, 2, 3):
        total = total + from_plane(sends[d - 1], SIDE - d).astype(F32)
    return total.astype(BF16)


def solution(mesh):
    placed = (
        P("ctx", "kvh"),
        P(None, "ctx", "kvh", None),
        P(None, None, "kvh", None),
        P(),
        P("kvh", "ctx"),
    )
    return jax.shard_map(
        on_device, mesh=mesh, in_specs=placed, out_specs=P("kvh", "ctx"), check_vma=False
    )
```

time: 380 us -> 135 us (0.36)
  waiting for transfers between devices: 133 us -> 47 us
  matrix products: 79 us -> 0 us
  local copies, waits for them, and re-layouts: 64.2 us -> 22 us
  loops' own time: 40.7 us -> 0 us
  Pallas kernels: 0 us -> 38.7 us
  other arithmetic: 33.7 us -> 1.62 us
  between operations: 13.4 us -> 0.18 us
  starting transfers between devices: 13.2 us -> 24.6 us
    dot_general x35 -> x0, matrix products: 79 us -> none  [the longest x16 43.3 us: partial_scores(): jnp.dot(weights.astype(jnp.bfloat16), values, preferred_element_type=jnp....]
    all_gather x2 -> x0, waiting for transfers between devices: 74.5 us -> none  [the longest x1 41.1 us: on_device(): attended = lax.all_gather(own_rows, 'ctx', axis=0, tiled=True)]
    ppermute x0 -> x27, waiting for transfers between devices: none -> 47 us  [the longest x9 27.7 us: from_second(): return lax.ppermute(value, 'ctx', pairs)]
    another operation x1 -> x0, loops' own time: 40.7 us -> none  [cache_partials(): lax.map(one, jnp.arange(REQS * kv_local, dtype=jnp.int32))]
    pallas_call x0 -> x6, Pallas kernels: none -> 38.7 us  [the longest x2 29.9 us: attend(): pl.pallas_call(functools.partial(attend_kernel, new is not None), out_sha...]
    all_to_all x3 -> x0, waiting for transfers between devices: 37.1 us -> none  [the longest x1 25.3 us: on_device(): lax.all_to_all(normals, 'ctx', split_axis=0, concat_axis=0, tiled=True)]
    dynamic_slice x48 -> x1, local copies, waits for them, and re-layouts: 33.7 us -> 0.04 us  [on_device(): lax.dynamic_slice(new_kv, (request, 0, core, 0), (1, NEW, 1, 2 * HD))]
    ppermute x0 -> x27, starting transfers between devices: none -> 24.6 us  [the longest x9 9.84 us: from_second(): return lax.ppermute(value, 'ctx', pairs)]
  transfers between devices with their start and end apart: 6 -> 27, of which waited for: 6 -> 18; matrix products, arithmetic and copies ran while one was open for 6% -> 12% of each run, Pallas kernels for 0% -> 11%
where the time goes in v1:
time: 135 us; the launch traced here: 134 us
  waiting for transfers between devices  47 us (35%)
  Pallas kernels  38.7 us (29%)
  starting transfers between devices  24.6 us (18%)
  local copies, waits for them, and re-layouts  22 us (16%)
  other arithmetic  1.62 us (1%)
    pallas_call x2, Pallas kernels, attend(): pl.pallas_call(functools.partial(attend_kernel, new is not None), out_sha...  29.9 us
    ppermute x9, waiting for transfers between devices, from_second(): return lax.ppermute(value, 'ctx', pairs)  27.7 us
    unnamed x24, local copies, waits for them, and re-layouts  21.9 us
    ppermute x6, waiting for transfers between devices, from_first(): return lax.ppermute(value, 'ctx', pairs)  12.6 us
    ppermute x9, starting transfers between devices, from_second(): return lax.ppermute(value, 'ctx', pairs)  9.84 us
    ppermute x6, starting transfers between devices, from_first(): return lax.ppermute(value, 'ctx', pairs)  9.63 us
    ppermute x3, waiting for transfers between devices, from_plane(): lax.ppermute(value, 'kvh', [((s + step) % SIDE, s) for s in range(SIDE)])  5.16 us
    ppermute x3, starting transfers between devices, from_plane(): lax.ppermute(value, 'kvh', [((s + step) % SIDE, s) for s in range(SIDE)])  4.68 us
  transfers between devices with their start and end apart: 27, of which 18 were waited for; matrix products, arithmetic and copies ran while one was open for 12% of the time, Pallas kernels for 11%

profile of v1, /device:TPU:0, one launch (start us, length us, event | category | flops | bytes accessed | tf_op | source)
XLA Modules:
  0.0 134.1 jit_solution(4630723333996247622)
XLA Ops:
  0.0 1.6 %collective-permute-start.2 = (bf16[8,4096]{1,0:T(8,128)(2,1)}, bf16[8,4096]{1,0:T(8,128)(2,1)S(1)}, u32[]{:S(2)}, u32[]{:S(2)}) collective-permute-start(bf16[8,4096]{1,0:T(8,128)(2,1)} %param.5), channel_id=1, source_target_pairs={{24,0},{100,4},{0,8},{108,12},{8,16},{116,20},{16,24},{124,28},{56... | collective-permute-start | bytes 196616 | tf_op jit(solution)/shard_map/ppermute | solution.py:38
  1.6 2.7 %collective-permute-start.1 = (bf16[8,4096]{1,0:T(8,128)(2,1)}, bf16[8,4096]{1,0:T(8,128)(2,1)S(1)}, u32[]{:S(2)}, u32[]{:S(2)}) collective-permute-start(bf16[8,4096]{1,0:T(8,128)(2,1)} %param.5), channel_id=1, source_target_pairs={{16,0},{68,4},{24,8},{76,12},{0,16},{84,20},{8,24},{92,28},{48,32}... | collective-permute-start | bytes 196616 | tf_op jit(solution)/shard_map/ppermute | solution.py:38
  4.3 1.4 %collective-permute-start = (bf16[8,4096]{1,0:T(8,128)(2,1)}, bf16[8,4096]{1,0:T(8,128)(2,1)S(1)}, u32[]{:S(2)}, u32[]{:S(2)}) collective-permute-start(bf16[8,4096]{1,0:T(8,128)(2,1)} %param.5), channel_id=1, source_target_pairs={{8,0},{36,4},{16,8},{44,12},{24,16},{52,20},{0,24},{60,28},{40,32}... | collective-permute-start | bytes 196616 | tf_op jit(solution)/shard_map/ppermute | solution.py:38
  5.7 1.8 %collective-permute-done.1 = bf16[8,4096]{1,0:T(8,128)(2,1)S(1)} collective-permute-done((bf16[8,4096]{1,0:T(8,128)(2,1)}, bf16[8,4096]{1,0:T(8,128)(2,1)S(1)}, u32[]{:S(2)}, u32[]{:S(2)}) %collective-permute-start.1) | collective-permute-done | bytes 65568 | tf_op jit(solution)/shard_map/ppermute | solution.py:38
  7.6 1.2 collective-permute-done
  9.7 4.1 %collective-permute-start.3 = (bf16[4,8,4096]{2,1,0:T(8,128)(2,1)S(1)}, bf16[4,8,4096]{2,1,0:T(8,128)(2,1)S(1)}, u32[]{:S(2)}, u32[]{:S(2)}) collective-permute-start(bf16[4,8,4096]{2,1,0:T(8,128)(2,1)S(1)} %pad_maximum_fusion.refs_0_), channel_id=1, source_target_pairs={{32,0},{12,4},{40,8},{20,12},{48,16},{28,20},{56,24},{4,28},{64,32... | collective-permute-start | bytes 786440 | tf_op jit(solution)/shard_map/ppermute | solution.py:43
  13.8 1.3 collective-permute-start.5
  15.0 5.4 %collective-permute-done.3.refs_1_ = bf16[4,8,4096]{2,1,0:T(8,128)(2,1)S(1)} collective-permute-done((bf16[4,8,4096]{2,1,0:T(8,128)(2,1)S(1)}, bf16[4,8,4096]{2,1,0:T(8,128)(2,1)S(1)}, u32[]{:S(2)}, u32[]{:S(2)}) %collective-permute-start.3) | collective-permute-done | bytes 262176 | tf_op jit(solution)/shard_map/ppermute | solution.py:43
  20.5 1.3 collective-permute-done.4.refs_2_
  21.8 2.4 %collective-permute-done.5.refs_3_ = bf16[4,8,4096]{2,1,0:T(8,128)(2,1)S(1)} collective-permute-done((bf16[4,8,4096]{2,1,0:T(8,128)(2,1)S(1)}, bf16[4,8,4096]{2,1,0:T(8,128)(2,1)S(1)}, u32[]{:S(2)}, u32[]{:S(2)}) %collective-permute-start.5) | collective-permute-done | bytes 262176 | tf_op jit(solution)/shard_map/ppermute | solution.py:43
  24.2 15.3 %copy.12 = bf16[8,2048,2,256]{3,1,0,2:T(8,128)(2,1)} copy(bf16[8,2048,2,256]{3,2,1,0:T(2,128)(2,1)} %param.6) | data formatting | bytes 33554432 | tf_op args[1]
  39.6 14.8 %attend.1 = bf16[16,16,2176]{2,1,0:T(8,128)(2,1)S(1)} custom-call(s32[4]{0:T(128)S(1)} %pad_add_fusion.info, s32[8]{0:T(128)S(1)} %subtract_clamp_fusion.valid, bf16[4,8,4096]{2,1,0:T(8,128)(2,1)S(1)} %pad_maximum_fusion.refs_0_, bf16[4,8,4096]{2,1,0:T(8,128)(2,1)S(1)} %collective-permute-done.3.refs_1_, ...), custom_call_target="tpu_custom_call" | custom-call | flops 4294967296 | bytes 8388608 | tf_op jit(solution)/shard_map/attend/pallas_call | solution.py:179
  61.6 15.1 %attend_new.1 = (bf16[16,16,2176]{2,1,0:T(8,128)(2,1)S(1)}, bf16[1,16,2176]{2,1,0:T(8,128)(2,1)S(1)}) custom-call(s32[4]{0:T(128)S(1)} %pad_add_fusion.info, s32[8]{0:T(128)S(1)} %subtract_clamp_fusion.valid, bf16[4,8,4096]{2,1,0:T(8,128)(2,1)S(1)} %pad_maximum_fusion.refs_0_, bf16[4,8,4096]{2,1,0:T(8,128)(2,1)S(1)} %collective-permute-done.3.refs_1_, ...), custom_call_target="tpu_custom_call" | custom-call | flops 4294967296 | bytes 8388608 | tf_op jit(solution)/shard_map/attend_new/pallas_call | solution.py:179
  76.8 4.0 %merge_twins.1 = (bf16[4,16,2176]{2,1,0:T(8,128)(2,1)S(1)}, bf16[4,16,2176]{2,1,0:T(8,128)(2,1)S(1)}, bf16[4,16,2176]{2,1,0:T(8,128)(2,1)S(1)}, bf16[4,16,2176]{2,1,0:T(8,128)(2,1)S(1)}) custom-call(s32[4]{0:T(128)S(1)} %pad_add_fusion.info, bf16[16,16,2176]{2,1,0:T(8,128)(2,1)S(1)} %get-tuple-element.15.mine, ...), custom_call_target="tpu_custom_call" | custom-call | tf_op jit(solution)/shard_map/merge_twins/pallas_call | solution.py:244
  81.6 1.2 collective-permute-start.13
  82.8 4.5 %collective-permute-done.11.b = bf16[4,16,2176]{2,1,0:T(8,128)(2,1)S(1)} collective-permute-done((bf16[4,16,2176]{2,1,0:T(8,128)(2,1)S(1)}, bf16[4,16,2176]{2,1,0:T(8,128)(2,1)S(1)}, u32[]{:S(2)}, u32[]{:S(2)}) %collective-permute-start.11) | collective-permute-done | bytes 278560 | tf_op jit(solution)/shard_map/ppermute | solution.py:43
  87.3 1.7 %collective-permute-done.12.c = bf16[4,16,2176]{2,1,0:T(8,128)(2,1)S(1)} collective-permute-done((bf16[4,16,2176]{2,1,0:T(8,128)(2,1)S(1)}, bf16[4,16,2176]{2,1,0:T(8,128)(2,1)S(1)}, u32[]{:S(2)}, u32[]{:S(2)}) %collective-permute-start.12) | collective-permute-done | bytes 278560 | tf_op jit(solution)/shard_map/ppermute | solution.py:43
  89.0 2.9 %collective-permute-done.13.d = bf16[4,16,2176]{2,1,0:T(8,128)(2,1)S(1)} collective-permute-done((bf16[4,16,2176]{2,1,0:T(8,128)(2,1)S(1)}, bf16[4,16,2176]{2,1,0:T(8,128)(2,1)S(1)}, u32[]{:S(2)}, u32[]{:S(2)}) %collective-permute-start.13) | collective-permute-done | bytes 278560 | tf_op jit(solution)/shard_map/ppermute | solution.py:43
  92.9 2.7 %collective-permute-start.14 = (bf16[4,16,2176]{2,1,0:T(8,128)(2,1)S(1)}, bf16[4,16,2176]{2,1,0:T(8,128)(2,1)S(1)}, u32[]{:S(2)}, u32[]{:S(2)}) collective-permute-start(bf16[4,16,2176]{2,1,0:T(8,128)(2,1)S(1)} %merge_four.1.a), channel_id=1, source_target_pairs={{8,0},{36,4},{16,8},{44,12},{24,16},{52,20},{0,24},{60,28},{40,32}... | collective-permute-start | bytes 835592 | tf_op jit(solution)/shard_map/ppermute | solution.py:38
  95.7 1.2 collective-permute-start.16
  96.8 5.9 %collective-permute-done.14.b = bf16[4,16,2176]{2,1,0:T(8,128)(2,1)S(1)} collective-permute-done((bf16[4,16,2176]{2,1,0:T(8,128)(2,1)S(1)}, bf16[4,16,2176]{2,1,0:T(8,128)(2,1)S(1)}, u32[]{:S(2)}, u32[]{:S(2)}) %collective-permute-start.14) | collective-permute-done | bytes 278560 | tf_op jit(solution)/shard_map/ppermute | solution.py:38
  103.8 2.6 %collective-permute-done.16.d = bf16[4,16,2176]{2,1,0:T(8,128)(2,1)S(1)} collective-permute-done((bf16[4,16,2176]{2,1,0:T(8,128)(2,1)S(1)}, bf16[4,16,2176]{2,1,0:T(8,128)(2,1)S(1)}, u32[]{:S(2)}, u32[]{:S(2)}) %collective-permute-start.16) | collective-permute-done | bytes 278560 | tf_op jit(solution)/shard_map/ppermute | solution.py:38
  106.4 1.2 merge_final.1.refs_0_
  108.8 1.2 collective-permute-start.18
  110.0 4.1 %collective-permute-done.17.refs_1_ = bf16[4,16,2048]{2,1,0:T(8,128)(2,1)S(1)} collective-permute-done((bf16[4,16,2048]{2,1,0:T(8,128)(2,1)S(1)}, bf16[4,16,2048]{2,1,0:T(8,128)(2,1)S(1)}, u32[]{:S(2)}, u32[]{:S(2)}) %collective-permute-start.17) | collective-permute-done | bytes 262176 | tf_op jit(solution)/shard_map/ppermute | solution.py:43
  114.1 2.7 %collective-permute-done.18.refs_2_ = bf16[4,16,2048]{2,1,0:T(8,128)(2,1)S(1)} collective-permute-done((bf16[4,16,2048]{2,1,0:T(8,128)(2,1)S(1)}, bf16[4,16,2048]{2,1,0:T(8,128)(2,1)S(1)}, u32[]{:S(2)}, u32[]{:S(2)}) %collective-permute-start.18) | collective-permute-done | bytes 262176 | tf_op jit(solution)/shard_map/ppermute | solution.py:43
  116.8 2.7 %collective-permute-done.19.refs_3_ = bf16[4,16,2048]{2,1,0:T(8,128)(2,1)S(1)} collective-permute-done((bf16[4,16,2048]{2,1,0:T(8,128)(2,1)S(1)}, bf16[4,16,2048]{2,1,0:T(8,128)(2,1)S(1)}, u32[]{:S(2)}, u32[]{:S(2)}) %collective-permute-start.19) | collective-permute-done | bytes 262176 | tf_op jit(solution)/shard_map/ppermute | solution.py:43
  119.5 1.5 %collective-permute-done.23.refs_7_ = bf16[4,16,2048]{2,1,0:T(8,128)(2,1)S(1)} collective-permute-done((bf16[4,16,2048]{2,1,0:T(8,128)(2,1)S(1)}, bf16[4,16,2048]{2,1,0:T(8,128)(2,1)S(1)}, u32[]{:S(2)}, u32[]{:S(2)}) %collective-permute-start.23) | collective-permute-done | bytes 262176 | tf_op jit(solution)/shard_map/ppermute | solution.py:47
  121.0 2.6 %project.1 = (f32[64,512]{1,0:T(8,128)S(1)}, bf16[64,512]{1,0:T(8,128)(2,1)S(1)}, bf16[64,512]{1,0:T(8,128)(2,1)S(1)}, bf16[64,512]{1,0:T(8,128)(2,1)S(1)}) custom-call(s32[4]{0:T(128)S(1)} %pad_add_fusion.info, bf16[4,16,2048]{2,1,0:T(8,128)(2,1)S(1)} %merge_final.1.refs_0_, bf16[4,16,2048]{2,1,0:T(8,128)(2,1)S(1)} %collective-permute-done.17.refs_1_, ...), custom_call_target="tpu_custom_call" | custom-call | tf_op jit(solution)/shard_map/project/pallas_call | solution.py:338
  123.6 3.1 %collective-permute-start.26 = (bf16[64,512]{1,0:T(8,128)(2,1)S(1)}, bf16[64,512]{1,0:T(8,128)(2,1)S(1)}, u32[]{:S(2)}, u32[]{:S(2)}) collective-permute-start(bf16[64,512]{1,0:T(8,128)(2,1)S(1)} %get-tuple-element.24), channel_id=1, source_target_pairs={{1,0},{2,1},{3,2},{0,3},{5,4},{6,5},{7,6},{4,7},{9,8},{10,9},{11,1... | collective-permute-start | bytes 196616 | tf_op jit(solution)/shard_map/ppermute | solution.py:51
  128.3 1.5 %collective-permute-done.26 = bf16[64,512]{1,0:T(8,128)(2,1)S(1)} collective-permute-done((bf16[64,512]{1,0:T(8,128)(2,1)S(1)}, bf16[64,512]{1,0:T(8,128)(2,1)S(1)}, u32[]{:S(2)}, u32[]{:S(2)}) %collective-permute-start.26) | collective-permute-done | bytes 65568 | tf_op jit(solution)/shard_map/ppermute | solution.py:51
  129.9 3.0 %collective-permute-done.25 = bf16[64,512]{1,0:T(8,128)(2,1)S(1)} collective-permute-done((bf16[64,512]{1,0:T(8,128)(2,1)S(1)}, bf16[64,512]{1,0:T(8,128)(2,1)S(1)}, u32[]{:S(2)}, u32[]{:S(2)}) %collective-permute-start.25) | collective-permute-done | bytes 65568 | tf_op jit(solution)/shard_map/ppermute | solution.py:51
  (57 shorter events, 15.2 us)
Async XLA Ops:
  0.0 57.7 %copy-start = (bf16[8,32,2,256]{3,2,1,0:T(2,128)(2,1)S(1)}, bf16[8,32,2,256]{3,2,1,0:T(2,128)(2,1)}, u32[]{:S(2)}) copy-start(bf16[8,32,2,256]{3,2,1,0:T(2,128)(2,1)} %param.7) | copy-start | bytes 786436
  0.0 5.7 %collective-permute-start.2 = (bf16[8,4096]{1,0:T(8,128)(2,1)}, bf16[8,4096]{1,0:T(8,128)(2,1)S(1)}, u32[]{:S(2)}, u32[]{:S(2)}) collective-permute-start(bf16[8,4096]{1,0:T(8,128)(2,1)} %param.5), channel_id=1, source_target_pairs={{24,0},{100,4},{0,8},{108,12},{8,16},{116,20},{16,24},{124,28},{56... | collective-permute-start | bytes 196616 | tf_op jit(solution)/shard_map/ppermute | solution.py:38
  1.6 6.0 %collective-permute-start.1 = (bf16[8,4096]{1,0:T(8,128)(2,1)}, bf16[8,4096]{1,0:T(8,128)(2,1)S(1)}, u32[]{:S(2)}, u32[]{:S(2)}) collective-permute-start(bf16[8,4096]{1,0:T(8,128)(2,1)} %param.5), channel_id=1, source_target_pairs={{16,0},{68,4},{24,8},{76,12},{0,16},{84,20},{8,24},{92,28},{48,32}... | collective-permute-start | bytes 196616 | tf_op jit(solution)/shard_map/ppermute | solution.py:38
  4.3 4.5 %collective-permute-start = (bf16[8,4096]{1,0:T(8,128)(2,1)}, bf16[8,4096]{1,0:T(8,128)(2,1)S(1)}, u32[]{:S(2)}, u32[]{:S(2)}) collective-permute-start(bf16[8,4096]{1,0:T(8,128)(2,1)} %param.5), channel_id=1, source_target_pairs={{8,0},{36,4},{16,8},{44,12},{24,16},{52,20},{0,24},{60,28},{40,32}... | collective-permute-start | bytes 196616 | tf_op jit(solution)/shard_map/ppermute | solution.py:38
  9.7 10.8 %collective-permute-start.3 = (bf16[4,8,4096]{2,1,0:T(8,128)(2,1)S(1)}, bf16[4,8,4096]{2,1,0:T(8,128)(2,1)S(1)}, u32[]{:S(2)}, u32[]{:S(2)}) collective-permute-start(bf16[4,8,4096]{2,1,0:T(8,128)(2,1)S(1)} %pad_maximum_fusion.refs_0_), channel_id=1, source_target_pairs={{32,0},{12,4},{40,8},{20,12},{48,16},{28,20},{56,24},{4,28},{64,32... | collective-permute-start | bytes 786440 | tf_op jit(solution)/shard_map/ppermute | solution.py:43
  13.8 8.0 %collective-permute-start.4 = (bf16[4,8,4096]{2,1,0:T(8,128)(2,1)S(1)}, bf16[4,8,4096]{2,1,0:T(8,128)(2,1)S(1)}, u32[]{:S(2)}, u32[]{:S(2)}) collective-permute-start(bf16[4,8,4096]{2,1,0:T(8,128)(2,1)S(1)} %pad_maximum_fusion.refs_0_), channel_id=1, source_target_pairs={{64,0},{20,4},{72,8},{28,12},{80,16},{4,20},{88,24},{12,28},{96,32... | collective-permute-start | bytes 786440 | tf_op jit(solution)/shard_map/ppermute | solution.py:43
  13.8 10.4 %collective-permute-start.5 = (bf16[4,8,4096]{2,1,0:T(8,128)(2,1)S(1)}, bf16[4,8,4096]{2,1,0:T(8,128)(2,1)S(1)}, u32[]{:S(2)}, u32[]{:S(2)}) collective-permute-start(bf16[4,8,4096]{2,1,0:T(8,128)(2,1)S(1)} %pad_maximum_fusion.refs_0_), channel_id=1, source_target_pairs={{96,0},{28,4},{104,8},{4,12},{112,16},{12,20},{120,24},{20,28},{0,... | collective-permute-start | bytes 786440 | tf_op jit(solution)/shard_map/ppermute | solution.py:43
  15.0 24.6 %collective-permute-start.6 = (bf16[4,8,4096]{2,1,0:T(8,128)(2,1)S(1)}, bf16[4,8,4096]{2,1,0:T(8,128)(2,1)S(1)}, u32[]{:S(2)}, u32[]{:S(2)}) collective-permute-start(bf16[4,8,4096]{2,1,0:T(8,128)(2,1)S(1)} %pad_maximum_fusion.refs_0_), channel_id=1, source_target_pairs={{4,0},{0,4},{12,8},{8,12},{20,16},{16,20},{28,24},{24,28},{36,32},... | collective-permute-start | bytes 786440 | tf_op jit(solution)/shard_map/ppermute | solution.py:47
  20.5 19.1 %collective-permute-start.7 = (bf16[4,8,4096]{2,1,0:T(8,128)(2,1)S(1)}, bf16[4,8,4096]{2,1,0:T(8,128)(2,1)S(1)}, u32[]{:S(2)}, u32[]{:S(2)}) collective-permute-start(bf16[4,8,4096]{2,1,0:T(8,128)(2,1)S(1)} %collective-permute-done.3.refs_1_), channel_id=1, source_target_pairs={{4,0},{0,4},{12,8},{8,12},{20,16},{16,20},{28,24},{24,28},{36,32},... | collective-permute-start | bytes 786440 | tf_op jit(solution)/shard_map/ppermute | solution.py:47
  21.8 17.9 %collective-permute-start.8 = (bf16[4,8,4096]{2,1,0:T(8,128)(2,1)S(1)}, bf16[4,8,4096]{2,1,0:T(8,128)(2,1)S(1)}, u32[]{:S(2)}, u32[]{:S(2)}) collective-permute-start(bf16[4,8,4096]{2,1,0:T(8,128)(2,1)S(1)} %collective-permute-done.4.refs_2_), channel_id=1, source_target_pairs={{4,0},{0,4},{12,8},{8,12},{20,16},{16,20},{28,24},{24,28},{36,32},... | collective-permute-start | bytes 786440 | tf_op jit(solution)/shard_map/ppermute | solution.py:47
  24.2 15.5 %collective-permute-start.9 = (bf16[4,8,4096]{2,1,0:T(8,128)(2,1)S(1)}, bf16[4,8,4096]{2,1,0:T(8,128)(2,1)S(1)}, u32[]{:S(2)}, u32[]{:S(2)}) collective-permute-start(bf16[4,8,4096]{2,1,0:T(8,128)(2,1)S(1)} %collective-permute-done.5.refs_3_), channel_id=1, source_target_pairs={{4,0},{0,4},{12,8},{8,12},{20,16},{16,20},{28,24},{24,28},{36,32},... | collective-permute-start | bytes 786440 | tf_op jit(solution)/shard_map/ppermute | solution.py:47
  24.2 15.3 %copy-start.10 = (s32[8]{0:T(128)S(1)}, s32[8]{0:T(128)}, u32[]{:S(2)}) copy-start(s32[8]{0:T(128)} %param.8) | copy-start | bytes 100
  57.2 19.5 %collective-permute-start.10 = (bf16[16,16,2176]{2,1,0:T(8,128)(2,1)S(1)}, bf16[16,16,2176]{2,1,0:T(8,128)(2,1)S(1)}, u32[]{:S(2)}, u32[]{:S(2)}) collective-permute-start(bf16[16,16,2176]{2,1,0:T(8,128)(2,1)S(1)} %attend.1), channel_id=1, source_target_pairs={{4,0},{0,4},{12,8},{8,12},{20,16},{16,20},{28,24},{24,28},{36,32},... | collective-permute-start | bytes 3342344 | tf_op jit(solution)/shard_map/ppermute | solution.py:47
  57.8 1.0 copy-start.3
  58.7 0.9 copy-start.5
  76.7 44.3 %copy-start.1 = (bf16[4096,512]{1,0:T(8,128)(2,1)S(1)}, bf16[4096,512]{1,0:T(8,128)(2,1)}, u32[]{:S(2)}) copy-start(bf16[4096,512]{1,0:T(8,128)(2,1)} %refs_8_.1) | copy-start | bytes 12582916
  80.7 6.6 %collective-permute-start.11 = (bf16[4,16,2176]{2,1,0:T(8,128)(2,1)S(1)}, bf16[4,16,2176]{2,1,0:T(8,128)(2,1)S(1)}, u32[]{:S(2)}, u32[]{:S(2)}) collective-permute-start(bf16[4,16,2176]{2,1,0:T(8,128)(2,1)S(1)} %get-tuple-element.18), channel_id=1, source_target_pairs={{32,0},{12,4},{40,8},{20,12},{48,16},{28,20},{56,24},{4,28},{64,32... | collective-permute-start | bytes 835592 | tf_op jit(solution)/shard_map/ppermute | solution.py:43
  80.8 8.2 %collective-permute-start.12 = (bf16[4,16,2176]{2,1,0:T(8,128)(2,1)S(1)}, bf16[4,16,2176]{2,1,0:T(8,128)(2,1)S(1)}, u32[]{:S(2)}, u32[]{:S(2)}) collective-permute-start(bf16[4,16,2176]{2,1,0:T(8,128)(2,1)S(1)} %get-tuple-element.19), channel_id=1, source_target_pairs={{64,0},{20,4},{72,8},{28,12},{80,16},{4,20},{88,24},{12,28},{96,32... | collective-permute-start | bytes 835592 | tf_op jit(solution)/shard_map/ppermute | solution.py:43
  81.6 10.3 %collective-permute-start.13 = (bf16[4,16,2176]{2,1,0:T(8,128)(2,1)S(1)}, bf16[4,16,2176]{2,1,0:T(8,128)(2,1)S(1)}, u32[]{:S(2)}, u32[]{:S(2)}) collective-permute-start(bf16[4,16,2176]{2,1,0:T(8,128)(2,1)S(1)} %get-tuple-element.20), channel_id=1, source_target_pairs={{96,0},{28,4},{104,8},{4,12},{112,16},{12,20},{120,24},{20,28},{0,... | collective-permute-start | bytes 835592 | tf_op jit(solution)/shard_map/ppermute | solution.py:43
  92.9 9.8 %collective-permute-start.14 = (bf16[4,16,2176]{2,1,0:T(8,128)(2,1)S(1)}, bf16[4,16,2176]{2,1,0:T(8,128)(2,1)S(1)}, u32[]{:S(2)}, u32[]{:S(2)}) collective-permute-start(bf16[4,16,2176]{2,1,0:T(8,128)(2,1)S(1)} %merge_four.1.a), channel_id=1, source_target_pairs={{8,0},{36,4},{16,8},{44,12},{24,16},{52,20},{0,24},{60,28},{40,32}... | collective-permute-start | bytes 835592 | tf_op jit(solution)/shard_map/ppermute | solution.py:38
  95.7 8.2 %collective-permute-start.15 = (bf16[4,16,2176]{2,1,0:T(8,128)(2,1)S(1)}, bf16[4,16,2176]{2,1,0:T(8,128)(2,1)S(1)}, u32[]{:S(2)}, u32[]{:S(2)}) collective-permute-start(bf16[4,16,2176]{2,1,0:T(8,128)(2,1)S(1)} %merge_four.1.a), channel_id=1, source_target_pairs={{16,0},{68,4},{24,8},{76,12},{0,16},{84,20},{8,24},{92,28},{48,32}... | collective-permute-start | bytes 835592 | tf_op jit(solution)/shard_map/ppermute | solution.py:38
  95.7 10.7 %collective-permute-start.16 = (bf16[4,16,2176]{2,1,0:T(8,128)(2,1)S(1)}, bf16[4,16,2176]{2,1,0:T(8,128)(2,1)S(1)}, u32[]{:S(2)}, u32[]{:S(2)}) collective-permute-start(bf16[4,16,2176]{2,1,0:T(8,128)(2,1)S(1)} %merge_four.1.a), channel_id=1, source_target_pairs={{24,0},{100,4},{0,8},{108,12},{8,16},{116,20},{16,24},{124,28},{56... | collective-permute-start | bytes 835592 | tf_op jit(solution)/shard_map/ppermute | solution.py:38
  107.7 6.4 %collective-permute-start.17 = (bf16[4,16,2048]{2,1,0:T(8,128)(2,1)S(1)}, bf16[4,16,2048]{2,1,0:T(8,128)(2,1)S(1)}, u32[]{:S(2)}, u32[]{:S(2)}) collective-permute-start(bf16[4,16,2048]{2,1,0:T(8,128)(2,1)S(1)} %merge_final.1.refs_0_), channel_id=1, source_target_pairs={{32,0},{12,4},{40,8},{20,12},{48,16},{28,20},{56,24},{4,28},{64,32... | collective-permute-start | bytes 786440 | tf_op jit(solution)/shard_map/ppermute | solution.py:43
  108.8 8.0 %collective-permute-start.18 = (bf16[4,16,2048]{2,1,0:T(8,128)(2,1)S(1)}, bf16[4,16,2048]{2,1,0:T(8,128)(2,1)S(1)}, u32[]{:S(2)}, u32[]{:S(2)}) collective-permute-start(bf16[4,16,2048]{2,1,0:T(8,128)(2,1)S(1)} %merge_final.1.refs_0_), channel_id=1, source_target_pairs={{64,0},{20,4},{72,8},{28,12},{80,16},{4,20},{88,24},{12,28},{96,32... | collective-permute-start | bytes 786440 | tf_op jit(solution)/shard_map/ppermute | solution.py:43
  110.0 9.5 %collective-permute-start.19 = (bf16[4,16,2048]{2,1,0:T(8,128)(2,1)S(1)}, bf16[4,16,2048]{2,1,0:T(8,128)(2,1)S(1)}, u32[]{:S(2)}, u32[]{:S(2)}) collective-permute-start(bf16[4,16,2048]{2,1,0:T(8,128)(2,1)S(1)} %merge_final.1.refs_0_), channel_id=1, source_target_pairs={{96,0},{28,4},{104,8},{4,12},{112,16},{12,20},{120,24},{20,28},{0,... | collective-permute-start | bytes 786440 | tf_op jit(solution)/shard_map/ppermute | solution.py:43
  110.0 9.5 %collective-permute-start.20 = (bf16[4,16,2048]{2,1,0:T(8,128)(2,1)S(1)}, bf16[4,16,2048]{2,1,0:T(8,128)(2,1)S(1)}, u32[]{:S(2)}, u32[]{:S(2)}) collective-permute-start(bf16[4,16,2048]{2,1,0:T(8,128)(2,1)S(1)} %merge_final.1.refs_0_), channel_id=1, source_target_pairs={{4,0},{0,4},{12,8},{8,12},{20,16},{16,20},{28,24},{24,28},{36,32},... | collective-permute-start | bytes 786440 | tf_op jit(solution)/shard_map/ppermute | solution.py:47
  114.1 5.4 %collective-permute-start.21 = (bf16[4,16,2048]{2,1,0:T(8,128)(2,1)S(1)}, bf16[4,16,2048]{2,1,0:T(8,128)(2,1)S(1)}, u32[]{:S(2)}, u32[]{:S(2)}) collective-permute-start(bf16[4,16,2048]{2,1,0:T(8,128)(2,1)S(1)} %collective-permute-done.17.refs_1_), channel_id=1, source_target_pairs={{4,0},{0,4},{12,8},{8,12},{20,16},{16,20},{28,24},{24,28},{36,32},... | collective-permute-start | bytes 786440 | tf_op jit(solution)/shard_map/ppermute | solution.py:47
  116.8 2.7 %collective-permute-start.22 = (bf16[4,16,2048]{2,1,0:T(8,128)(2,1)S(1)}, bf16[4,16,2048]{2,1,0:T(8,128)(2,1)S(1)}, u32[]{:S(2)}, u32[]{:S(2)}) collective-permute-start(bf16[4,16,2048]{2,1,0:T(8,128)(2,1)S(1)} %collective-permute-done.18.refs_2_), channel_id=1, source_target_pairs={{4,0},{0,4},{12,8},{8,12},{20,16},{16,20},{28,24},{24,28},{36,32},... | collective-permute-start | bytes 786440 | tf_op jit(solution)/shard_map/ppermute | solution.py:47
  119.5 1.5 %collective-permute-start.23 = (bf16[4,16,2048]{2,1,0:T(8,128)(2,1)S(1)}, bf16[4,16,2048]{2,1,0:T(8,128)(2,1)S(1)}, u32[]{:S(2)}, u32[]{:S(2)}) collective-permute-start(bf16[4,16,2048]{2,1,0:T(8,128)(2,1)S(1)} %collective-permute-done.19.refs_3_), channel_id=1, source_target_pairs={{4,0},{0,4},{12,8},{8,12},{20,16},{16,20},{28,24},{24,28},{36,32},... | collective-permute-start | bytes 786440 | tf_op jit(solution)/shard_map/ppermute | solution.py:47
  123.6 6.2 %collective-permute-start.26 = (bf16[64,512]{1,0:T(8,128)(2,1)S(1)}, bf16[64,512]{1,0:T(8,128)(2,1)S(1)}, u32[]{:S(2)}, u32[]{:S(2)}) collective-permute-start(bf16[64,512]{1,0:T(8,128)(2,1)S(1)} %get-tuple-element.24), channel_id=1, source_target_pairs={{1,0},{2,1},{3,2},{0,3},{5,4},{6,5},{7,6},{4,7},{9,8},{10,9},{11,1... | collective-permute-start | bytes 196616 | tf_op jit(solution)/shard_map/ppermute | solution.py:51
  126.7 6.1 %collective-permute-start.25 = (bf16[64,512]{1,0:T(8,128)(2,1)S(1)}, bf16[64,512]{1,0:T(8,128)(2,1)S(1)}, u32[]{:S(2)}, u32[]{:S(2)}) collective-permute-start(bf16[64,512]{1,0:T(8,128)(2,1)S(1)} %get-tuple-element.23), channel_id=1, source_target_pairs={{2,0},{3,1},{0,2},{1,3},{6,4},{7,5},{4,6},{5,7},{10,8},{11,9},{8,1... | collective-permute-start | bytes 196616 | tf_op jit(solution)/shard_map/ppermute | solution.py:51
  127.3 6.1 %collective-permute-start.24 = (bf16[64,512]{1,0:T(8,128)(2,1)S(1)}, bf16[64,512]{1,0:T(8,128)(2,1)S(1)}, u32[]{:S(2)}, u32[]{:S(2)}) collective-permute-start(bf16[64,512]{1,0:T(8,128)(2,1)S(1)} %get-tuple-element.22), channel_id=1, source_target_pairs={{3,0},{0,1},{1,2},{2,3},{7,4},{4,5},{5,6},{6,7},{11,8},{8,9},{9,10... | collective-permute-start | bytes 196616 | tf_op jit(solution)/shard_map/ppermute | solution.py:51
  (6 other events, 4.7 us)

commit v2 on v1

v2 whole, which is shorter than its diff:
```python
import functools
import math

import jax
import jax.numpy as jnp
from jax import lax
from jax.experimental import pallas as pl
from jax.experimental.pallas import tpu as pltpu
from jax.sharding import PartitionSpec as P

KV_HEADS = 8
QH = 128
HD = 128
REQS = 8
NEW = 32
GROUP = QH // KV_HEADS
SIDE = 4
ROWS = 16
BLOCK = GROUP * ROWS
FEATS = GROUP * HD
WIDE = FEATS + HD
SCALE = HD ** (-0.5) * math.log2(math.e)
EMPTY = -1e30
F32, BF16 = jnp.float32, jnp.bfloat16
MIB = 2**20


def at(z, x, core):
    return ((z % SIDE) * SIDE + x % SIDE) * 2 + core


def places():
    return [(z, x, c) for z in range(SIDE) for x in range(SIDE) for c in range(2)]


def from_first(value, step):
    pairs = [(at(z, x + step, c) if c == 0 else at(z + step, x, c), at(z, x, c)) for z, x, c in places()]
    return lax.ppermute(value, "ctx", pairs)


def from_second(value, step):
    pairs = [(at(z + step, x, c) if c == 0 else at(z, x + step, c), at(z, x, c)) for z, x, c in places()]
    return lax.ppermute(value, "ctx", pairs)


def from_twin(value):
    return lax.ppermute(value, "ctx", [(at(z, x, 1 - c), at(z, x, c)) for z, x, c in places()])


def from_plane(value, step):
    return lax.ppermute(value, "kvh", [((s + step) % SIDE, s) for s in range(SIDE)])


def whole():
    return pl.BlockSpec(memory_space=pltpu.VMEM)


def stack_kernel(*refs):
    for i, ref in enumerate(refs[:-1]):
        refs[-1][i] = ref[...]


def stack(parts):
    return pl.pallas_call(
        stack_kernel,
        out_shape=jax.ShapeDtypeStruct((len(parts), *parts[0].shape), parts[0].dtype),
        in_specs=[whole()] * len(parts),
        out_specs=whole(),
        compiler_params=pltpu.CompilerParams(vmem_limit_bytes=8 * MIB),
        name="stack",
    )(*parts)


def dot_nt(a, b):
    return lax.dot_general(a, b, (((1,), (1,)), ((), ())), preferred_element_type=F32)


def weigh(s):
    most = jnp.max(s, axis=1, keepdims=True)
    w = jnp.exp2((s - most) * SCALE)
    exact = most * SCALE
    top = exact.astype(BF16).astype(F32)
    return top, jnp.exp2(exact - top), jnp.sum(w, axis=1, keepdims=True), w.astype(BF16)


def put_partial(out, index, top, total, summed):
    lane = lax.broadcasted_iota(jnp.int32, (ROWS, HD), 1)
    high = total.astype(BF16).astype(F32)
    low = total - high
    stats = jnp.zeros((ROWS, HD), F32)
    for g in range(GROUP):
        rows = slice(g * ROWS, (g + 1) * ROWS)
        out[index, :, g * HD : (g + 1) * HD] = summed[rows].astype(BF16)
        stats = jnp.where(lane == g, top[rows], stats)
        stats = jnp.where(lane == GROUP + g, high[rows], stats)
        stats = jnp.where(lane == 2 * GROUP + g, low[rows], stats)
    out[index, :, FEATS:] = stats.astype(BF16)


def assemble(info, begin, end, own, other, held):
    z, x, core = info[0], info[1], info[2]
    for dz in range(SIDE):
        plane = (z + dz) % SIDE

        def lay(zeros, ones, dz=dz, plane=plane):
            for dx in range(SIDE):
                zero, one = zeros(dz, dx), ones(dz, dx)
                for head in range(2):
                    for g in range(GROUP):
                        cols = slice(head * FEATS + g * HD, head * FEATS + (g + 1) * HD)
                        pair = jnp.concatenate([zero[:, cols].astype(F32), one[:, cols].astype(F32)], axis=0)
                        held[head, plane * SIDE + (x + dx) % SIDE, g * ROWS : (g + 1) * ROWS, :] = pair.astype(BF16)

        used = jnp.logical_and(2 * plane + 1 >= begin, 2 * plane < end)
        if dz == 0:
            used = True

        @pl.when(jnp.logical_and(used, core == 0))
        def _(lay=lay):
            lay(lambda dz, dx: own[dz][dx], lambda dz, dx: other[dx][dz])

        @pl.when(jnp.logical_and(used, core == 1))
        def _(lay=lay):
            lay(lambda dz, dx: other[dz][dx], lambda dz, dx: own[dx][dz])


def split_heads(cache, held):
    r = lax.broadcasted_iota(jnp.int32, (2 * HD, 2 * HD), 0)
    c = lax.broadcasted_iota(jnp.int32, (2 * HD, 2 * HD), 1)
    pick = (c == jnp.where(r < HD, 2 * r, 2 * (r - HD) + 1)).astype(BF16)
    for i in range(cache.shape[1] // HD):
        rows = slice(i * HD, (i + 1) * HD)
        both = cache[0, rows].reshape(2 * HD, 2 * HD)
        apart = jnp.dot(pick, both, preferred_element_type=F32).astype(BF16)
        held[0, rows] = apart[:HD]
        held[1, rows] = apart[HD:]


def attend_kernel(begin, with_new, info, valid, *refs):
    own, other, cache = refs[:SIDE], refs[SIDE : 2 * SIDE], refs[2 * SIDE]
    refs = refs[2 * SIDE + 1 :]
    if with_new:
        new, sent, mine, new_out, queries, keys = refs
    else:
        sent, mine, queries, keys = refs
    step = pl.program_id(0)
    last = pl.num_programs(0) - 1
    core = info[2]

    @pl.when(step == 0)
    def _():
        assemble(info, begin, begin + pl.num_programs(0), own, other, queries)

    request = begin + step
    count = valid[request]
    slot = cache.shape[1]
    where = [(head, out, half) for head, out in ((1 - core, sent), (core, mine)) for half in range(2)]

    def scores(head, _, half):
        return dot_nt(queries[head, 2 * request + half], keys[head, :, :HD])

    def finish(head, out, half, s):
        top, factor, total, w = weigh(s)
        summed = jnp.dot(w, keys[head, :, HD:], preferred_element_type=F32)
        put_partial(out, half, top, total * factor, summed * factor)

    @pl.when(count >= slot)
    def _():
        split_heads(cache, keys)
        s = scores(*where[0])
        for i, block in enumerate(where):
            later = scores(*where[i + 1]) if i + 1 < len(where) else None
            finish(*block, s)
            s = later

    @pl.when(jnp.logical_and(count > 0, count < slot))
    def _():
        split_heads(cache, keys)
        for block in where:
            s = scores(*block)
            position = lax.broadcasted_iota(jnp.int32, s.shape, 1)
            finish(*block, jnp.where(position < count, s, EMPTY))

    @pl.when(count <= 0)
    def _():
        lane = lax.broadcasted_iota(jnp.int32, (ROWS, WIDE), 1)
        tops = jnp.logical_and(lane >= FEATS, lane < FEATS + GROUP)
        none = jnp.where(tops, EMPTY, 0.0).astype(BF16)
        for _, out, half in where:
            out[half] = none

    if with_new:
        @pl.when(step == last)
        def _():
            z, x = info[0], info[1]
            s = dot_nt(queries[core, z * SIDE + x], new[0, :, :HD])
            token = (x % 2) * ROWS + lax.broadcasted_iota(jnp.int32, s.shape, 0) % ROWS
            key = lax.broadcasted_iota(jnp.int32, s.shape, 1)
            top, factor, total, w = weigh(jnp.where(key <= token, s, EMPTY))
            summed = jnp.dot(w, new[0, :, HD:], preferred_element_type=F32)
            put_partial(new_out, 0, top, total * factor, summed * factor)


def attend(info, valid, own, other, cache, new, begin, count):
    per = cache.shape[1]
    in_specs = [whole()] * (2 * SIDE) + [
        pl.BlockSpec((1, per, 2, 2 * HD), lambda i, info, valid: (begin + i, 0, 0, 0))
    ]
    out_specs = [pl.BlockSpec((2, ROWS, WIDE), lambda i, info, valid: (i, 0, 0))] * 2
    out_shape = [jax.ShapeDtypeStruct((2 * count, ROWS, WIDE), BF16)] * 2
    args = [*own, *other, cache]
    if new is not None:
        in_specs.append(whole())
        out_specs.append(pl.BlockSpec((1, ROWS, WIDE), lambda i, info, valid: (0, 0, 0)))
        out_shape.append(jax.ShapeDtypeStruct((1, ROWS, WIDE), BF16))
        args.append(new)
    return pl.pallas_call(
        functools.partial(attend_kernel, begin, new is not None),
        out_shape=out_shape,
        grid_spec=pltpu.PrefetchScalarGridSpec(
            num_scalar_prefetch=2,
            grid=(count,),
            in_specs=in_specs,
            out_specs=out_specs,
            scratch_shapes=[
                pltpu.VMEM((2, SIDE * SIDE, BLOCK, HD), BF16),
                pltpu.VMEM((2, per, 2 * HD), BF16),
            ],
        ),
        compiler_params=pltpu.CompilerParams(vmem_limit_bytes=50 * MIB),
        cost_estimate=pl.CostEstimate(
            flops=16 * count * BLOCK * per * HD, bytes_accessed=count * per * 4 * HD * 2, transcendentals=0
        ),
        name="attend_new" if new is not None else "attend",
    )(info, valid, *args)


def factors_of(parts):
    stats = [ref[index, :, FEATS:].astype(F32) for ref, index, _ in parts]
    tops = [
        p[:, :GROUP] if counts is None else jnp.where(counts, p[:, :GROUP], EMPTY)
        for p, (_, _, counts) in zip(stats, parts)
    ]
    totals = [p[:, GROUP : 2 * GROUP] + p[:, 2 * GROUP : 3 * GROUP] for p in stats]
    best = functools.reduce(jnp.maximum, tops)
    factors = [
        jnp.exp2(t - best) if counts is None else jnp.where(counts, jnp.exp2(t - best), 0.0)
        for t, (_, _, counts) in zip(tops, parts)
    ]
    return best, sum(f * t for f, t in zip(factors, totals)), factors


def summed_of(parts, factors, g):
    cols = slice(g * HD, (g + 1) * HD)
    return sum(f[:, g : g + 1] * ref[index, :, cols].astype(F32) for f, (ref, index, _) in zip(factors, parts))


def merge_into(jobs):
    ready = [factors_of(parts) for _, _, parts in jobs]
    for (out, index, _), (best, total, _) in zip(jobs, ready):
        high = total.astype(BF16)
        low = (total - high.astype(F32)).astype(BF16)
        rest = jnp.zeros((ROWS, HD - 3 * GROUP), BF16)
        out[index, :, FEATS:] = jnp.concatenate([best.astype(BF16), high, low, rest], axis=1)
    for (out, index, parts), (_, _, factors) in zip(jobs, ready):
        for g in range(GROUP):
            out[index, :, g * HD : (g + 1) * HD] = summed_of(parts, factors, g).astype(BF16)


def twin_kernel(info, *refs):
    mine_parts, got_parts, new = refs[:2], refs[2:4], refs[4]
    outs, (mine, got) = refs[5 : 5 + SIDE], refs[5 + SIDE :]
    for held, parts in ((mine, mine_parts), (got, got_parts)):
        first = 0
        for part in parts:
            held[first : first + part.shape[0]] = part[...]
            first += part.shape[0]
    z, x, core = info[0], info[1], info[2]
    jobs = []
    for d in range(SIDE):
        for j in range(SIDE):
            chip = jnp.where(core == 0, ((z + d) % SIDE) * SIDE + j, j * SIDE + (x + d) % SIDE)
            parts = [(mine, chip, None), (got, chip, None)]
            if d == 0:
                parts.append((new, 0, chip == z * SIDE + x))
            jobs.append((outs[d], j, parts))
    merge_into(jobs)


def merge_twins(info, mine, got, new):
    return pl.pallas_call(
        twin_kernel,
        out_shape=[jax.ShapeDtypeStruct((SIDE, ROWS, WIDE), BF16)] * SIDE,
        in_specs=[pl.BlockSpec(memory_space=pltpu.SMEM)] + [whole()] * 5,
        out_specs=[whole()] * SIDE,
        scratch_shapes=[pltpu.VMEM((SIDE * SIDE, ROWS, WIDE), BF16)] * 2,
        compiler_params=pltpu.CompilerParams(vmem_limit_bytes=24 * MIB),
        name="merge_twins",
    )(info, *mine, *got, new)


def four_kernel(*refs):
    out = refs[-1]
    merge_into([(out, j, [(ref, j, None) for ref in refs[:-1]]) for j in range(SIDE)])


def merge_four(parts):
    return pl.pallas_call(
        four_kernel,
        out_shape=jax.ShapeDtypeStruct((SIDE, ROWS, WIDE), BF16),
        in_specs=[whole()] * SIDE,
        out_specs=whole(),
        compiler_params=pltpu.CompilerParams(vmem_limit_bytes=24 * MIB),
        name="merge_four",
    )(*parts)


def final_kernel(*refs):
    out = refs[-1]
    blocks = [[(ref, j, None) for ref in refs[:-1]] for j in range(SIDE)]
    ready = []
    for parts in blocks:
        _, total, factors = factors_of(parts)
        ready.append([f / total for f in factors])
    for j, (parts, factors) in enumerate(zip(blocks, ready)):
        for g in range(GROUP):
            out[j, :, g * HD : (g + 1) * HD] = summed_of(parts, factors, g).astype(BF16)


def merge_final(parts):
    return pl.pallas_call(
        final_kernel,
        out_shape=jax.ShapeDtypeStruct((SIDE, ROWS, FEATS), BF16),
        in_specs=[whole()] * SIDE,
        out_specs=whole(),
        compiler_params=pltpu.CompilerParams(vmem_limit_bytes=24 * MIB),
        name="merge_final",
    )(*parts)


def project_kernel(info, *refs):
    own, other, weight = refs[:SIDE], refs[SIDE : 2 * SIDE], refs[2 * SIDE]
    keep, sends, held, acc = refs[2 * SIDE + 1], refs[2 * SIDE + 2 : 3 * SIDE + 1], refs[-2], refs[-1]
    step = pl.program_id(0)
    z, x, core, y = info[0], info[1], info[2], info[3]
    depth = weight.shape[0]
    per = FEATS // depth

    @pl.when(step == 0)
    def _():
        acc[...] = jnp.zeros_like(acc)

        def place(zero, one):
            for d in range(SIDE):
                for j in range(SIDE):
                    for half, values, chip in (
                        (0, zero, ((z + d) % SIDE) * SIDE + j),
                        (1, one, j * SIDE + (x + d) % SIDE),
                    ):
                        rows = pl.ds(pl.multiple_of(chip * ROWS, ROWS), ROWS)
                        for k in range(per):
                            held[half * per + k, rows, :] = values[d][j, :, k * depth : (k + 1) * depth]

        @pl.when(core == 0)
        def _():
            place(own, other)

        @pl.when(core == 1)
        def _():
            place(other, own)

    acc[...] += jnp.dot(held[step], weight[...], preferred_element_type=F32)

    @pl.when(step == pl.num_programs(0) - 1)
    def _():
        count = keep.shape[0]
        for d in range(SIDE):
            rows = acc[pl.ds(pl.multiple_of(((y + d) % SIDE) * count, count), count), :]
            if d == 0:
                keep[...] = rows
            else:
                sends[d - 1][...] = rows.astype(BF16)


def project(info, own, other, weight):
    depth = 1024
    cols = weight.shape[1]
    rows = SIDE * SIDE * ROWS
    return pl.pallas_call(
        project_kernel,
        out_shape=[jax.ShapeDtypeStruct((rows // SIDE, cols), F32)]
        + [jax.ShapeDtypeStruct((rows // SIDE, cols), BF16)] * (SIDE - 1),
        grid=(weight.shape[0] // depth,),
        in_specs=[pl.BlockSpec(memory_space=pltpu.SMEM)]
        + [whole()] * (2 * SIDE)
        + [pl.BlockSpec((depth, cols), lambda i: (i, 0))],
        out_specs=[whole()] * SIDE,
        scratch_shapes=[
            pltpu.VMEM((weight.shape[0] // depth, rows, depth), BF16),
            pltpu.VMEM((rows, cols), F32),
        ],
        compiler_params=pltpu.CompilerParams(vmem_limit_bytes=32 * MIB),
        name="project",
    )(info, *own, *other, weight)


def on_device(queries, cache, new_kv, lengths, out_weight):
    index = lax.axis_index("ctx")
    z, x, core = index // (2 * SIDE), (index // 2) % SIDE, index % 2
    info = jnp.stack([z, x, core, lax.axis_index("kvh")]).astype(jnp.int32)
    slot = cache.shape[1]
    valid = jnp.clip(lengths - index * slot, 0, slot).astype(jnp.int32)

    request = 2 * z + x // 2
    new = lax.dynamic_slice(new_kv, (request, 0, core, 0), (1, NEW, 1, 2 * HD)).reshape(1, NEW, 2 * HD)
    line = stack([queries] + [from_first(queries, s) for s in (1, 2, 3)])
    info, valid, new, line = lax.optimization_barrier((info, valid, new, line))
    own = [line] + [from_second(line, s) for s in (1, 2, 3)]
    other = [from_twin(part) for part in own]

    early = REQS - 2
    sent0, mine0 = attend(info, valid, own, other, cache, None, 0, early)
    got0 = from_twin(sent0)
    sent1, mine1, from_new = attend(info, valid, own, other, cache, new, early, REQS - early)
    parts = merge_twins(info, [mine0, mine1], [got0, from_twin(sent1)], from_new)
    zs = merge_four([parts[0]] + [from_second(parts[SIDE - s], s) for s in (1, 2, 3)])
    rows = merge_final([zs] + [from_first(zs, s) for s in (1, 2, 3)])

    own = [rows] + [from_second(rows, s) for s in (1, 2, 3)]
    other = [from_twin(part) for part in own]
    keep, *sends = project(info, own, other, out_weight)
    total = keep
    for d in (1, 2, 3):
        total = total + from_plane(sends[d - 1], SIDE - d).astype(F32)
    return total.astype(BF16)


def solution(mesh):
    placed = (
        P("ctx", "kvh"),
        P(None, "ctx", "kvh", None),
        P(None, None, "kvh", None),
        P(),
        P("kvh", "ctx"),
    )
    return jax.shard_map(
        on_device, mesh=mesh, in_specs=placed, out_specs=P("kvh", "ctx"), check_vma=False
    )
```

time: 135 us -> 120 us (0.89)
  local copies, waits for them, and re-layouts: 22 us -> 0.9 us
  Pallas kernels: 38.7 us -> 45.6 us
  starting transfers between devices: 24.6 us -> 31.4 us
  waiting for transfers between devices: 47 us -> 40.6 us
    unnamed x24 -> x7, local copies, waits for them, and re-layouts: 21.9 us -> 0.86 us
    pallas_call x2 -> x3, Pallas kernels: 29.9 us -> 38.6 us  [the longest x2 38.5 us: attend(): pl.pallas_call(functools.partial(attend_kernel, begin, new is not None),...]
    ppermute x9, waiting for transfers between devices: 27.7 us -> 21 us  [from_second(): return lax.ppermute(value, 'ctx', pairs)]
    ppermute x9, starting transfers between devices: 9.84 us -> 15.4 us  [from_second(): return lax.ppermute(value, 'ctx', pairs)]
    ppermute x9 -> x10, waiting for transfers between devices: 1.53 us -> 4.22 us  [from_twin(): lax.ppermute(value, 'ctx', [(at(z, x, 1 - c), at(z, x, c)) for z, x, c in...]
    ppermute x3, waiting for transfers between devices: 5.16 us -> 2.92 us  [from_plane(): lax.ppermute(value, 'kvh', [((s + step) % SIDE, s) for s in range(SIDE)])]
  transfers between devices with their start and end apart: 27 -> 28, of which waited for: 18 -> 18; matrix products, arithmetic and copies ran while one was open for 12% -> 1% of each run, Pallas kernels for 11% -> 9%
where the time goes in v2:
time: 120 us
  Pallas kernels  45.6 us (38%)
  waiting for transfers between devices  40.6 us (34%)
  starting transfers between devices  31.4 us (26%)
  other arithmetic  1.4 us (1%)
    pallas_call x2, Pallas kernels, attend(): pl.pallas_call(functools.partial(attend_kernel, begin, new is not None),...  38.5 us
    ppermute x9, waiting for transfers between devices, from_second(): return lax.ppermute(value, 'ctx', pairs)  21 us
    ppermute x9, starting transfers between devices, from_second(): return lax.ppermute(value, 'ctx', pairs)  15.4 us
    ppermute x6, waiting for transfers between devices, from_first(): return lax.ppermute(value, 'ctx', pairs)  12.4 us
    ppermute x6, starting transfers between devices, from_first(): return lax.ppermute(value, 'ctx', pairs)  8.44 us
    ppermute x3, starting transfers between devices, from_plane(): lax.ppermute(value, 'kvh', [((s + step) % SIDE, s) for s in range(SIDE)])  5.89 us
    ppermute x10, waiting for transfers between devices, from_twin(): lax.ppermute(value, 'ctx', [(at(z, x, 1 - c), at(z, x, c)) for z, x, c in...  4.22 us
    ppermute x3, waiting for transfers between devices, from_plane(): lax.ppermute(value, 'kvh', [((s + step) % SIDE, s) for s in range(SIDE)])  2.92 us
  transfers between devices with their start and end apart: 28, of which 18 were waited for; matrix products, arithmetic and copies ran while one was open for 1% of the time, Pallas kernels for 9%

profile of v2, /device:TPU:0, one launch (start us, length us, event | category | flops | bytes accessed | tf_op | source)
XLA Modules:
  0.0 120.0 jit_solution(6806394768926504897)
XLA Ops:
  0.0 3.1 %collective-permute-start.1 = (bf16[8,4096]{1,0:T(8,128)(2,1)}, bf16[8,4096]{1,0:T(8,128)(2,1)S(1)}, u32[]{:S(2)}, u32[]{:S(2)}) collective-permute-start(bf16[8,4096]{1,0:T(8,128)(2,1)} %refs_0_.1), channel_id=1, source_target_pairs={{16,0},{68,4},{24,8},{76,12},{0,16},{84,20},{8,24},{92,28},{48,32}... | collective-permute-start | bytes 196616 | tf_op jit(solution)/shard_map/ppermute | solution.py:38
  3.1 1.1 collective-permute-start
  6.0 1.6 %collective-permute-done.refs_1_ = bf16[8,4096]{1,0:T(8,128)(2,1)S(1)} collective-permute-done((bf16[8,4096]{1,0:T(8,128)(2,1)}, bf16[8,4096]{1,0:T(8,128)(2,1)S(1)}, u32[]{:S(2)}, u32[]{:S(2)}) %collective-permute-start) | collective-permute-done | bytes 65568 | tf_op jit(solution)/shard_map/ppermute | solution.py:38
  7.6 2.4 %collective-permute-done.2.refs_3_ = bf16[8,4096]{1,0:T(8,128)(2,1)S(1)} collective-permute-done((bf16[8,4096]{1,0:T(8,128)(2,1)}, bf16[8,4096]{1,0:T(8,128)(2,1)S(1)}, u32[]{:S(2)}, u32[]{:S(2)}) %collective-permute-start.2) | collective-permute-done | bytes 65568 | tf_op jit(solution)/shard_map/ppermute | solution.py:38
  10.8 2.0 %collective-permute-start.5 = (bf16[4,8,4096]{2,1,0:T(8,128)(2,1)S(1)}, bf16[4,8,4096]{2,1,0:T(8,128)(2,1)S(1)}, u32[]{:S(2)}, u32[]{:S(2)}) collective-permute-start(bf16[4,8,4096]{2,1,0:T(8,128)(2,1)S(1)} %stack.21.refs_0_), channel_id=1, source_target_pairs={{96,0},{28,4},{104,8},{4,12},{112,16},{12,20},{120,24},{20,28},{0,... | collective-permute-start | bytes 786440 | tf_op jit(solution)/shard_map/ppermute | solution.py:43
  12.8 3.6 %collective-permute-start.4 = (bf16[4,8,4096]{2,1,0:T(8,128)(2,1)S(1)}, bf16[4,8,4096]{2,1,0:T(8,128)(2,1)S(1)}, u32[]{:S(2)}, u32[]{:S(2)}) collective-permute-start(bf16[4,8,4096]{2,1,0:T(8,128)(2,1)S(1)} %stack.21.refs_0_), channel_id=1, source_target_pairs={{64,0},{20,4},{72,8},{28,12},{80,16},{4,20},{88,24},{12,28},{96,32... | collective-permute-start | bytes 786440 | tf_op jit(solution)/shard_map/ppermute | solution.py:43
  16.4 1.0 collective-permute-start.3
  17.4 1.9 %collective-permute-done.5.refs_3_ = bf16[4,8,4096]{2,1,0:T(8,128)(2,1)S(1)} collective-permute-done((bf16[4,8,4096]{2,1,0:T(8,128)(2,1)S(1)}, bf16[4,8,4096]{2,1,0:T(8,128)(2,1)S(1)}, u32[]{:S(2)}, u32[]{:S(2)}) %collective-permute-start.5) | collective-permute-done | bytes 262176 | tf_op jit(solution)/shard_map/ppermute | solution.py:43
  19.3 4.3 %collective-permute-done.4.refs_2_ = bf16[4,8,4096]{2,1,0:T(8,128)(2,1)S(1)} collective-permute-done((bf16[4,8,4096]{2,1,0:T(8,128)(2,1)S(1)}, bf16[4,8,4096]{2,1,0:T(8,128)(2,1)S(1)}, u32[]{:S(2)}, u32[]{:S(2)}) %collective-permute-start.4) | collective-permute-done | bytes 262176 | tf_op jit(solution)/shard_map/ppermute | solution.py:43
  24.0 1.0 collective-permute-done.8.refs_6_
  25.4 27.3 %attend.1 = (bf16[12,16,2176]{2,1,0:T(8,128)(2,1)S(1)}, bf16[12,16,2176]{2,1,0:T(8,128)(2,1)S(1)}) custom-call(s32[4]{0:T(128)S(1)} %pad_add_fusion.info, s32[8]{0:T(128)S(1)} %subtract_clamp_fusion.valid, bf16[4,8,4096]{2,1,0:T(8,128)(2,1)S(1)} %stack.21.refs_0_, bf16[4,8,4096]{2,1,0:T(8,128)(2,1)S(1)} %collective-permute-done.3.refs_1_, ...), custom_call_target="tpu_custom_call" | custom-call | flops 6442450944 | bytes 12582912 | tf_op jit(solution)/shard_map/attend/pallas_call | solution.py:217
  53.2 11.3 %attend_new.1 = (bf16[4,16,2176]{2,1,0:T(8,128)(2,1)S(1)}, bf16[4,16,2176]{2,1,0:T(8,128)(2,1)S(1)}, bf16[1,16,2176]{2,1,0:T(8,128)(2,1)S(1)}) custom-call(s32[4]{0:T(128)S(1)} %pad_add_fusion.info, s32[8]{0:T(128)S(1)} %subtract_clamp_fusion.valid, bf16[4,8,4096]{2,1,0:T(8,128)(2,1)S(1)} %stack.21.refs_0_, ...), custom_call_target="tpu_custom_call" | custom-call | flops 2147483648 | bytes 4194304 | tf_op jit(solution)/shard_map/attend_new/pallas_call | solution.py:217
  64.7 1.4 %collective-permute-done.11.refs_3_ = bf16[4,16,2176]{2,1,0:T(8,128)(2,1)S(1)} collective-permute-done((bf16[4,16,2176]{2,1,0:T(8,128)(2,1)S(1)}, bf16[4,16,2176]{2,1,0:T(8,128)(2,1)S(1)}, u32[]{:S(2)}, u32[]{:S(2)}) %collective-permute-start.11) | collective-permute-done | bytes 278560 | tf_op jit(solution)/shard_map/ppermute | solution.py:47
  66.1 2.8 %merge_twins.1 = (bf16[4,16,2176]{2,1,0:T(8,128)(2,1)S(1)}, bf16[4,16,2176]{2,1,0:T(8,128)(2,1)S(1)}, bf16[4,16,2176]{2,1,0:T(8,128)(2,1)S(1)}, bf16[4,16,2176]{2,1,0:T(8,128)(2,1)S(1)}) custom-call(s32[4]{0:T(128)S(1)} %pad_add_fusion.info, bf16[12,16,2176]{2,1,0:T(8,128)(2,1)S(1)} %get-tuple-element.25.refs_0_, ...), custom_call_target="tpu_custom_call" | custom-call | tf_op jit(solution)/shard_map/merge_twins/pallas_call | solution.py:291
  69.2 3.2 %collective-permute-start.13 = (bf16[4,16,2176]{2,1,0:T(8,128)(2,1)S(1)}, bf16[4,16,2176]{2,1,0:T(8,128)(2,1)S(1)}, u32[]{:S(2)}, u32[]{:S(2)}) collective-permute-start(bf16[4,16,2176]{2,1,0:T(8,128)(2,1)S(1)} %get-tuple-element.33), channel_id=1, source_target_pairs={{64,0},{20,4},{72,8},{28,12},{80,16},{4,20},{88,24},{12,28},{96,32... | collective-permute-start | bytes 835592 | tf_op jit(solution)/shard_map/ppermute | solution.py:43
  72.4 3.3 %collective-permute-done.12.refs_1_ = bf16[4,16,2176]{2,1,0:T(8,128)(2,1)S(1)} collective-permute-done((bf16[4,16,2176]{2,1,0:T(8,128)(2,1)S(1)}, bf16[4,16,2176]{2,1,0:T(8,128)(2,1)S(1)}, u32[]{:S(2)}, u32[]{:S(2)}) %collective-permute-start.12) | collective-permute-done | bytes 278560 | tf_op jit(solution)/shard_map/ppermute | solution.py:43
  75.8 1.6 %collective-permute-done.13.refs_2_ = bf16[4,16,2176]{2,1,0:T(8,128)(2,1)S(1)} collective-permute-done((bf16[4,16,2176]{2,1,0:T(8,128)(2,1)S(1)}, bf16[4,16,2176]{2,1,0:T(8,128)(2,1)S(1)}, u32[]{:S(2)}, u32[]{:S(2)}) %collective-permute-start.13) | collective-permute-done | bytes 278560 | tf_op jit(solution)/shard_map/ppermute | solution.py:43
  77.4 2.9 %collective-permute-done.14.refs_3_ = bf16[4,16,2176]{2,1,0:T(8,128)(2,1)S(1)} collective-permute-done((bf16[4,16,2176]{2,1,0:T(8,128)(2,1)S(1)}, bf16[4,16,2176]{2,1,0:T(8,128)(2,1)S(1)}, u32[]{:S(2)}, u32[]{:S(2)}) %collective-permute-start.14) | collective-permute-done | bytes 278560 | tf_op jit(solution)/shard_map/ppermute | solution.py:43
  81.3 1.4 %collective-permute-start.16 = (bf16[4,16,2176]{2,1,0:T(8,128)(2,1)S(1)}, bf16[4,16,2176]{2,1,0:T(8,128)(2,1)S(1)}, u32[]{:S(2)}, u32[]{:S(2)}) collective-permute-start(bf16[4,16,2176]{2,1,0:T(8,128)(2,1)S(1)} %merge_four.1.refs_0_), channel_id=1, source_target_pairs={{16,0},{68,4},{24,8},{76,12},{0,16},{84,20},{8,24},{92,28},{48,32}... | collective-permute-start | bytes 835592 | tf_op jit(solution)/shard_map/ppermute | solution.py:38
  82.7 1.8 %collective-permute-start.15 = (bf16[4,16,2176]{2,1,0:T(8,128)(2,1)S(1)}, bf16[4,16,2176]{2,1,0:T(8,128)(2,1)S(1)}, u32[]{:S(2)}, u32[]{:S(2)}) collective-permute-start(bf16[4,16,2176]{2,1,0:T(8,128)(2,1)S(1)} %merge_four.1.refs_0_), channel_id=1, source_target_pairs={{8,0},{36,4},{16,8},{44,12},{24,16},{52,20},{0,24},{60,28},{40,32}... | collective-permute-start | bytes 835592 | tf_op jit(solution)/shard_map/ppermute | solution.py:38
  84.5 7.5 %collective-permute-done.17.refs_3_ = bf16[4,16,2176]{2,1,0:T(8,128)(2,1)S(1)} collective-permute-done((bf16[4,16,2176]{2,1,0:T(8,128)(2,1)S(1)}, bf16[4,16,2176]{2,1,0:T(8,128)(2,1)S(1)}, u32[]{:S(2)}, u32[]{:S(2)}) %collective-permute-start.17) | collective-permute-done | bytes 278560 | tf_op jit(solution)/shard_map/ppermute | solution.py:38
  92.0 0.9 collective-permute-done.15.refs_1_
  93.8 1.7 %collective-permute-start.20 = (bf16[4,16,2048]{2,1,0:T(8,128)(2,1)S(1)}, bf16[4,16,2048]{2,1,0:T(8,128)(2,1)S(1)}, u32[]{:S(2)}, u32[]{:S(2)}) collective-permute-start(bf16[4,16,2048]{2,1,0:T(8,128)(2,1)S(1)} %merge_final.1.refs_0_), channel_id=1, source_target_pairs={{96,0},{28,4},{104,8},{4,12},{112,16},{12,20},{120,24},{20,28},{0,... | collective-permute-start | bytes 786440 | tf_op jit(solution)/shard_map/ppermute | solution.py:43
  95.5 3.4 %collective-permute-start.19 = (bf16[4,16,2048]{2,1,0:T(8,128)(2,1)S(1)}, bf16[4,16,2048]{2,1,0:T(8,128)(2,1)S(1)}, u32[]{:S(2)}, u32[]{:S(2)}) collective-permute-start(bf16[4,16,2048]{2,1,0:T(8,128)(2,1)S(1)} %merge_final.1.refs_0_), channel_id=1, source_target_pairs={{64,0},{20,4},{72,8},{28,12},{80,16},{4,20},{88,24},{12,28},{96,32... | collective-permute-start | bytes 786440 | tf_op jit(solution)/shard_map/ppermute | solution.py:43
  99.0 2.7 %collective-permute-done.20.refs_3_ = bf16[4,16,2048]{2,1,0:T(8,128)(2,1)S(1)} collective-permute-done((bf16[4,16,2048]{2,1,0:T(8,128)(2,1)S(1)}, bf16[4,16,2048]{2,1,0:T(8,128)(2,1)S(1)}, u32[]{:S(2)}, u32[]{:S(2)}) %collective-permute-start.20) | collective-permute-done | bytes 262176 | tf_op jit(solution)/shard_map/ppermute | solution.py:43
  101.7 4.3 %collective-permute-done.19.refs_2_ = bf16[4,16,2048]{2,1,0:T(8,128)(2,1)S(1)} collective-permute-done((bf16[4,16,2048]{2,1,0:T(8,128)(2,1)S(1)}, bf16[4,16,2048]{2,1,0:T(8,128)(2,1)S(1)}, u32[]{:S(2)}, u32[]{:S(2)}) %collective-permute-start.19) | collective-permute-done | bytes 262176 | tf_op jit(solution)/shard_map/ppermute | solution.py:43
  106.5 1.0 collective-permute-done.23.refs_6_
  107.9 2.6 %project.1 = (f32[64,512]{1,0:T(8,128)S(1)}, bf16[64,512]{1,0:T(8,128)(2,1)S(1)}, bf16[64,512]{1,0:T(8,128)(2,1)S(1)}, bf16[64,512]{1,0:T(8,128)(2,1)S(1)}) custom-call(s32[4]{0:T(128)S(1)} %pad_add_fusion.info, bf16[4,16,2048]{2,1,0:T(8,128)(2,1)S(1)} %merge_final.1.refs_0_, bf16[4,16,2048]{2,1,0:T(8,128)(2,1)S(1)} %collective-permute-done.18.refs_1_, ...), custom_call_target="tpu_custom_call" | custom-call | tf_op jit(solution)/shard_map/project/pallas_call | solution.py:389
  110.5 1.6 %collective-permute-start.25 = (bf16[64,512]{1,0:T(8,128)(2,1)S(1)}, bf16[64,512]{1,0:T(8,128)(2,1)S(1)}, u32[]{:S(2)}, u32[]{:S(2)}) collective-permute-start(bf16[64,512]{1,0:T(8,128)(2,1)S(1)} %get-tuple-element.36), channel_id=1, source_target_pairs={{3,0},{0,1},{1,2},{2,3},{7,4},{4,5},{5,6},{6,7},{11,8},{8,9},{9,10... | collective-permute-start | bytes 196616 | tf_op jit(solution)/shard_map/ppermute | solution.py:51
  112.1 2.9 %collective-permute-start.26 = (bf16[64,512]{1,0:T(8,128)(2,1)S(1)}, bf16[64,512]{1,0:T(8,128)(2,1)S(1)}, u32[]{:S(2)}, u32[]{:S(2)}) collective-permute-start(bf16[64,512]{1,0:T(8,128)(2,1)S(1)} %get-tuple-element.37), channel_id=1, source_target_pairs={{2,0},{3,1},{0,2},{1,3},{6,4},{7,5},{4,6},{5,7},{10,8},{11,9},{8,1... | collective-permute-start | bytes 196616 | tf_op jit(solution)/shard_map/ppermute | solution.py:51
  115.1 1.3 %collective-permute-start.27 = (bf16[64,512]{1,0:T(8,128)(2,1)S(1)}, bf16[64,512]{1,0:T(8,128)(2,1)S(1)}, u32[]{:S(2)}, u32[]{:S(2)}) collective-permute-start(bf16[64,512]{1,0:T(8,128)(2,1)S(1)} %get-tuple-element.38), channel_id=1, source_target_pairs={{1,0},{2,1},{3,2},{0,3},{5,4},{6,5},{7,6},{4,7},{9,8},{10,9},{11,1... | collective-permute-start | bytes 196616 | tf_op jit(solution)/shard_map/ppermute | solution.py:51
  116.4 2.2 %collective-permute-done.26 = bf16[64,512]{1,0:T(8,128)(2,1)S(1)} collective-permute-done((bf16[64,512]{1,0:T(8,128)(2,1)S(1)}, bf16[64,512]{1,0:T(8,128)(2,1)S(1)}, u32[]{:S(2)}, u32[]{:S(2)}) %collective-permute-start.26) | collective-permute-done | bytes 65568 | tf_op jit(solution)/shard_map/ppermute | solution.py:51
  (42 shorter events, 8.8 us)
Async XLA Ops:
  0.0 5.1 %copy-start = (bf16[8,32,2,256]{3,2,1,0:T(2,128)(2,1)S(1)}, bf16[8,32,2,256]{3,2,1,0:T(2,128)(2,1)}, u32[]{:S(2)}) copy-start(bf16[8,32,2,256]{3,2,1,0:T(2,128)(2,1)} %param.7) | copy-start | bytes 786436
  0.0 6.0 %collective-permute-start.1 = (bf16[8,4096]{1,0:T(8,128)(2,1)}, bf16[8,4096]{1,0:T(8,128)(2,1)S(1)}, u32[]{:S(2)}, u32[]{:S(2)}) collective-permute-start(bf16[8,4096]{1,0:T(8,128)(2,1)} %refs_0_.1), channel_id=1, source_target_pairs={{16,0},{68,4},{24,8},{76,12},{0,16},{84,20},{8,24},{92,28},{48,32}... | collective-permute-start | bytes 196616 | tf_op jit(solution)/shard_map/ppermute | solution.py:38
  3.1 4.5 %collective-permute-start = (bf16[8,4096]{1,0:T(8,128)(2,1)}, bf16[8,4096]{1,0:T(8,128)(2,1)S(1)}, u32[]{:S(2)}, u32[]{:S(2)}) collective-permute-start(bf16[8,4096]{1,0:T(8,128)(2,1)} %refs_0_.1), channel_id=1, source_target_pairs={{8,0},{36,4},{16,8},{44,12},{24,16},{52,20},{0,24},{60,28},{40,32}... | collective-permute-start | bytes 196616 | tf_op jit(solution)/shard_map/ppermute | solution.py:38
  4.3 5.7 %collective-permute-start.2 = (bf16[8,4096]{1,0:T(8,128)(2,1)}, bf16[8,4096]{1,0:T(8,128)(2,1)S(1)}, u32[]{:S(2)}, u32[]{:S(2)}) collective-permute-start(bf16[8,4096]{1,0:T(8,128)(2,1)} %refs_0_.1), channel_id=1, source_target_pairs={{24,0},{100,4},{0,8},{108,12},{8,16},{116,20},{16,24},{124,28},{56... | collective-permute-start | bytes 196616 | tf_op jit(solution)/shard_map/ppermute | solution.py:38
  9.9 0.8 copy-start.2
  10.8 8.5 %collective-permute-start.5 = (bf16[4,8,4096]{2,1,0:T(8,128)(2,1)S(1)}, bf16[4,8,4096]{2,1,0:T(8,128)(2,1)S(1)}, u32[]{:S(2)}, u32[]{:S(2)}) collective-permute-start(bf16[4,8,4096]{2,1,0:T(8,128)(2,1)S(1)} %stack.21.refs_0_), channel_id=1, source_target_pairs={{96,0},{28,4},{104,8},{4,12},{112,16},{12,20},{120,24},{20,28},{0,... | collective-permute-start | bytes 786440 | tf_op jit(solution)/shard_map/ppermute | solution.py:43
  12.8 10.7 %collective-permute-start.4 = (bf16[4,8,4096]{2,1,0:T(8,128)(2,1)S(1)}, bf16[4,8,4096]{2,1,0:T(8,128)(2,1)S(1)}, u32[]{:S(2)}, u32[]{:S(2)}) collective-permute-start(bf16[4,8,4096]{2,1,0:T(8,128)(2,1)S(1)} %stack.21.refs_0_), channel_id=1, source_target_pairs={{64,0},{20,4},{72,8},{28,12},{80,16},{4,20},{88,24},{12,28},{96,32... | collective-permute-start | bytes 786440 | tf_op jit(solution)/shard_map/ppermute | solution.py:43
  16.4 7.2 %collective-permute-start.3 = (bf16[4,8,4096]{2,1,0:T(8,128)(2,1)S(1)}, bf16[4,8,4096]{2,1,0:T(8,128)(2,1)S(1)}, u32[]{:S(2)}, u32[]{:S(2)}) collective-permute-start(bf16[4,8,4096]{2,1,0:T(8,128)(2,1)S(1)} %stack.21.refs_0_), channel_id=1, source_target_pairs={{32,0},{12,4},{40,8},{20,12},{48,16},{28,20},{56,24},{4,28},{64,32... | collective-permute-start | bytes 786440 | tf_op jit(solution)/shard_map/ppermute | solution.py:43
  17.4 6.7 %collective-permute-start.6 = (bf16[4,8,4096]{2,1,0:T(8,128)(2,1)S(1)}, bf16[4,8,4096]{2,1,0:T(8,128)(2,1)S(1)}, u32[]{:S(2)}, u32[]{:S(2)}) collective-permute-start(bf16[4,8,4096]{2,1,0:T(8,128)(2,1)S(1)} %stack.21.refs_0_), channel_id=1, source_target_pairs={{4,0},{0,4},{12,8},{8,12},{20,16},{16,20},{28,24},{24,28},{36,32},... | collective-permute-start | bytes 786440 | tf_op jit(solution)/shard_map/ppermute | solution.py:47
  19.3 4.8 %collective-permute-start.9 = (bf16[4,8,4096]{2,1,0:T(8,128)(2,1)S(1)}, bf16[4,8,4096]{2,1,0:T(8,128)(2,1)S(1)}, u32[]{:S(2)}, u32[]{:S(2)}) collective-permute-start(bf16[4,8,4096]{2,1,0:T(8,128)(2,1)S(1)} %collective-permute-done.5.refs_3_), channel_id=1, source_target_pairs={{4,0},{0,4},{12,8},{8,12},{20,16},{16,20},{28,24},{24,28},{36,32},... | collective-permute-start | bytes 786440 | tf_op jit(solution)/shard_map/ppermute | solution.py:47
  23.5 1.5 %collective-permute-start.8 = (bf16[4,8,4096]{2,1,0:T(8,128)(2,1)S(1)}, bf16[4,8,4096]{2,1,0:T(8,128)(2,1)S(1)}, u32[]{:S(2)}, u32[]{:S(2)}) collective-permute-start(bf16[4,8,4096]{2,1,0:T(8,128)(2,1)S(1)} %collective-permute-done.4.refs_2_), channel_id=1, source_target_pairs={{4,0},{0,4},{12,8},{8,12},{20,16},{16,20},{28,24},{24,28},{36,32},... | collective-permute-start | bytes 786440 | tf_op jit(solution)/shard_map/ppermute | solution.py:47
  23.5 1.9 %collective-permute-start.7 = (bf16[4,8,4096]{2,1,0:T(8,128)(2,1)S(1)}, bf16[4,8,4096]{2,1,0:T(8,128)(2,1)S(1)}, u32[]{:S(2)}, u32[]{:S(2)}) collective-permute-start(bf16[4,8,4096]{2,1,0:T(8,128)(2,1)S(1)} %collective-permute-done.3.refs_1_), channel_id=1, source_target_pairs={{4,0},{0,4},{12,8},{8,12},{20,16},{16,20},{28,24},{24,28},{36,32},... | collective-permute-start | bytes 786440 | tf_op jit(solution)/shard_map/ppermute | solution.py:47
  52.7 55.2 %copy-start.1 = (bf16[4096,512]{1,0:T(8,128)(2,1)S(1)}, bf16[4096,512]{1,0:T(8,128)(2,1)}, u32[]{:S(2)}) copy-start(bf16[4096,512]{1,0:T(8,128)(2,1)} %refs_8_.5) | copy-start | bytes 12582916
  52.7 13.4 %collective-permute-start.10 = (bf16[12,16,2176]{2,1,0:T(8,128)(2,1)S(1)}, bf16[12,16,2176]{2,1,0:T(8,128)(2,1)S(1)}, u32[]{:S(2)}, u32[]{:S(2)}) collective-permute-start(bf16[12,16,2176]{2,1,0:T(8,128)(2,1)S(1)} %get-tuple-element.28), channel_id=1, source_target_pairs={{4,0},{0,4},{12,8},{8,12},{20,16},{16,20},{28,24},{24,28},{36,32},... | collective-permute-start | bytes 2506760 | tf_op jit(solution)/shard_map/ppermute | solution.py:47
  64.4 1.6 %collective-permute-start.11 = (bf16[4,16,2176]{2,1,0:T(8,128)(2,1)S(1)}, bf16[4,16,2176]{2,1,0:T(8,128)(2,1)S(1)}, u32[]{:S(2)}, u32[]{:S(2)}) collective-permute-start(bf16[4,16,2176]{2,1,0:T(8,128)(2,1)S(1)} %get-tuple-element.29), channel_id=1, source_target_pairs={{4,0},{0,4},{12,8},{8,12},{20,16},{16,20},{28,24},{24,28},{36,32},... | collective-permute-start | bytes 835592 | tf_op jit(solution)/shard_map/ppermute | solution.py:47
  68.9 6.9 %collective-permute-start.12 = (bf16[4,16,2176]{2,1,0:T(8,128)(2,1)S(1)}, bf16[4,16,2176]{2,1,0:T(8,128)(2,1)S(1)}, u32[]{:S(2)}, u32[]{:S(2)}) collective-permute-start(bf16[4,16,2176]{2,1,0:T(8,128)(2,1)S(1)} %get-tuple-element.32), channel_id=1, source_target_pairs={{32,0},{12,4},{40,8},{20,12},{48,16},{28,20},{56,24},{4,28},{64,32... | collective-permute-start | bytes 835592 | tf_op jit(solution)/shard_map/ppermute | solution.py:43
  69.2 8.2 %collective-permute-start.13 = (bf16[4,16,2176]{2,1,0:T(8,128)(2,1)S(1)}, bf16[4,16,2176]{2,1,0:T(8,128)(2,1)S(1)}, u32[]{:S(2)}, u32[]{:S(2)}) collective-permute-start(bf16[4,16,2176]{2,1,0:T(8,128)(2,1)S(1)} %get-tuple-element.33), channel_id=1, source_target_pairs={{64,0},{20,4},{72,8},{28,12},{80,16},{4,20},{88,24},{12,28},{96,32... | collective-permute-start | bytes 835592 | tf_op jit(solution)/shard_map/ppermute | solution.py:43
  72.4 7.9 %collective-permute-start.14 = (bf16[4,16,2176]{2,1,0:T(8,128)(2,1)S(1)}, bf16[4,16,2176]{2,1,0:T(8,128)(2,1)S(1)}, u32[]{:S(2)}, u32[]{:S(2)}) collective-permute-start(bf16[4,16,2176]{2,1,0:T(8,128)(2,1)S(1)} %get-tuple-element.34), channel_id=1, source_target_pairs={{96,0},{28,4},{104,8},{4,12},{112,16},{12,20},{120,24},{20,28},{0,... | collective-permute-start | bytes 835592 | tf_op jit(solution)/shard_map/ppermute | solution.py:43
  81.2 10.8 %collective-permute-start.17 = (bf16[4,16,2176]{2,1,0:T(8,128)(2,1)S(1)}, bf16[4,16,2176]{2,1,0:T(8,128)(2,1)S(1)}, u32[]{:S(2)}, u32[]{:S(2)}) collective-permute-start(bf16[4,16,2176]{2,1,0:T(8,128)(2,1)S(1)} %merge_four.1.refs_0_), channel_id=1, source_target_pairs={{24,0},{100,4},{0,8},{108,12},{8,16},{116,20},{16,24},{124,28},{56... | collective-permute-start | bytes 835592 | tf_op jit(solution)/shard_map/ppermute | solution.py:38
  81.3 10.7 %collective-permute-start.16 = (bf16[4,16,2176]{2,1,0:T(8,128)(2,1)S(1)}, bf16[4,16,2176]{2,1,0:T(8,128)(2,1)S(1)}, u32[]{:S(2)}, u32[]{:S(2)}) collective-permute-start(bf16[4,16,2176]{2,1,0:T(8,128)(2,1)S(1)} %merge_four.1.refs_0_), channel_id=1, source_target_pairs={{16,0},{68,4},{24,8},{76,12},{0,16},{84,20},{8,24},{92,28},{48,32}... | collective-permute-start | bytes 835592 | tf_op jit(solution)/shard_map/ppermute | solution.py:38
  82.7 10.2 %collective-permute-start.15 = (bf16[4,16,2176]{2,1,0:T(8,128)(2,1)S(1)}, bf16[4,16,2176]{2,1,0:T(8,128)(2,1)S(1)}, u32[]{:S(2)}, u32[]{:S(2)}) collective-permute-start(bf16[4,16,2176]{2,1,0:T(8,128)(2,1)S(1)} %merge_four.1.refs_0_), channel_id=1, source_target_pairs={{8,0},{36,4},{16,8},{44,12},{24,16},{52,20},{0,24},{60,28},{40,32}... | collective-permute-start | bytes 835592 | tf_op jit(solution)/shard_map/ppermute | solution.py:38
  93.8 8.0 %collective-permute-start.20 = (bf16[4,16,2048]{2,1,0:T(8,128)(2,1)S(1)}, bf16[4,16,2048]{2,1,0:T(8,128)(2,1)S(1)}, u32[]{:S(2)}, u32[]{:S(2)}) collective-permute-start(bf16[4,16,2048]{2,1,0:T(8,128)(2,1)S(1)} %merge_final.1.refs_0_), channel_id=1, source_target_pairs={{96,0},{28,4},{104,8},{4,12},{112,16},{12,20},{120,24},{20,28},{0,... | collective-permute-start | bytes 786440 | tf_op jit(solution)/shard_map/ppermute | solution.py:43
  95.5 10.5 %collective-permute-start.19 = (bf16[4,16,2048]{2,1,0:T(8,128)(2,1)S(1)}, bf16[4,16,2048]{2,1,0:T(8,128)(2,1)S(1)}, u32[]{:S(2)}, u32[]{:S(2)}) collective-permute-start(bf16[4,16,2048]{2,1,0:T(8,128)(2,1)S(1)} %merge_final.1.refs_0_), channel_id=1, source_target_pairs={{64,0},{20,4},{72,8},{28,12},{80,16},{4,20},{88,24},{12,28},{96,32... | collective-permute-start | bytes 786440 | tf_op jit(solution)/shard_map/ppermute | solution.py:43
  98.8 7.2 %collective-permute-start.18 = (bf16[4,16,2048]{2,1,0:T(8,128)(2,1)S(1)}, bf16[4,16,2048]{2,1,0:T(8,128)(2,1)S(1)}, u32[]{:S(2)}, u32[]{:S(2)}) collective-permute-start(bf16[4,16,2048]{2,1,0:T(8,128)(2,1)S(1)} %merge_final.1.refs_0_), channel_id=1, source_target_pairs={{32,0},{12,4},{40,8},{20,12},{48,16},{28,20},{56,24},{4,28},{64,32... | collective-permute-start | bytes 786440 | tf_op jit(solution)/shard_map/ppermute | solution.py:43
  99.0 7.5 %collective-permute-start.21 = (bf16[4,16,2048]{2,1,0:T(8,128)(2,1)S(1)}, bf16[4,16,2048]{2,1,0:T(8,128)(2,1)S(1)}, u32[]{:S(2)}, u32[]{:S(2)}) collective-permute-start(bf16[4,16,2048]{2,1,0:T(8,128)(2,1)S(1)} %merge_final.1.refs_0_), channel_id=1, source_target_pairs={{4,0},{0,4},{12,8},{8,12},{20,16},{16,20},{28,24},{24,28},{36,32},... | collective-permute-start | bytes 786440 | tf_op jit(solution)/shard_map/ppermute | solution.py:47
  101.7 4.8 %collective-permute-start.24 = (bf16[4,16,2048]{2,1,0:T(8,128)(2,1)S(1)}, bf16[4,16,2048]{2,1,0:T(8,128)(2,1)S(1)}, u32[]{:S(2)}, u32[]{:S(2)}) collective-permute-start(bf16[4,16,2048]{2,1,0:T(8,128)(2,1)S(1)} %collective-permute-done.20.refs_3_), channel_id=1, source_target_pairs={{4,0},{0,4},{12,8},{8,12},{20,16},{16,20},{28,24},{24,28},{36,32},... | collective-permute-start | bytes 786440 | tf_op jit(solution)/shard_map/ppermute | solution.py:47
  106.0 1.5 %collective-permute-start.23 = (bf16[4,16,2048]{2,1,0:T(8,128)(2,1)S(1)}, bf16[4,16,2048]{2,1,0:T(8,128)(2,1)S(1)}, u32[]{:S(2)}, u32[]{:S(2)}) collective-permute-start(bf16[4,16,2048]{2,1,0:T(8,128)(2,1)S(1)} %collective-permute-done.19.refs_2_), channel_id=1, source_target_pairs={{4,0},{0,4},{12,8},{8,12},{20,16},{16,20},{28,24},{24,28},{36,32},... | collective-permute-start | bytes 786440 | tf_op jit(solution)/shard_map/ppermute | solution.py:47
  106.0 1.9 %collective-permute-start.22 = (bf16[4,16,2048]{2,1,0:T(8,128)(2,1)S(1)}, bf16[4,16,2048]{2,1,0:T(8,128)(2,1)S(1)}, u32[]{:S(2)}, u32[]{:S(2)}) collective-permute-start(bf16[4,16,2048]{2,1,0:T(8,128)(2,1)S(1)} %collective-permute-done.18.refs_1_), channel_id=1, source_target_pairs={{4,0},{0,4},{12,8},{8,12},{20,16},{16,20},{28,24},{24,28},{36,32},... | collective-permute-start | bytes 786440 | tf_op jit(solution)/shard_map/ppermute | solution.py:47
  110.5 5.9 %collective-permute-start.25 = (bf16[64,512]{1,0:T(8,128)(2,1)S(1)}, bf16[64,512]{1,0:T(8,128)(2,1)S(1)}, u32[]{:S(2)}, u32[]{:S(2)}) collective-permute-start(bf16[64,512]{1,0:T(8,128)(2,1)S(1)} %get-tuple-element.36), channel_id=1, source_target_pairs={{3,0},{0,1},{1,2},{2,3},{7,4},{4,5},{5,6},{6,7},{11,8},{8,9},{9,10... | collective-permute-start | bytes 196616 | tf_op jit(solution)/shard_map/ppermute | solution.py:51
  112.1 6.4 %collective-permute-start.26 = (bf16[64,512]{1,0:T(8,128)(2,1)S(1)}, bf16[64,512]{1,0:T(8,128)(2,1)S(1)}, u32[]{:S(2)}, u32[]{:S(2)}) collective-permute-start(bf16[64,512]{1,0:T(8,128)(2,1)S(1)} %get-tuple-element.37), channel_id=1, source_target_pairs={{2,0},{3,1},{0,2},{1,3},{6,4},{7,5},{4,6},{5,7},{10,8},{11,9},{8,1... | collective-permute-start | bytes 196616 | tf_op jit(solution)/shard_map/ppermute | solution.py:51
  115.1 4.3 %collective-permute-start.27 = (bf16[64,512]{1,0:T(8,128)(2,1)S(1)}, bf16[64,512]{1,0:T(8,128)(2,1)S(1)}, u32[]{:S(2)}, u32[]{:S(2)}) collective-permute-start(bf16[64,512]{1,0:T(8,128)(2,1)S(1)} %get-tuple-element.38), channel_id=1, source_target_pairs={{1,0},{2,1},{3,2},{0,3},{5,4},{6,5},{7,6},{4,7},{9,8},{10,9},{11,1... | collective-permute-start | bytes 196616 | tf_op jit(solution)/shard_map/ppermute | solution.py:51

commit v3 on v2

--- a/solution.py
+++ b/solution.py
@@ -14,6 +14,7 @@
 REQS = 8
 NEW = 32
 GROUP = QH // KV_HEADS
+AHEAD = 4
 SIDE = 4
 ROWS = 16
 BLOCK = GROUP * ROWS
@@ -76,28 +77,42 @@
 
 
 def weigh(s):
-    most = jnp.max(s, axis=1, keepdims=True)
-    w = jnp.exp2((s - most) * SCALE)
-    exact = most * SCALE
-    top = exact.astype(BF16).astype(F32)
-    return top, jnp.exp2(exact - top), jnp.sum(w, axis=1, keepdims=True), w.astype(BF16)
+    top = jnp.max(s, axis=1, keepdims=True)
+    w = jnp.exp2((s - top) * SCALE)
+    return top, jnp.sum(w, axis=1, keepdims=True), w.astype(BF16)
+
+
+def in_parts(value, count):
+    parts = []
+    for _ in range(count):
+        part = value.astype(BF16)
+        parts.append(part)
+        value = value - part.astype(F32)
+    return parts
+
+
+def pack_stats(top, total):
+    rest = jnp.zeros((ROWS, HD - 5 * GROUP), BF16)
+    return jnp.concatenate([*in_parts(top, 3), *in_parts(total, 2), rest], axis=1)
+
+
+def unpack_stats(tile):
+    parts = [tile[:, i * GROUP : (i + 1) * GROUP].astype(F32) for i in range(5)]
+    return (parts[0] + parts[1]) + parts[2], parts[3] + parts[4]
 
 
 def put_partial(out, index, top, total, summed):
     lane = lax.broadcasted_iota(jnp.int32, (ROWS, HD), 1)
-    high = total.astype(BF16).astype(F32)
-    low = total - high
-    stats = jnp.zeros((ROWS, HD), F32)
+    tops = totals = jnp.zeros((ROWS, HD), F32)
     for g in range(GROUP):
         rows = slice(g * ROWS, (g + 1) * ROWS)
         out[index, :, g * HD : (g + 1) * HD] = summed[rows].astype(BF16)
-        stats = jnp.where(lane == g, top[rows], stats)
-        stats = jnp.where(lane == GROUP + g, high[rows], stats)
-        stats = jnp.where(lane == 2 * GROUP + g, low[rows], stats)
-    out[index, :, FEATS:] = stats.astype(BF16)
-
-
-def assemble(info, begin, end, own, other, held):
+        tops = jnp.where(lane == g, top[rows], tops)
+        totals = jnp.where(lane == g, total[rows], totals)
+    out[index, :, FEATS:] = pack_stats(tops[:, :GROUP], totals[:, :GROUP])
+
+
+def assemble(info, own, other, held):
     z, x, core = info[0], info[1], info[2]
     for dz in range(SIDE):
         plane = (z + dz) % SIDE
@@ -111,143 +126,185 @@
                         pair = jnp.concatenate([zero[:, cols].astype(F32), one[:, cols].astype(F32)], axis=0)
                         held[head, plane * SIDE + (x + dx) % SIDE, g * ROWS : (g + 1) * ROWS, :] = pair.astype(BF16)
 
-        used = jnp.logical_and(2 * plane + 1 >= begin, 2 * plane < end)
-        if dz == 0:
-            used = True
-
-        @pl.when(jnp.logical_and(used, core == 0))
+        @pl.when(core == 0)
         def _(lay=lay):
             lay(lambda dz, dx: own[dz][dx], lambda dz, dx: other[dx][dz])
 
-        @pl.when(jnp.logical_and(used, core == 1))
+        @pl.when(core == 1)
         def _(lay=lay):
             lay(lambda dz, dx: other[dz][dx], lambda dz, dx: own[dx][dz])
 
 
-def split_heads(cache, held):
+def split_heads(cache, at, out):
     r = lax.broadcasted_iota(jnp.int32, (2 * HD, 2 * HD), 0)
     c = lax.broadcasted_iota(jnp.int32, (2 * HD, 2 * HD), 1)
     pick = (c == jnp.where(r < HD, 2 * r, 2 * (r - HD) + 1)).astype(BF16)
     for i in range(cache.shape[1] // HD):
         rows = slice(i * HD, (i + 1) * HD)
-        both = cache[0, rows].reshape(2 * HD, 2 * HD)
+        both = cache[at, rows].reshape(2 * HD, 2 * HD)
         apart = jnp.dot(pick, both, preferred_element_type=F32).astype(BF16)
-        held[0, rows] = apart[:HD]
-        held[1, rows] = apart[HD:]
-
-
-def attend_kernel(begin, with_new, info, valid, *refs):
-    own, other, cache = refs[:SIDE], refs[SIDE : 2 * SIDE], refs[2 * SIDE]
-    refs = refs[2 * SIDE + 1 :]
-    if with_new:
-        new, sent, mine, new_out, queries, keys = refs
-    else:
-        sent, mine, queries, keys = refs
+        out(0, rows, apart[:HD])
+        out(1, rows, apart[HD:])
+
+
+def ahead_kernel(cache, *refs):
+    out = refs[-1]
+
+    def put(head, rows, value):
+        out[0, head, rows] = value
+
+    split_heads(cache, 0, put)
+
+
+def split_ahead(cache, held, begin, count):
+    per = cache.shape[1]
+    return pl.pallas_call(
+        ahead_kernel,
+        grid=(count,),
+        in_specs=[pl.BlockSpec((1, per, 2, 2 * HD), lambda i: (begin + i, 0, 0, 0))]
+        + ([] if held is None else [pl.BlockSpec(memory_space=pl.ANY)]),
+        out_specs=pl.BlockSpec((1, 2, per, 2 * HD), lambda i: (begin + i, 0, 0, 0)),
+        out_shape=jax.ShapeDtypeStruct((AHEAD, 2, per, 2 * HD), BF16),
+        input_output_aliases={} if held is None else {1: 0},
+        compiler_params=pltpu.CompilerParams(vmem_limit_bytes=54 * MIB),
+        cost_estimate=pl.CostEstimate(flops=0, bytes_accessed=count * 8 * MIB, transcendentals=0),
+        name="split_ahead",
+    )(cache, *([] if held is None else [held]))
+
+
+def attend_kernel(info, valid, *refs):
+    own, other, ahead, cache, new = refs[:SIDE], refs[SIDE : 2 * SIDE], *refs[2 * SIDE : 2 * SIDE + 3]
+    sent, mine, new_out, queries, keys, held, arrived = refs[2 * SIDE + 3 :]
     step = pl.program_id(0)
     last = pl.num_programs(0) - 1
     core = info[2]
+    slot = cache.shape[1]
+    side = step % 2
+
+    def fetch(request):
+        if request < AHEAD:
+            return pltpu.make_async_copy(
+                ahead.at[request], keys.at[request // 2 % 2, request % 2], arrived.at[request]
+            )
+        return pltpu.make_async_copy(cache.at[request], held.at[request - AHEAD], arrived.at[request])
 
     @pl.when(step == 0)
     def _():
-        assemble(info, begin, begin + pl.num_programs(0), own, other, queries)
-
-    request = begin + step
-    count = valid[request]
-    slot = cache.shape[1]
-    where = [(head, out, half) for head, out in ((1 - core, sent), (core, mine)) for half in range(2)]
-
-    def scores(head, _, half):
-        return dot_nt(queries[head, 2 * request + half], keys[head, :, :HD])
-
-    def finish(head, out, half, s):
-        top, factor, total, w = weigh(s)
-        summed = jnp.dot(w, keys[head, :, HD:], preferred_element_type=F32)
-        put_partial(out, half, top, total * factor, summed * factor)
-
-    @pl.when(count >= slot)
-    def _():
-        split_heads(cache, keys)
+        for request in range(REQS):
+            fetch(request).start()
+        assemble(info, own, other, queries)
+
+    for now in range(REQS // 2):
+
+        @pl.when(step == now)
+        def _(now=now):
+            for r in range(2):
+                fetch(2 * now + r).wait()
+
+    @pl.when(2 * step >= AHEAD)
+    def _():
+        for r in range(2):
+
+            def put(head, rows, value, r=r):
+                keys[side, r, head, rows] = value
+
+            split_heads(held, 2 * step - AHEAD + r, put)
+
+    first, second = valid[2 * step], valid[2 * step + 1]
+    where = [
+        (r, head, out, half)
+        for r in range(2)
+        for head, out in ((1 - core, sent), (core, mine))
+        for half in range(2)
+    ]
+
+    def scores(r, head, _, half):
+        return dot_nt(queries[head, 4 * step + 2 * r + half], keys[side, r, head, :, :HD])
+
+    def finish(r, head, out, half, s):
+        top, total, w = weigh(s)
+        summed = jnp.dot(w, keys[side, r, head, :, HD:], preferred_element_type=F32)
+        put_partial(out, 2 * r + half, top, total, summed)
+
+    full = jnp.logical_and(first >= slot, second >= slot)
+
+    @pl.when(full)
+    def _():
         s = scores(*where[0])
         for i, block in enumerate(where):
             later = scores(*where[i + 1]) if i + 1 < len(where) else None
             finish(*block, s)
             s = later
 
-    @pl.when(jnp.logical_and(count > 0, count < slot))
-    def _():
-        split_heads(cache, keys)
-        for block in where:
-            s = scores(*block)
-            position = lax.broadcasted_iota(jnp.int32, s.shape, 1)
-            finish(*block, jnp.where(position < count, s, EMPTY))
-
-    @pl.when(count <= 0)
-    def _():
-        lane = lax.broadcasted_iota(jnp.int32, (ROWS, WIDE), 1)
-        tops = jnp.logical_and(lane >= FEATS, lane < FEATS + GROUP)
-        none = jnp.where(tops, EMPTY, 0.0).astype(BF16)
-        for _, out, half in where:
-            out[half] = none
-
-    if with_new:
-        @pl.when(step == last)
-        def _():
-            z, x = info[0], info[1]
-            s = dot_nt(queries[core, z * SIDE + x], new[0, :, :HD])
-            token = (x % 2) * ROWS + lax.broadcasted_iota(jnp.int32, s.shape, 0) % ROWS
-            key = lax.broadcasted_iota(jnp.int32, s.shape, 1)
-            top, factor, total, w = weigh(jnp.where(key <= token, s, EMPTY))
-            summed = jnp.dot(w, new[0, :, HD:], preferred_element_type=F32)
-            put_partial(new_out, 0, top, total * factor, summed * factor)
-
-
-def attend(info, valid, own, other, cache, new, begin, count):
-    per = cache.shape[1]
-    in_specs = [whole()] * (2 * SIDE) + [
-        pl.BlockSpec((1, per, 2, 2 * HD), lambda i, info, valid: (begin + i, 0, 0, 0))
-    ]
-    out_specs = [pl.BlockSpec((2, ROWS, WIDE), lambda i, info, valid: (i, 0, 0))] * 2
-    out_shape = [jax.ShapeDtypeStruct((2 * count, ROWS, WIDE), BF16)] * 2
-    args = [*own, *other, cache]
-    if new is not None:
-        in_specs.append(whole())
-        out_specs.append(pl.BlockSpec((1, ROWS, WIDE), lambda i, info, valid: (0, 0, 0)))
-        out_shape.append(jax.ShapeDtypeStruct((1, ROWS, WIDE), BF16))
-        args.append(new)
-    return pl.pallas_call(
-        functools.partial(attend_kernel, begin, new is not None),
-        out_shape=out_shape,
+    @pl.when(jnp.logical_not(full))
+    def _():
+        @pl.loop(0, 2)
+        def _(r):
+            count = valid[2 * step + r]
+
+            @pl.when(count > 0)
+            def _():
+                for head, out in ((1 - core, sent), (core, mine)):
+
+                    @pl.loop(0, 2)
+                    def _(half, head=head, out=out):
+                        s = scores(r, head, out, half)
+                        position = lax.broadcasted_iota(jnp.int32, s.shape, 1)
+                        finish(r, head, out, half, jnp.where(position < count, s, EMPTY))
+
+            @pl.when(count <= 0)
+            def _():
+                none = pack_stats(jnp.full((ROWS, GROUP), EMPTY, F32), jnp.zeros((ROWS, GROUP), F32))
+                for out in (sent, mine):
+                    for half in range(2):
+                        out[2 * r + half, :, :FEATS] = jnp.zeros((ROWS, FEATS), BF16)
+                        out[2 * r + half, :, FEATS:] = none
+
+    @pl.when(step == last)
+    def _():
+        z, x = info[0], info[1]
+        s = dot_nt(queries[core, z * SIDE + x], new[0, :, :HD])
+        token = (x % 2) * ROWS + lax.broadcasted_iota(jnp.int32, s.shape, 0) % ROWS
+        key = lax.broadcasted_iota(jnp.int32, s.shape, 1)
+        top, total, w = weigh(jnp.where(key <= token, s, EMPTY))
+        summed = jnp.dot(w, new[0, :, HD:], preferred_element_type=F32)
+        put_partial(new_out, 0, top, total, summed)
+
+
+def attend(info, valid, own, other, ahead, cache, new):
+    reqs, per = cache.shape[:2]
+    blocks = jax.ShapeDtypeStruct((2 * reqs, ROWS, WIDE), BF16)
+    return pl.pallas_call(
+        attend_kernel,
+        out_shape=[blocks, blocks, jax.ShapeDtypeStruct((1, ROWS, WIDE), BF16)],
         grid_spec=pltpu.PrefetchScalarGridSpec(
             num_scalar_prefetch=2,
-            grid=(count,),
-            in_specs=in_specs,
-            out_specs=out_specs,
+            grid=(reqs // 2,),
+            in_specs=[whole()] * (2 * SIDE) + [pl.BlockSpec(memory_space=pl.ANY)] * 2 + [whole()],
+            out_specs=[pl.BlockSpec((4, ROWS, WIDE), lambda i, info, valid: (i, 0, 0))] * 2
+            + [pl.BlockSpec((1, ROWS, WIDE), lambda i, info, valid: (0, 0, 0))],
             scratch_shapes=[
                 pltpu.VMEM((2, SIDE * SIDE, BLOCK, HD), BF16),
-                pltpu.VMEM((2, per, 2 * HD), BF16),
+                pltpu.VMEM((2, 2, 2, per, 2 * HD), BF16),
+                pltpu.VMEM((REQS - AHEAD, *cache.shape[1:]), BF16),
+                pltpu.SemaphoreType.DMA((REQS,)),
             ],
         ),
-        compiler_params=pltpu.CompilerParams(vmem_limit_bytes=50 * MIB),
+        compiler_params=pltpu.CompilerParams(vmem_limit_bytes=46 * MIB),
         cost_estimate=pl.CostEstimate(
-            flops=16 * count * BLOCK * per * HD, bytes_accessed=count * per * 4 * HD * 2, transcendentals=0
+            flops=16 * reqs * BLOCK * per * HD, bytes_accessed=reqs * per * 4 * HD * 2, transcendentals=0
         ),
-        name="attend_new" if new is not None else "attend",
-    )(info, valid, *args)
+        name="attend",
+    )(info, valid, *own, *other, ahead, cache, new)
 
 
 def factors_of(parts):
-    stats = [ref[index, :, FEATS:].astype(F32) for ref, index, _ in parts]
-    tops = [
-        p[:, :GROUP] if counts is None else jnp.where(counts, p[:, :GROUP], EMPTY)
-        for p, (_, _, counts) in zip(stats, parts)
-    ]
-    totals = [p[:, GROUP : 2 * GROUP] + p[:, 2 * GROUP : 3 * GROUP] for p in stats]
+    stats = [unpack_stats(ref[index, :, FEATS:]) for ref, index, _ in parts]
+    tops = [top if counts is None else jnp.where(counts, top, EMPTY) for (top, _), (_, _, counts) in zip(stats, parts)]
     best = functools.reduce(jnp.maximum, tops)
-    factors = [
-        jnp.exp2(t - best) if counts is None else jnp.where(counts, jnp.exp2(t - best), 0.0)
-        for t, (_, _, counts) in zip(tops, parts)
-    ]
-    return best, sum(f * t for f, t in zip(factors, totals)), factors
+    factors = [jnp.exp2((top - best) * SCALE) for top in tops]
+    factors = [f if counts is None else jnp.where(counts, f, 0.0) for f, (_, _, counts) in zip(factors, parts)]
+    return best, sum(f * total for f, (_, total) in zip(factors, stats)), factors
 
 
 def summed_of(parts, factors, g):
@@ -258,23 +315,13 @@
 def merge_into(jobs):
     ready = [factors_of(parts) for _, _, parts in jobs]
     for (out, index, _), (best, total, _) in zip(jobs, ready):
-        high = total.astype(BF16)
-        low = (total - high.astype(F32)).astype(BF16)
-        rest = jnp.zeros((ROWS, HD - 3 * GROUP), BF16)
-        out[index, :, FEATS:] = jnp.concatenate([best.astype(BF16), high, low, rest], axis=1)
+        out[index, :, FEATS:] = pack_stats(best, total)
     for (out, index, parts), (_, _, factors) in zip(jobs, ready):
         for g in range(GROUP):
             out[index, :, g * HD : (g + 1) * HD] = summed_of(parts, factors, g).astype(BF16)
 
 
-def twin_kernel(info, *refs):
-    mine_parts, got_parts, new = refs[:2], refs[2:4], refs[4]
-    outs, (mine, got) = refs[5 : 5 + SIDE], refs[5 + SIDE :]
-    for held, parts in ((mine, mine_parts), (got, got_parts)):
-        first = 0
-        for part in parts:
-            held[first : first + part.shape[0]] = part[...]
-            first += part.shape[0]
+def twin_kernel(info, mine, got, new, *outs):
     z, x, core = info[0], info[1], info[2]
     jobs = []
     for d in range(SIDE):
@@ -291,12 +338,11 @@
     return pl.pallas_call(
         twin_kernel,
         out_shape=[jax.ShapeDtypeStruct((SIDE, ROWS, WIDE), BF16)] * SIDE,
-        in_specs=[pl.BlockSpec(memory_space=pltpu.SMEM)] + [whole()] * 5,
+        in_specs=[pl.BlockSpec(memory_space=pltpu.SMEM)] + [whole()] * 3,
         out_specs=[whole()] * SIDE,
-        scratch_shapes=[pltpu.VMEM((SIDE * SIDE, ROWS, WIDE), BF16)] * 2,
         compiler_params=pltpu.CompilerParams(vmem_limit_bytes=24 * MIB),
         name="merge_twins",
-    )(info, *mine, *got, new)
+    )(info, mine, got, new)
 
 
 def four_kernel(*refs):
@@ -413,16 +459,16 @@
 
     request = 2 * z + x // 2
     new = lax.dynamic_slice(new_kv, (request, 0, core, 0), (1, NEW, 1, 2 * HD)).reshape(1, NEW, 2 * HD)
+    ahead = split_ahead(cache, None, 0, 1)
     line = stack([queries] + [from_first(queries, s) for s in (1, 2, 3)])
-    info, valid, new, line = lax.optimization_barrier((info, valid, new, line))
+    info, valid, new, line, ahead = lax.optimization_barrier((info, valid, new, line, ahead))
     own = [line] + [from_second(line, s) for s in (1, 2, 3)]
+    ahead = split_ahead(cache, ahead, 1, AHEAD - 1)
+    *own, ahead = lax.optimization_barrier((*own, ahead))
     other = [from_twin(part) for part in own]
 
-    early = REQS - 2
-    sent0, mine0 = attend(info, valid, own, other, cache, None, 0, early)
-    got0 = from_twin(sent0)
-    sent1, mine1, from_new = attend(info, valid, own, other, cache, new, early, REQS - early)
-    parts = merge_twins(info, [mine0, mine1], [got0, from_twin(sent1)], from_new)
+    sent, mine, from_new = attend(info, valid, own, other, ahead, cache, new)
+    parts = merge_twins(info, mine, from_twin(sent), from_new)
     zs = merge_four([parts[0]] + [from_second(parts[SIDE - s], s) for s in (1, 2, 3)])
     rows = merge_final([zs] + [from_first(zs, s) for s in (1, 2, 3)])
 

time: 120 us -> 115 us (0.958)
  waiting for transfers between devices: 40.6 us -> 33.9 us
  Pallas kernels: 45.6 us -> 47.8 us
    ppermute x9, waiting for transfers between devices: 21 us -> 15.4 us  [from_second(): return lax.ppermute(value, 'ctx', pairs)]
    ppermute x6, waiting for transfers between devices: 12.4 us -> 9.79 us  [from_first(): return lax.ppermute(value, 'ctx', pairs)]
    ppermute x6, starting transfers between devices: 8.44 us -> 10.7 us  [from_first(): return lax.ppermute(value, 'ctx', pairs)]
    pallas_call x2 -> x3, Pallas kernels: 38.5 us -> 40.6 us  [the longest x1 28.5 us: attend(): pl.pallas_call(attend_kernel, out_shape=[blocks, blocks, jax.ShapeDtypeSt...]
    ppermute x9, starting transfers between devices: 15.4 us -> 13.7 us  [from_second(): return lax.ppermute(value, 'ctx', pairs)]
    ppermute x10 -> x9, waiting for transfers between devices: 4.22 us -> 5.77 us  [from_twin(): lax.ppermute(value, 'ctx', [(at(z, x, 1 - c), at(z, x, c)) for z, x, c in...]
  transfers between devices with their start and end apart: 28 -> 27, of which waited for: 18 -> 20; matrix products, arithmetic and copies ran while one was open for 1% -> 0% of each run, Pallas kernels for 9% -> 11%
where the time goes in v3:
time: 115 us; the launch traced here: 114 us
  Pallas kernels  47.8 us (42%)
  waiting for transfers between devices  33.9 us (29%)
  starting transfers between devices  31.7 us (28%)
    pallas_call x1, Pallas kernels, attend(): pl.pallas_call(attend_kernel, out_shape=[blocks, blocks, jax.ShapeDtypeSt...  28.5 us
    ppermute x9, waiting for transfers between devices, from_second(): return lax.ppermute(value, 'ctx', pairs)  15.4 us
    ppermute x9, starting transfers between devices, from_second(): return lax.ppermute(value, 'ctx', pairs)  13.7 us
    pallas_call x2, Pallas kernels, split_ahead(): pl.pallas_call(ahead_kernel, grid=(count,), in_specs=[pl.BlockSpec((1, pe...  12 us
    ppermute x6, starting transfers between devices, from_first(): return lax.ppermute(value, 'ctx', pairs)  10.7 us
    ppermute x6, waiting for transfers between devices, from_first(): return lax.ppermute(value, 'ctx', pairs)  9.79 us
    ppermute x3, starting transfers between devices, from_plane(): lax.ppermute(value, 'kvh', [((s + step) % SIDE, s) for s in range(SIDE)])  5.89 us
    ppermute x9, waiting for transfers between devices, from_twin(): lax.ppermute(value, 'ctx', [(at(z, x, 1 - c), at(z, x, c)) for z, x, c in...  5.77 us
  transfers between devices with their start and end apart: 27, of which 20 were waited for; matrix products, arithmetic and copies ran while one was open for 0% of the time, Pallas kernels for 11%

profile of v3, /device:TPU:0, one launch (start us, length us, event | category | flops | bytes accessed | tf_op | source)
XLA Modules:
  0.0 114.4 jit_solution(8322526941089168888)
XLA Ops:
  0.0 2.8 %collective-permute-start = (bf16[8,4096]{1,0:T(8,128)(2,1)}, bf16[8,4096]{1,0:T(8,128)(2,1)S(1)}, u32[]{:S(2)}, u32[]{:S(2)}) collective-permute-start(bf16[8,4096]{1,0:T(8,128)(2,1)} %refs_0_.1), channel_id=1, source_target_pairs={{8,0},{36,4},{16,8},{44,12},{24,16},{52,20},{0,24},{60,28},{40,32}... | collective-permute-start | bytes 196616 | tf_op jit(solution)/shard_map/ppermute | solution.py:39
  3.6 0.9 collective-permute-start.2
  4.6 4.0 %split_ahead.2.refs_0_ = bf16[4,2,2048,256]{3,2,1,0:T(8,128)(2,1)} custom-call(bf16[8,2048,2,256]{3,2,1,0:T(2,128)(2,1)} %refs_9_.1), custom_call_target="tpu_custom_call" | custom-call | bytes 8388608 | tf_op jit(solution)/shard_map/split_ahead/pallas_call | solution.py:161
  9.6 4.1 %collective-permute-start.3 = (bf16[4,8,4096]{2,1,0:T(8,128)(2,1)S(1)}, bf16[4,8,4096]{2,1,0:T(8,128)(2,1)S(1)}, u32[]{:S(2)}, u32[]{:S(2)}) collective-permute-start(bf16[4,8,4096]{2,1,0:T(8,128)(2,1)S(1)} %stack.21.refs_0_), channel_id=1, source_target_pairs={{32,0},{12,4},{40,8},{20,12},{48,16},{28,20},{56,24},{4,28},{64,32... | collective-permute-start | bytes 786440 | tf_op jit(solution)/shard_map/ppermute | solution.py:44
  13.7 1.3 %collective-permute-start.5 = (bf16[4,8,4096]{2,1,0:T(8,128)(2,1)S(1)}, bf16[4,8,4096]{2,1,0:T(8,128)(2,1)S(1)}, u32[]{:S(2)}, u32[]{:S(2)}) collective-permute-start(bf16[4,8,4096]{2,1,0:T(8,128)(2,1)S(1)} %stack.21.refs_0_), channel_id=1, source_target_pairs={{96,0},{28,4},{104,8},{4,12},{112,16},{12,20},{120,24},{20,28},{0,... | collective-permute-start | bytes 786440 | tf_op jit(solution)/shard_map/ppermute | solution.py:44
  14.9 8.1 %split_ahead.3.refs_8_ = bf16[4,2,2048,256]{3,2,1,0:T(8,128)(2,1)} custom-call(bf16[8,2048,2,256]{3,2,1,0:T(2,128)(2,1)} %refs_9_.1, bf16[4,2,2048,256]{3,2,1,0:T(8,128)(2,1)} %split_ahead.2.refs_0_), custom_call_target="tpu_custom_call", output_to_operand_aliasing={{}: (1, {})} | custom-call | bytes 25165824 | tf_op jit(solution)/shard_map/split_ahead/pallas_call | solution.py:161
  23.0 1.1 collective-permute-done.5.refs_3_
  26.7 28.5 %attend.1 = (bf16[16,16,2176]{2,1,0:T(8,128)(2,1)S(1)}, bf16[16,16,2176]{2,1,0:T(8,128)(2,1)S(1)}, bf16[1,16,2176]{2,1,0:T(8,128)(2,1)S(1)}) custom-call(s32[4]{0:T(128)S(1)} %pad_add_fusion.info, s32[8]{0:T(128)S(1)} %subtract_clamp_fusion.valid, bf16[4,8,4096]{2,1,0:T(8,128)(2,1)S(1)} %stack.21.refs_0_, ...), custom_call_target="tpu_custom_call" | custom-call | flops 8589934592 | bytes 16777216 | tf_op jit(solution)/shard_map/attend/pallas_call | solution.py:277
  55.7 2.6 %collective-permute-done.10.got = bf16[16,16,2176]{2,1,0:T(8,128)(2,1)S(1)} collective-permute-done((bf16[16,16,2176]{2,1,0:T(8,128)(2,1)S(1)}, bf16[16,16,2176]{2,1,0:T(8,128)(2,1)S(1)}, u32[]{:S(2)}, u32[]{:S(2)}) %collective-permute-start.10) | collective-permute-done | bytes 1114144 | tf_op jit(solution)/shard_map/ppermute | solution.py:48
  58.3 2.9 %merge_twins.1 = (bf16[4,16,2176]{2,1,0:T(8,128)(2,1)S(1)}, bf16[4,16,2176]{2,1,0:T(8,128)(2,1)S(1)}, bf16[4,16,2176]{2,1,0:T(8,128)(2,1)S(1)}, bf16[4,16,2176]{2,1,0:T(8,128)(2,1)S(1)}) custom-call(s32[4]{0:T(128)S(1)} %pad_add_fusion.info, bf16[16,16,2176]{2,1,0:T(8,128)(2,1)S(1)} %get-tuple-element.36.mine, ...), custom_call_target="tpu_custom_call" | custom-call | tf_op jit(solution)/shard_map/merge_twins/pallas_call | solution.py:338
  61.3 3.3 %collective-permute-start.12 = (bf16[4,16,2176]{2,1,0:T(8,128)(2,1)S(1)}, bf16[4,16,2176]{2,1,0:T(8,128)(2,1)S(1)}, u32[]{:S(2)}, u32[]{:S(2)}) collective-permute-start(bf16[4,16,2176]{2,1,0:T(8,128)(2,1)S(1)} %get-tuple-element.41), channel_id=1, source_target_pairs={{64,0},{20,4},{72,8},{28,12},{80,16},{4,20},{88,24},{12,28},{96,32... | collective-permute-start | bytes 835592 | tf_op jit(solution)/shard_map/ppermute | solution.py:44
  64.6 1.0 collective-permute-start.13
  65.6 2.2 %collective-permute-done.11.refs_1_ = bf16[4,16,2176]{2,1,0:T(8,128)(2,1)S(1)} collective-permute-done((bf16[4,16,2176]{2,1,0:T(8,128)(2,1)S(1)}, bf16[4,16,2176]{2,1,0:T(8,128)(2,1)S(1)}, u32[]{:S(2)}, u32[]{:S(2)}) %collective-permute-start.11) | collective-permute-done | bytes 278560 | tf_op jit(solution)/shard_map/ppermute | solution.py:44
  67.8 1.6 %collective-permute-done.12.refs_2_ = bf16[4,16,2176]{2,1,0:T(8,128)(2,1)S(1)} collective-permute-done((bf16[4,16,2176]{2,1,0:T(8,128)(2,1)S(1)}, bf16[4,16,2176]{2,1,0:T(8,128)(2,1)S(1)}, u32[]{:S(2)}, u32[]{:S(2)}) %collective-permute-start.12) | collective-permute-done | bytes 278560 | tf_op jit(solution)/shard_map/ppermute | solution.py:44
  69.4 3.0 %collective-permute-done.13.refs_3_ = bf16[4,16,2176]{2,1,0:T(8,128)(2,1)S(1)} collective-permute-done((bf16[4,16,2176]{2,1,0:T(8,128)(2,1)S(1)}, bf16[4,16,2176]{2,1,0:T(8,128)(2,1)S(1)}, u32[]{:S(2)}, u32[]{:S(2)}) %collective-permute-start.13) | collective-permute-done | bytes 278560 | tf_op jit(solution)/shard_map/ppermute | solution.py:44
  72.4 0.8 merge_four.1.refs_0_
  73.3 4.0 %collective-permute-start.14 = (bf16[4,16,2176]{2,1,0:T(8,128)(2,1)S(1)}, bf16[4,16,2176]{2,1,0:T(8,128)(2,1)S(1)}, u32[]{:S(2)}, u32[]{:S(2)}) collective-permute-start(bf16[4,16,2176]{2,1,0:T(8,128)(2,1)S(1)} %merge_four.1.refs_0_), channel_id=1, source_target_pairs={{8,0},{36,4},{16,8},{44,12},{24,16},{52,20},{0,24},{60,28},{40,32}... | collective-permute-start | bytes 835592 | tf_op jit(solution)/shard_map/ppermute | solution.py:39
  78.1 1.3 %collective-permute-start.16 = (bf16[4,16,2176]{2,1,0:T(8,128)(2,1)S(1)}, bf16[4,16,2176]{2,1,0:T(8,128)(2,1)S(1)}, u32[]{:S(2)}, u32[]{:S(2)}) collective-permute-start(bf16[4,16,2176]{2,1,0:T(8,128)(2,1)S(1)} %merge_four.1.refs_0_), channel_id=1, source_target_pairs={{24,0},{100,4},{0,8},{108,12},{8,16},{116,20},{16,24},{124,28},{56... | collective-permute-start | bytes 835592 | tf_op jit(solution)/shard_map/ppermute | solution.py:39
  79.4 4.9 %collective-permute-done.14.refs_1_ = bf16[4,16,2176]{2,1,0:T(8,128)(2,1)S(1)} collective-permute-done((bf16[4,16,2176]{2,1,0:T(8,128)(2,1)S(1)}, bf16[4,16,2176]{2,1,0:T(8,128)(2,1)S(1)}, u32[]{:S(2)}, u32[]{:S(2)}) %collective-permute-start.14) | collective-permute-done | bytes 278560 | tf_op jit(solution)/shard_map/ppermute | solution.py:39
  84.4 1.1 collective-permute-done.15.refs_2_
  85.5 2.9 %collective-permute-done.16.refs_3_ = bf16[4,16,2176]{2,1,0:T(8,128)(2,1)S(1)} collective-permute-done((bf16[4,16,2176]{2,1,0:T(8,128)(2,1)S(1)}, bf16[4,16,2176]{2,1,0:T(8,128)(2,1)S(1)}, u32[]{:S(2)}, u32[]{:S(2)}) %collective-permute-start.16) | collective-permute-done | bytes 278560 | tf_op jit(solution)/shard_map/ppermute | solution.py:39
  88.3 0.9 merge_final.1.refs_0_
  89.6 3.5 %collective-permute-start.18 = (bf16[4,16,2048]{2,1,0:T(8,128)(2,1)S(1)}, bf16[4,16,2048]{2,1,0:T(8,128)(2,1)S(1)}, u32[]{:S(2)}, u32[]{:S(2)}) collective-permute-start(bf16[4,16,2048]{2,1,0:T(8,128)(2,1)S(1)} %merge_final.1.refs_0_), channel_id=1, source_target_pairs={{64,0},{20,4},{72,8},{28,12},{80,16},{4,20},{88,24},{12,28},{96,32... | collective-permute-start | bytes 786440 | tf_op jit(solution)/shard_map/ppermute | solution.py:44
  93.2 2.5 %collective-permute-done.17.refs_1_ = bf16[4,16,2048]{2,1,0:T(8,128)(2,1)S(1)} collective-permute-done((bf16[4,16,2048]{2,1,0:T(8,128)(2,1)S(1)}, bf16[4,16,2048]{2,1,0:T(8,128)(2,1)S(1)}, u32[]{:S(2)}, u32[]{:S(2)}) %collective-permute-start.17) | collective-permute-done | bytes 262176 | tf_op jit(solution)/shard_map/ppermute | solution.py:44
  95.7 1.9 %collective-permute-done.18.refs_2_ = bf16[4,16,2048]{2,1,0:T(8,128)(2,1)S(1)} collective-permute-done((bf16[4,16,2048]{2,1,0:T(8,128)(2,1)S(1)}, bf16[4,16,2048]{2,1,0:T(8,128)(2,1)S(1)}, u32[]{:S(2)}, u32[]{:S(2)}) %collective-permute-start.18) | collective-permute-done | bytes 262176 | tf_op jit(solution)/shard_map/ppermute | solution.py:44
  97.5 3.2 %collective-permute-done.19.refs_3_ = bf16[4,16,2048]{2,1,0:T(8,128)(2,1)S(1)} collective-permute-done((bf16[4,16,2048]{2,1,0:T(8,128)(2,1)S(1)}, bf16[4,16,2048]{2,1,0:T(8,128)(2,1)S(1)}, u32[]{:S(2)}, u32[]{:S(2)}) %collective-permute-start.19) | collective-permute-done | bytes 262176 | tf_op jit(solution)/shard_map/ppermute | solution.py:44
  100.8 1.5 %collective-permute-done.23.refs_7_ = bf16[4,16,2048]{2,1,0:T(8,128)(2,1)S(1)} collective-permute-done((bf16[4,16,2048]{2,1,0:T(8,128)(2,1)S(1)}, bf16[4,16,2048]{2,1,0:T(8,128)(2,1)S(1)}, u32[]{:S(2)}, u32[]{:S(2)}) %collective-permute-start.23) | collective-permute-done | bytes 262176 | tf_op jit(solution)/shard_map/ppermute | solution.py:48
  102.3 2.6 %project.1 = (f32[64,512]{1,0:T(8,128)S(1)}, bf16[64,512]{1,0:T(8,128)(2,1)S(1)}, bf16[64,512]{1,0:T(8,128)(2,1)S(1)}, bf16[64,512]{1,0:T(8,128)(2,1)S(1)}) custom-call(s32[4]{0:T(128)S(1)} %pad_add_fusion.info, bf16[4,16,2048]{2,1,0:T(8,128)(2,1)S(1)} %merge_final.1.refs_0_, bf16[4,16,2048]{2,1,0:T(8,128)(2,1)S(1)} %collective-permute-done.17.refs_1_, ...), custom_call_target="tpu_custom_call" | custom-call | tf_op jit(solution)/shard_map/project/pallas_call | solution.py:435
  104.9 1.6 %collective-permute-start.24 = (bf16[64,512]{1,0:T(8,128)(2,1)S(1)}, bf16[64,512]{1,0:T(8,128)(2,1)S(1)}, u32[]{:S(2)}, u32[]{:S(2)}) collective-permute-start(bf16[64,512]{1,0:T(8,128)(2,1)S(1)} %get-tuple-element.44), channel_id=1, source_target_pairs={{3,0},{0,1},{1,2},{2,3},{7,4},{4,5},{5,6},{6,7},{11,8},{8,9},{9,10... | collective-permute-start | bytes 196616 | tf_op jit(solution)/shard_map/ppermute | solution.py:52
  106.5 2.9 %collective-permute-start.25 = (bf16[64,512]{1,0:T(8,128)(2,1)S(1)}, bf16[64,512]{1,0:T(8,128)(2,1)S(1)}, u32[]{:S(2)}, u32[]{:S(2)}) collective-permute-start(bf16[64,512]{1,0:T(8,128)(2,1)S(1)} %get-tuple-element.45), channel_id=1, source_target_pairs={{2,0},{3,1},{0,2},{1,3},{6,4},{7,5},{4,6},{5,7},{10,8},{11,9},{8,1... | collective-permute-start | bytes 196616 | tf_op jit(solution)/shard_map/ppermute | solution.py:52
  109.4 1.3 %collective-permute-start.26 = (bf16[64,512]{1,0:T(8,128)(2,1)S(1)}, bf16[64,512]{1,0:T(8,128)(2,1)S(1)}, u32[]{:S(2)}, u32[]{:S(2)}) collective-permute-start(bf16[64,512]{1,0:T(8,128)(2,1)S(1)} %get-tuple-element.46), channel_id=1, source_target_pairs={{1,0},{2,1},{3,2},{0,3},{5,4},{6,5},{7,6},{4,7},{9,8},{10,9},{11,1... | collective-permute-start | bytes 196616 | tf_op jit(solution)/shard_map/ppermute | solution.py:52
  110.8 2.2 %collective-permute-done.25 = bf16[64,512]{1,0:T(8,128)(2,1)S(1)} collective-permute-done((bf16[64,512]{1,0:T(8,128)(2,1)S(1)}, bf16[64,512]{1,0:T(8,128)(2,1)S(1)}, u32[]{:S(2)}, u32[]{:S(2)}) %collective-permute-start.25) | collective-permute-done | bytes 65568 | tf_op jit(solution)/shard_map/ppermute | solution.py:52
  (43 shorter events, 7.6 us)
Async XLA Ops:
  0.0 4.5 %copy-start = (bf16[8,32,2,256]{3,2,1,0:T(2,128)(2,1)S(1)}, bf16[8,32,2,256]{3,2,1,0:T(2,128)(2,1)}, u32[]{:S(2)}) copy-start(bf16[8,32,2,256]{3,2,1,0:T(2,128)(2,1)} %param.7) | copy-start | bytes 786436
  0.0 8.7 %collective-permute-start = (bf16[8,4096]{1,0:T(8,128)(2,1)}, bf16[8,4096]{1,0:T(8,128)(2,1)S(1)}, u32[]{:S(2)}, u32[]{:S(2)}) collective-permute-start(bf16[8,4096]{1,0:T(8,128)(2,1)} %refs_0_.1), channel_id=1, source_target_pairs={{8,0},{36,4},{16,8},{44,12},{24,16},{52,20},{0,24},{60,28},{40,32}... | collective-permute-start | bytes 196616 | tf_op jit(solution)/shard_map/ppermute | solution.py:39
  2.8 6.0 %collective-permute-start.1 = (bf16[8,4096]{1,0:T(8,128)(2,1)}, bf16[8,4096]{1,0:T(8,128)(2,1)S(1)}, u32[]{:S(2)}, u32[]{:S(2)}) collective-permute-start(bf16[8,4096]{1,0:T(8,128)(2,1)} %refs_0_.1), channel_id=1, source_target_pairs={{16,0},{68,4},{24,8},{76,12},{0,16},{84,20},{8,24},{92,28},{48,32}... | collective-permute-start | bytes 196616 | tf_op jit(solution)/shard_map/ppermute | solution.py:39
  3.6 5.9 %collective-permute-start.2 = (bf16[8,4096]{1,0:T(8,128)(2,1)}, bf16[8,4096]{1,0:T(8,128)(2,1)S(1)}, u32[]{:S(2)}, u32[]{:S(2)}) collective-permute-start(bf16[8,4096]{1,0:T(8,128)(2,1)} %refs_0_.1), channel_id=1, source_target_pairs={{24,0},{100,4},{0,8},{108,12},{8,16},{116,20},{16,24},{124,28},{56... | collective-permute-start | bytes 196616 | tf_op jit(solution)/shard_map/ppermute | solution.py:39
  4.6 4.0 %copy-start.3 = (s32[8]{0:T(128)S(1)}, s32[8]{0:T(128)}, u32[]{:S(2)}) copy-start(s32[8]{0:T(128)} %param.8) | copy-start | bytes 100
  4.6 4.9 %copy-start.2 = (bf16[8,4096]{1,0:T(8,128)(2,1)S(1)}, bf16[8,4096]{1,0:T(8,128)(2,1)}, u32[]{:S(2)}) copy-start(bf16[8,4096]{1,0:T(8,128)(2,1)} %refs_0_.1) | copy-start | bytes 196612
  9.6 13.4 %collective-permute-start.3 = (bf16[4,8,4096]{2,1,0:T(8,128)(2,1)S(1)}, bf16[4,8,4096]{2,1,0:T(8,128)(2,1)S(1)}, u32[]{:S(2)}, u32[]{:S(2)}) collective-permute-start(bf16[4,8,4096]{2,1,0:T(8,128)(2,1)S(1)} %stack.21.refs_0_), channel_id=1, source_target_pairs={{32,0},{12,4},{40,8},{20,12},{48,16},{28,20},{56,24},{4,28},{64,32... | collective-permute-start | bytes 786440 | tf_op jit(solution)/shard_map/ppermute | solution.py:44
  13.7 9.3 %collective-permute-start.4 = (bf16[4,8,4096]{2,1,0:T(8,128)(2,1)S(1)}, bf16[4,8,4096]{2,1,0:T(8,128)(2,1)S(1)}, u32[]{:S(2)}, u32[]{:S(2)}) collective-permute-start(bf16[4,8,4096]{2,1,0:T(8,128)(2,1)S(1)} %stack.21.refs_0_), channel_id=1, source_target_pairs={{64,0},{20,4},{72,8},{28,12},{80,16},{4,20},{88,24},{12,28},{96,32... | collective-permute-start | bytes 786440 | tf_op jit(solution)/shard_map/ppermute | solution.py:44
  13.7 10.4 %collective-permute-start.5 = (bf16[4,8,4096]{2,1,0:T(8,128)(2,1)S(1)}, bf16[4,8,4096]{2,1,0:T(8,128)(2,1)S(1)}, u32[]{:S(2)}, u32[]{:S(2)}) collective-permute-start(bf16[4,8,4096]{2,1,0:T(8,128)(2,1)S(1)} %stack.21.refs_0_), channel_id=1, source_target_pairs={{96,0},{28,4},{104,8},{4,12},{112,16},{12,20},{120,24},{20,28},{0,... | collective-permute-start | bytes 786440 | tf_op jit(solution)/shard_map/ppermute | solution.py:44
  24.1 1.5 %collective-permute-start.6 = (bf16[4,8,4096]{2,1,0:T(8,128)(2,1)S(1)}, bf16[4,8,4096]{2,1,0:T(8,128)(2,1)S(1)}, u32[]{:S(2)}, u32[]{:S(2)}) collective-permute-start(bf16[4,8,4096]{2,1,0:T(8,128)(2,1)S(1)} %stack.21.refs_0_), channel_id=1, source_target_pairs={{4,0},{0,4},{12,8},{8,12},{20,16},{16,20},{28,24},{24,28},{36,32},... | collective-permute-start | bytes 786440 | tf_op jit(solution)/shard_map/ppermute | solution.py:48
  24.1 1.9 %collective-permute-start.7 = (bf16[4,8,4096]{2,1,0:T(8,128)(2,1)S(1)}, bf16[4,8,4096]{2,1,0:T(8,128)(2,1)S(1)}, u32[]{:S(2)}, u32[]{:S(2)}) collective-permute-start(bf16[4,8,4096]{2,1,0:T(8,128)(2,1)S(1)} %collective-permute-done.3.refs_1_), channel_id=1, source_target_pairs={{4,0},{0,4},{12,8},{8,12},{20,16},{16,20},{28,24},{24,28},{36,32},... | collective-permute-start | bytes 786440 | tf_op jit(solution)/shard_map/ppermute | solution.py:48
  24.6 1.8 %collective-permute-start.8 = (bf16[4,8,4096]{2,1,0:T(8,128)(2,1)S(1)}, bf16[4,8,4096]{2,1,0:T(8,128)(2,1)S(1)}, u32[]{:S(2)}, u32[]{:S(2)}) collective-permute-start(bf16[4,8,4096]{2,1,0:T(8,128)(2,1)S(1)} %collective-permute-done.4.refs_2_), channel_id=1, source_target_pairs={{4,0},{0,4},{12,8},{8,12},{20,16},{16,20},{28,24},{24,28},{36,32},... | collective-permute-start | bytes 786440 | tf_op jit(solution)/shard_map/ppermute | solution.py:48
  24.6 2.1 %collective-permute-start.9 = (bf16[4,8,4096]{2,1,0:T(8,128)(2,1)S(1)}, bf16[4,8,4096]{2,1,0:T(8,128)(2,1)S(1)}, u32[]{:S(2)}, u32[]{:S(2)}) collective-permute-start(bf16[4,8,4096]{2,1,0:T(8,128)(2,1)S(1)} %collective-permute-done.5.refs_3_), channel_id=1, source_target_pairs={{4,0},{0,4},{12,8},{8,12},{20,16},{16,20},{28,24},{24,28},{36,32},... | collective-permute-start | bytes 786440 | tf_op jit(solution)/shard_map/ppermute | solution.py:48
  55.3 47.0 %copy-start.1 = (bf16[4096,512]{1,0:T(8,128)(2,1)S(1)}, bf16[4096,512]{1,0:T(8,128)(2,1)}, u32[]{:S(2)}) copy-start(bf16[4096,512]{1,0:T(8,128)(2,1)} %refs_8_.1) | copy-start | bytes 12582916
  55.3 3.1 %collective-permute-start.10 = (bf16[16,16,2176]{2,1,0:T(8,128)(2,1)S(1)}, bf16[16,16,2176]{2,1,0:T(8,128)(2,1)S(1)}, u32[]{:S(2)}, u32[]{:S(2)}) collective-permute-start(bf16[16,16,2176]{2,1,0:T(8,128)(2,1)S(1)} %get-tuple-element.37), channel_id=1, source_target_pairs={{4,0},{0,4},{12,8},{8,12},{20,16},{16,20},{28,24},{24,28},{36,32},... | collective-permute-start | bytes 3342344 | tf_op jit(solution)/shard_map/ppermute | solution.py:48
  61.2 6.6 %collective-permute-start.11 = (bf16[4,16,2176]{2,1,0:T(8,128)(2,1)S(1)}, bf16[4,16,2176]{2,1,0:T(8,128)(2,1)S(1)}, u32[]{:S(2)}, u32[]{:S(2)}) collective-permute-start(bf16[4,16,2176]{2,1,0:T(8,128)(2,1)S(1)} %get-tuple-element.40), channel_id=1, source_target_pairs={{32,0},{12,4},{40,8},{20,12},{48,16},{28,20},{56,24},{4,28},{64,32... | collective-permute-start | bytes 835592 | tf_op jit(solution)/shard_map/ppermute | solution.py:44
  61.3 8.1 %collective-permute-start.12 = (bf16[4,16,2176]{2,1,0:T(8,128)(2,1)S(1)}, bf16[4,16,2176]{2,1,0:T(8,128)(2,1)S(1)}, u32[]{:S(2)}, u32[]{:S(2)}) collective-permute-start(bf16[4,16,2176]{2,1,0:T(8,128)(2,1)S(1)} %get-tuple-element.41), channel_id=1, source_target_pairs={{64,0},{20,4},{72,8},{28,12},{80,16},{4,20},{88,24},{12,28},{96,32... | collective-permute-start | bytes 835592 | tf_op jit(solution)/shard_map/ppermute | solution.py:44
  64.6 7.8 %collective-permute-start.13 = (bf16[4,16,2176]{2,1,0:T(8,128)(2,1)S(1)}, bf16[4,16,2176]{2,1,0:T(8,128)(2,1)S(1)}, u32[]{:S(2)}, u32[]{:S(2)}) collective-permute-start(bf16[4,16,2176]{2,1,0:T(8,128)(2,1)S(1)} %get-tuple-element.42), channel_id=1, source_target_pairs={{96,0},{28,4},{104,8},{4,12},{112,16},{12,20},{120,24},{20,28},{0,... | collective-permute-start | bytes 835592 | tf_op jit(solution)/shard_map/ppermute | solution.py:44
  73.3 11.1 %collective-permute-start.14 = (bf16[4,16,2176]{2,1,0:T(8,128)(2,1)S(1)}, bf16[4,16,2176]{2,1,0:T(8,128)(2,1)S(1)}, u32[]{:S(2)}, u32[]{:S(2)}) collective-permute-start(bf16[4,16,2176]{2,1,0:T(8,128)(2,1)S(1)} %merge_four.1.refs_0_), channel_id=1, source_target_pairs={{8,0},{36,4},{16,8},{44,12},{24,16},{52,20},{0,24},{60,28},{40,32}... | collective-permute-start | bytes 835592 | tf_op jit(solution)/shard_map/ppermute | solution.py:39
  77.3 8.2 %collective-permute-start.15 = (bf16[4,16,2176]{2,1,0:T(8,128)(2,1)S(1)}, bf16[4,16,2176]{2,1,0:T(8,128)(2,1)S(1)}, u32[]{:S(2)}, u32[]{:S(2)}) collective-permute-start(bf16[4,16,2176]{2,1,0:T(8,128)(2,1)S(1)} %merge_four.1.refs_0_), channel_id=1, source_target_pairs={{16,0},{68,4},{24,8},{76,12},{0,16},{84,20},{8,24},{92,28},{48,32}... | collective-permute-start | bytes 835592 | tf_op jit(solution)/shard_map/ppermute | solution.py:39
  78.1 10.3 %collective-permute-start.16 = (bf16[4,16,2176]{2,1,0:T(8,128)(2,1)S(1)}, bf16[4,16,2176]{2,1,0:T(8,128)(2,1)S(1)}, u32[]{:S(2)}, u32[]{:S(2)}) collective-permute-start(bf16[4,16,2176]{2,1,0:T(8,128)(2,1)S(1)} %merge_four.1.refs_0_), channel_id=1, source_target_pairs={{24,0},{100,4},{0,8},{108,12},{8,16},{116,20},{16,24},{124,28},{56... | collective-permute-start | bytes 835592 | tf_op jit(solution)/shard_map/ppermute | solution.py:39
  89.2 6.4 %collective-permute-start.17 = (bf16[4,16,2048]{2,1,0:T(8,128)(2,1)S(1)}, bf16[4,16,2048]{2,1,0:T(8,128)(2,1)S(1)}, u32[]{:S(2)}, u32[]{:S(2)}) collective-permute-start(bf16[4,16,2048]{2,1,0:T(8,128)(2,1)S(1)} %merge_final.1.refs_0_), channel_id=1, source_target_pairs={{32,0},{12,4},{40,8},{20,12},{48,16},{28,20},{56,24},{4,28},{64,32... | collective-permute-start | bytes 786440 | tf_op jit(solution)/shard_map/ppermute | solution.py:44
  89.6 7.9 %collective-permute-start.18 = (bf16[4,16,2048]{2,1,0:T(8,128)(2,1)S(1)}, bf16[4,16,2048]{2,1,0:T(8,128)(2,1)S(1)}, u32[]{:S(2)}, u32[]{:S(2)}) collective-permute-start(bf16[4,16,2048]{2,1,0:T(8,128)(2,1)S(1)} %merge_final.1.refs_0_), channel_id=1, source_target_pairs={{64,0},{20,4},{72,8},{28,12},{80,16},{4,20},{88,24},{12,28},{96,32... | collective-permute-start | bytes 786440 | tf_op jit(solution)/shard_map/ppermute | solution.py:44
  93.2 7.6 %collective-permute-start.19 = (bf16[4,16,2048]{2,1,0:T(8,128)(2,1)S(1)}, bf16[4,16,2048]{2,1,0:T(8,128)(2,1)S(1)}, u32[]{:S(2)}, u32[]{:S(2)}) collective-permute-start(bf16[4,16,2048]{2,1,0:T(8,128)(2,1)S(1)} %merge_final.1.refs_0_), channel_id=1, source_target_pairs={{96,0},{28,4},{104,8},{4,12},{112,16},{12,20},{120,24},{20,28},{0,... | collective-permute-start | bytes 786440 | tf_op jit(solution)/shard_map/ppermute | solution.py:44
  93.2 7.6 %collective-permute-start.20 = (bf16[4,16,2048]{2,1,0:T(8,128)(2,1)S(1)}, bf16[4,16,2048]{2,1,0:T(8,128)(2,1)S(1)}, u32[]{:S(2)}, u32[]{:S(2)}) collective-permute-start(bf16[4,16,2048]{2,1,0:T(8,128)(2,1)S(1)} %merge_final.1.refs_0_), channel_id=1, source_target_pairs={{4,0},{0,4},{12,8},{8,12},{20,16},{16,20},{28,24},{24,28},{36,32},... | collective-permute-start | bytes 786440 | tf_op jit(solution)/shard_map/ppermute | solution.py:48
  95.7 5.1 %collective-permute-start.21 = (bf16[4,16,2048]{2,1,0:T(8,128)(2,1)S(1)}, bf16[4,16,2048]{2,1,0:T(8,128)(2,1)S(1)}, u32[]{:S(2)}, u32[]{:S(2)}) collective-permute-start(bf16[4,16,2048]{2,1,0:T(8,128)(2,1)S(1)} %collective-permute-done.17.refs_1_), channel_id=1, source_target_pairs={{4,0},{0,4},{12,8},{8,12},{20,16},{16,20},{28,24},{24,28},{36,32},... | collective-permute-start | bytes 786440 | tf_op jit(solution)/shard_map/ppermute | solution.py:48
  97.5 3.2 %collective-permute-start.22 = (bf16[4,16,2048]{2,1,0:T(8,128)(2,1)S(1)}, bf16[4,16,2048]{2,1,0:T(8,128)(2,1)S(1)}, u32[]{:S(2)}, u32[]{:S(2)}) collective-permute-start(bf16[4,16,2048]{2,1,0:T(8,128)(2,1)S(1)} %collective-permute-done.18.refs_2_), channel_id=1, source_target_pairs={{4,0},{0,4},{12,8},{8,12},{20,16},{16,20},{28,24},{24,28},{36,32},... | collective-permute-start | bytes 786440 | tf_op jit(solution)/shard_map/ppermute | solution.py:48
  100.7 1.5 %collective-permute-start.23 = (bf16[4,16,2048]{2,1,0:T(8,128)(2,1)S(1)}, bf16[4,16,2048]{2,1,0:T(8,128)(2,1)S(1)}, u32[]{:S(2)}, u32[]{:S(2)}) collective-permute-start(bf16[4,16,2048]{2,1,0:T(8,128)(2,1)S(1)} %collective-permute-done.19.refs_3_), channel_id=1, source_target_pairs={{4,0},{0,4},{12,8},{8,12},{20,16},{16,20},{28,24},{24,28},{36,32},... | collective-permute-start | bytes 786440 | tf_op jit(solution)/shard_map/ppermute | solution.py:48
  104.9 5.9 %collective-permute-start.24 = (bf16[64,512]{1,0:T(8,128)(2,1)S(1)}, bf16[64,512]{1,0:T(8,128)(2,1)S(1)}, u32[]{:S(2)}, u32[]{:S(2)}) collective-permute-start(bf16[64,512]{1,0:T(8,128)(2,1)S(1)} %get-tuple-element.44), channel_id=1, source_target_pairs={{3,0},{0,1},{1,2},{2,3},{7,4},{4,5},{5,6},{6,7},{11,8},{8,9},{9,10... | collective-permute-start | bytes 196616 | tf_op jit(solution)/shard_map/ppermute | solution.py:52
  106.5 6.4 %collective-permute-start.25 = (bf16[64,512]{1,0:T(8,128)(2,1)S(1)}, bf16[64,512]{1,0:T(8,128)(2,1)S(1)}, u32[]{:S(2)}, u32[]{:S(2)}) collective-permute-start(bf16[64,512]{1,0:T(8,128)(2,1)S(1)} %get-tuple-element.45), channel_id=1, source_target_pairs={{2,0},{3,1},{0,2},{1,3},{6,4},{7,5},{4,6},{5,7},{10,8},{11,9},{8,1... | collective-permute-start | bytes 196616 | tf_op jit(solution)/shard_map/ppermute | solution.py:52
  109.4 4.3 %collective-permute-start.26 = (bf16[64,512]{1,0:T(8,128)(2,1)S(1)}, bf16[64,512]{1,0:T(8,128)(2,1)S(1)}, u32[]{:S(2)}, u32[]{:S(2)}) collective-permute-start(bf16[64,512]{1,0:T(8,128)(2,1)S(1)} %get-tuple-element.46), channel_id=1, source_target_pairs={{1,0},{2,1},{3,2},{0,3},{5,4},{6,5},{7,6},{4,7},{9,8},{10,9},{11,1... | collective-permute-start | bytes 196616 | tf_op jit(solution)/shard_map/ppermute | solution.py:52

commit v4 on v3

--- a/solution.py
+++ b/solution.py
@@ -78,8 +78,13 @@
 
 def weigh(s):
     top = jnp.max(s, axis=1, keepdims=True)
-    w = jnp.exp2((s - top) * SCALE)
-    return top, jnp.sum(w, axis=1, keepdims=True), w.astype(BF16)
+    return top, jnp.exp2((s - top) * SCALE).astype(BF16)
+
+
+def sum_up(w, values):
+    ones = jnp.ones(values.shape, BF16)
+    both = jnp.dot(w, jnp.concatenate([values, ones], axis=1), preferred_element_type=F32)
+    return both[:, :HD], both[:, HD:]
 
 
 def in_parts(value, count):
@@ -96,12 +101,7 @@
     return jnp.concatenate([*in_parts(top, 3), *in_parts(total, 2), rest], axis=1)
 
 
-def unpack_stats(tile):
-    parts = [tile[:, i * GROUP : (i + 1) * GROUP].astype(F32) for i in range(5)]
-    return (parts[0] + parts[1]) + parts[2], parts[3] + parts[4]
-
-
-def put_partial(out, index, top, total, summed):
+def put_partial(out, index, top, summed, total):
     lane = lax.broadcasted_iota(jnp.int32, (ROWS, HD), 1)
     tops = totals = jnp.zeros((ROWS, HD), F32)
     for g in range(GROUP):
@@ -174,9 +174,8 @@
 
 def attend_kernel(info, valid, *refs):
     own, other, ahead, cache, new = refs[:SIDE], refs[SIDE : 2 * SIDE], *refs[2 * SIDE : 2 * SIDE + 3]
-    sent, mine, new_out, queries, keys, held, arrived = refs[2 * SIDE + 3 :]
+    sent, mine, queries, keys, held, mine_new, arrived = refs[2 * SIDE + 3 :]
     step = pl.program_id(0)
-    last = pl.num_programs(0) - 1
     core = info[2]
     slot = cache.shape[1]
     side = step % 2
@@ -190,7 +189,7 @@
 
     @pl.when(step == 0)
     def _():
-        for request in range(REQS):
+        for request in range(2):
             fetch(request).start()
         assemble(info, own, other, queries)
 
@@ -200,15 +199,18 @@
         def _(now=now):
             for r in range(2):
                 fetch(2 * now + r).wait()
-
-    @pl.when(2 * step >= AHEAD)
-    def _():
-        for r in range(2):
-
-            def put(head, rows, value, r=r):
+            if now == 0:
+                for request in range(2, REQS):
+                    fetch(request).start()
+
+    for r in range(2):
+
+        @pl.when(2 * step + r >= AHEAD)
+        def _(r=r):
+            def put(head, rows, value):
                 keys[side, r, head, rows] = value
 
-            split_heads(held, 2 * step - AHEAD + r, put)
+            split_heads(held, 2 * step + r - AHEAD, put)
 
     first, second = valid[2 * step], valid[2 * step + 1]
     where = [
@@ -222,9 +224,8 @@
         return dot_nt(queries[head, 4 * step + 2 * r + half], keys[side, r, head, :, :HD])
 
     def finish(r, head, out, half, s):
-        top, total, w = weigh(s)
-        summed = jnp.dot(w, keys[side, r, head, :, HD:], preferred_element_type=F32)
-        put_partial(out, 2 * r + half, top, total, summed)
+        top, w = weigh(s)
+        put_partial(out, 2 * r + half, top, *sum_up(w, keys[side, r, head, :, HD:]))
 
     full = jnp.logical_and(first >= slot, second >= slot)
 
@@ -260,15 +261,16 @@
                         out[2 * r + half, :, :FEATS] = jnp.zeros((ROWS, FEATS), BF16)
                         out[2 * r + half, :, FEATS:] = none
 
-    @pl.when(step == last)
+    z, x = info[0], info[1]
+
+    @pl.when(step == z)
     def _():
-        z, x = info[0], info[1]
         s = dot_nt(queries[core, z * SIDE + x], new[0, :, :HD])
         token = (x % 2) * ROWS + lax.broadcasted_iota(jnp.int32, s.shape, 0) % ROWS
         key = lax.broadcasted_iota(jnp.int32, s.shape, 1)
-        top, total, w = weigh(jnp.where(key <= token, s, EMPTY))
-        summed = jnp.dot(w, new[0, :, HD:], preferred_element_type=F32)
-        put_partial(new_out, 0, top, total, summed)
+        top, w = weigh(jnp.where(key <= token, s, EMPTY))
+        put_partial(mine_new, 0, top, *sum_up(w, new[0, :, HD:]))
+        merge_into([(mine, x)], [[(mine, x)], [(mine_new, 0)]])
 
 
 def attend(info, valid, own, other, ahead, cache, new):
@@ -276,17 +278,17 @@
     blocks = jax.ShapeDtypeStruct((2 * reqs, ROWS, WIDE), BF16)
     return pl.pallas_call(
         attend_kernel,
-        out_shape=[blocks, blocks, jax.ShapeDtypeStruct((1, ROWS, WIDE), BF16)],
+        out_shape=[blocks, blocks],
         grid_spec=pltpu.PrefetchScalarGridSpec(
             num_scalar_prefetch=2,
             grid=(reqs // 2,),
             in_specs=[whole()] * (2 * SIDE) + [pl.BlockSpec(memory_space=pl.ANY)] * 2 + [whole()],
-            out_specs=[pl.BlockSpec((4, ROWS, WIDE), lambda i, info, valid: (i, 0, 0))] * 2
-            + [pl.BlockSpec((1, ROWS, WIDE), lambda i, info, valid: (0, 0, 0))],
+            out_specs=[pl.BlockSpec((4, ROWS, WIDE), lambda i, info, valid: (i, 0, 0))] * 2,
             scratch_shapes=[
                 pltpu.VMEM((2, SIDE * SIDE, BLOCK, HD), BF16),
                 pltpu.VMEM((2, 2, 2, per, 2 * HD), BF16),
                 pltpu.VMEM((REQS - AHEAD, *cache.shape[1:]), BF16),
+                pltpu.VMEM((1, ROWS, WIDE), BF16),
                 pltpu.SemaphoreType.DMA((REQS,)),
             ],
         ),
@@ -298,56 +300,78 @@
     )(info, valid, *own, *other, ahead, cache, new)
 
 
-def factors_of(parts):
-    stats = [unpack_stats(ref[index, :, FEATS:]) for ref, index, _ in parts]
-    tops = [top if counts is None else jnp.where(counts, top, EMPTY) for (top, _), (_, _, counts) in zip(stats, parts)]
+def zero_one(shape, test):
+    return test(lax.broadcasted_iota(jnp.int32, shape, 0), lax.broadcasted_iota(jnp.int32, shape, 1)).astype(BF16)
+
+
+def dot(a, b):
+    return jnp.dot(a, b, preferred_element_type=F32)
+
+
+def factors_of(sources):
+    def apart(i, j):
+        part, head = i // GROUP, i % GROUP
+        top = (j < HD) & (head == j) & (part < 3)
+        return top | ((head == j - HD) & ((part == 3) | (part == 4)))
+
+    pick = zero_one((HD, 2 * HD), apart)
+    tops, totals = [], []
+    for blocks in sources:
+        both = dot(jnp.concatenate([ref[index, :, FEATS:] for ref, index in blocks], axis=0), pick)
+        tops.append(both[:, :HD])
+        totals.append(both[:, HD:])
     best = functools.reduce(jnp.maximum, tops)
     factors = [jnp.exp2((top - best) * SCALE) for top in tops]
-    factors = [f if counts is None else jnp.where(counts, f, 0.0) for f, (_, _, counts) in zip(factors, parts)]
-    return best, sum(f * total for f, (_, total) in zip(factors, stats)), factors
-
-
-def summed_of(parts, factors, g):
-    cols = slice(g * HD, (g + 1) * HD)
-    return sum(f[:, g : g + 1] * ref[index, :, cols].astype(F32) for f, (ref, index, _) in zip(factors, parts))
-
-
-def merge_into(jobs):
-    ready = [factors_of(parts) for _, _, parts in jobs]
-    for (out, index, _), (best, total, _) in zip(jobs, ready):
-        out[index, :, FEATS:] = pack_stats(best, total)
-    for (out, index, parts), (_, _, factors) in zip(jobs, ready):
+    return best, sum(f * total for f, total in zip(factors, totals)), factors
+
+
+def spread(factors):
+    place = zero_one((2 * HD, FEATS), lambda i, j: i % HD == j // HD)
+    return dot(jnp.concatenate(in_parts(factors, 2), axis=1), place)
+
+
+def sum_into(outs, sources, factors):
+    wide = [spread(f) for f in factors]
+    for b, (out, index) in enumerate(outs):
+        rows = slice(b * ROWS, (b + 1) * ROWS)
         for g in range(GROUP):
-            out[index, :, g * HD : (g + 1) * HD] = summed_of(parts, factors, g).astype(BF16)
-
-
-def twin_kernel(info, mine, got, new, *outs):
+            cols = slice(g * HD, (g + 1) * HD)
+            terms = [f[rows, cols] * blocks[b][0][blocks[b][1], :, cols].astype(F32) for f, blocks in zip(wide, sources)]
+            out[index, :, cols] = sum(terms).astype(BF16)
+
+
+def merge_into(outs, sources):
+    best, total, factors = factors_of(sources)
+    join = zero_one((5 * HD, HD), lambda i, j: (i // HD * GROUP + i % HD == j) & (i % HD < GROUP))
+    stats = dot(jnp.concatenate([*in_parts(best, 3), *in_parts(total, 2)], axis=1), join).astype(BF16)
+    sum_into(outs, sources, factors)
+    for b, (out, index) in enumerate(outs):
+        out[index, :, FEATS:] = stats[b * ROWS : (b + 1) * ROWS]
+
+
+def twin_kernel(info, mine, got, *outs):
     z, x, core = info[0], info[1], info[2]
-    jobs = []
+    places, chips = [], []
     for d in range(SIDE):
         for j in range(SIDE):
-            chip = jnp.where(core == 0, ((z + d) % SIDE) * SIDE + j, j * SIDE + (x + d) % SIDE)
-            parts = [(mine, chip, None), (got, chip, None)]
-            if d == 0:
-                parts.append((new, 0, chip == z * SIDE + x))
-            jobs.append((outs[d], j, parts))
-    merge_into(jobs)
-
-
-def merge_twins(info, mine, got, new):
+            places.append((outs[d], j))
+            chips.append(jnp.where(core == 0, ((z + d) % SIDE) * SIDE + j, j * SIDE + (x + d) % SIDE))
+    merge_into(places, [[(mine, chip) for chip in chips], [(got, chip) for chip in chips]])
+
+
+def merge_twins(info, mine, got):
     return pl.pallas_call(
         twin_kernel,
         out_shape=[jax.ShapeDtypeStruct((SIDE, ROWS, WIDE), BF16)] * SIDE,
-        in_specs=[pl.BlockSpec(memory_space=pltpu.SMEM)] + [whole()] * 3,
+        in_specs=[pl.BlockSpec(memory_space=pltpu.SMEM)] + [whole()] * 2,
         out_specs=[whole()] * SIDE,
         compiler_params=pltpu.CompilerParams(vmem_limit_bytes=24 * MIB),
         name="merge_twins",
-    )(info, mine, got, new)
+    )(info, mine, got)
 
 
 def four_kernel(*refs):
-    out = refs[-1]
-    merge_into([(out, j, [(ref, j, None) for ref in refs[:-1]]) for j in range(SIDE)])
+    merge_into([(refs[-1], j) for j in range(SIDE)], [[(ref, j) for j in range(SIDE)] for ref in refs[:-1]])
 
 
 def merge_four(parts):
@@ -362,15 +386,11 @@
 
 
 def final_kernel(*refs):
-    out = refs[-1]
-    blocks = [[(ref, j, None) for ref in refs[:-1]] for j in range(SIDE)]
-    ready = []
-    for parts in blocks:
-        _, total, factors = factors_of(parts)
-        ready.append([f / total for f in factors])
-    for j, (parts, factors) in enumerate(zip(blocks, ready)):
-        for g in range(GROUP):
-            out[j, :, g * HD : (g + 1) * HD] = summed_of(parts, factors, g).astype(BF16)
+    sources = [[(ref, j) for j in range(SIDE)] for ref in refs[:-1]]
+    _, total, factors = factors_of(sources)
+    lane = lax.broadcasted_iota(jnp.int32, total.shape, 1)
+    total = jnp.where(lane < GROUP, total, 1.0)
+    sum_into([(refs[-1], j) for j in range(SIDE)], sources, [f / total for f in factors])
 
 
 def merge_final(parts):
@@ -386,66 +406,53 @@
 
 def project_kernel(info, *refs):
     own, other, weight = refs[:SIDE], refs[SIDE : 2 * SIDE], refs[2 * SIDE]
-    keep, sends, held, acc = refs[2 * SIDE + 1], refs[2 * SIDE + 2 : 3 * SIDE + 1], refs[-2], refs[-1]
-    step = pl.program_id(0)
+    keep, sends, held = refs[2 * SIDE + 1], refs[2 * SIDE + 2 : 3 * SIDE + 1], refs[-1]
     z, x, core, y = info[0], info[1], info[2], info[3]
-    depth = weight.shape[0]
-    per = FEATS // depth
-
-    @pl.when(step == 0)
+
+    def place(zero, one):
+        for d in range(SIDE):
+            for j in range(SIDE):
+                for half, values, chip in (
+                    (0, zero, ((z + d) % SIDE) * SIDE + j),
+                    (1, one, j * SIDE + (x + d) % SIDE),
+                ):
+                    rows = pl.ds(pl.multiple_of(chip * ROWS, ROWS), ROWS)
+                    held[rows, half * FEATS : (half + 1) * FEATS] = values[d][j]
+
+    @pl.when(core == 0)
     def _():
-        acc[...] = jnp.zeros_like(acc)
-
-        def place(zero, one):
-            for d in range(SIDE):
-                for j in range(SIDE):
-                    for half, values, chip in (
-                        (0, zero, ((z + d) % SIDE) * SIDE + j),
-                        (1, one, j * SIDE + (x + d) % SIDE),
-                    ):
-                        rows = pl.ds(pl.multiple_of(chip * ROWS, ROWS), ROWS)
-                        for k in range(per):
-                            held[half * per + k, rows, :] = values[d][j, :, k * depth : (k + 1) * depth]
-
-        @pl.when(core == 0)
-        def _():
-            place(own, other)
-
-        @pl.when(core == 1)
-        def _():
-            place(other, own)
-
-    acc[...] += jnp.dot(held[step], weight[...], preferred_element_type=F32)
-
-    @pl.when(step == pl.num_programs(0) - 1)
+        place(own, other)
+
+    @pl.when(core == 1)
     def _():
-        count = keep.shape[0]
+        place(other, own)
+
+    count = keep.shape[0]
+    total = dot(held[...], weight[...])
+    for group in range(SIDE):
+        rows = total[group * count : (group + 1) * count]
         for d in range(SIDE):
-            rows = acc[pl.ds(pl.multiple_of(((y + d) % SIDE) * count, count), count), :]
-            if d == 0:
-                keep[...] = rows
-            else:
-                sends[d - 1][...] = rows.astype(BF16)
+
+            @pl.when((y + d) % SIDE == group)
+            def _(rows=rows, d=d):
+                if d == 0:
+                    keep[...] = rows
+                else:
+                    sends[d - 1][...] = rows.astype(BF16)
 
 
 def project(info, own, other, weight):
-    depth = 1024
-    cols = weight.shape[1]
+    depth, cols = weight.shape
     rows = SIDE * SIDE * ROWS
     return pl.pallas_call(
         project_kernel,
         out_shape=[jax.ShapeDtypeStruct((rows // SIDE, cols), F32)]
         + [jax.ShapeDtypeStruct((rows // SIDE, cols), BF16)] * (SIDE - 1),
-        grid=(weight.shape[0] // depth,),
-        in_specs=[pl.BlockSpec(memory_space=pltpu.SMEM)]
-        + [whole()] * (2 * SIDE)
-        + [pl.BlockSpec((depth, cols), lambda i: (i, 0))],
+        in_specs=[pl.BlockSpec(memory_space=pltpu.SMEM)] + [whole()] * (2 * SIDE + 1),
         out_specs=[whole()] * SIDE,
-        scratch_shapes=[
-            pltpu.VMEM((weight.shape[0] // depth, rows, depth), BF16),
-            pltpu.VMEM((rows, cols), F32),
-        ],
-        compiler_params=pltpu.CompilerParams(vmem_limit_bytes=32 * MIB),
+        scratch_shapes=[pltpu.VMEM((rows, depth), BF16)],
+        compiler_params=pltpu.CompilerParams(vmem_limit_bytes=24 * MIB),
+        cost_estimate=pl.CostEstimate(flops=2 * rows * depth * cols, bytes_accessed=depth * cols * 2, transcendentals=0),
         name="project",
     )(info, *own, *other, weight)
 
@@ -467,8 +474,8 @@
     *own, ahead = lax.optimization_barrier((*own, ahead))
     other = [from_twin(part) for part in own]
 
-    sent, mine, from_new = attend(info, valid, own, other, ahead, cache, new)
-    parts = merge_twins(info, mine, from_twin(sent), from_new)
+    sent, mine = attend(info, valid, own, other, ahead, cache, new)
+    parts = merge_twins(info, mine, from_twin(sent))
     zs = merge_four([parts[0]] + [from_second(parts[SIDE - s], s) for s in (1, 2, 3)])
     rows = merge_final([zs] + [from_first(zs, s) for s in (1, 2, 3)])
 

time: 115 us -> 117 us (1.017)
  starting transfers between devices: 31.7 us -> 36.9 us
  Pallas kernels: 47.8 us -> 45.4 us
    ppermute x9, starting transfers between devices: 13.7 us -> 20.9 us  [from_second(): return lax.ppermute(value, 'ctx', pairs)]
    ppermute x6, starting transfers between devices: 10.7 us -> 8.62 us  [from_first(): return lax.ppermute(value, 'ctx', pairs)]
    pallas_call x1, Pallas kernels: 2.89 us -> 1.68 us  [merge_twins(): pl.pallas_call(twin_kernel, out_shape=[jax.ShapeDtypeStruct((SIDE, ROWS,...]
  transfers between devices with their start and end apart: 27 -> 27, of which waited for: 20 -> 19; matrix products, arithmetic and copies ran while one was open for 0% -> 0% of each run, Pallas kernels for 11% -> 10%
where the time goes in v4:
time: 117 us
  Pallas kernels  45.4 us (39%)
  starting transfers between devices  36.9 us (32%)
  waiting for transfers between devices  34.1 us (29%)
    pallas_call x1, Pallas kernels, attend(): pl.pallas_call(attend_kernel, out_shape=[blocks, blocks], grid_spec=pltpu...  28.2 us
    ppermute x9, starting transfers between devices, from_second(): return lax.ppermute(value, 'ctx', pairs)  20.9 us
    ppermute x9, waiting for transfers between devices, from_second(): return lax.ppermute(value, 'ctx', pairs)  15.1 us
    pallas_call x2, Pallas kernels, split_ahead(): pl.pallas_call(ahead_kernel, grid=(count,), in_specs=[pl.BlockSpec((1, pe...  12 us
    ppermute x6, waiting for transfers between devices, from_first(): return lax.ppermute(value, 'ctx', pairs)  10.3 us
    ppermute x6, starting transfers between devices, from_first(): return lax.ppermute(value, 'ctx', pairs)  8.62 us
    ppermute x3, starting transfers between devices, from_plane(): lax.ppermute(value, 'kvh', [((s + step) % SIDE, s) for s in range(SIDE)])  5.91 us
    ppermute x9, waiting for transfers between devices, from_twin(): lax.ppermute(value, 'ctx', [(at(z, x, 1 - c), at(z, x, c)) for z, x, c in...  5.77 us
  transfers between devices with their start and end apart: 27, of which 19 were waited for; matrix products, arithmetic and copies ran while one was open for 0% of the time, Pallas kernels for 10%

profile of v4, /device:TPU:0, one launch (start us, length us, event | category | flops | bytes accessed | tf_op | source)
XLA Modules:
  0.0 117.2 jit_solution(4783309811114827570)
XLA Ops:
  0.0 2.8 %collective-permute-start = (bf16[8,4096]{1,0:T(8,128)(2,1)}, bf16[8,4096]{1,0:T(8,128)(2,1)S(1)}, u32[]{:S(2)}, u32[]{:S(2)}) collective-permute-start(bf16[8,4096]{1,0:T(8,128)(2,1)} %refs_0_.1), channel_id=1, source_target_pairs={{8,0},{36,4},{16,8},{44,12},{24,16},{52,20},{0,24},{60,28},{40,32}... | collective-permute-start | bytes 196616 | tf_op jit(solution)/shard_map/ppermute | solution.py:39
  2.8 0.8 collective-permute-start.1
  3.6 0.9 collective-permute-start.2
  4.6 4.0 %split_ahead.2.refs_0_ = bf16[4,2,2048,256]{3,2,1,0:T(8,128)(2,1)} custom-call(bf16[8,2048,2,256]{3,2,1,0:T(2,128)(2,1)} %refs_9_.1), custom_call_target="tpu_custom_call" | custom-call | bytes 8388608 | tf_op jit(solution)/shard_map/split_ahead/pallas_call | solution.py:161
  9.6 4.1 %collective-permute-start.3 = (bf16[4,8,4096]{2,1,0:T(8,128)(2,1)S(1)}, bf16[4,8,4096]{2,1,0:T(8,128)(2,1)S(1)}, u32[]{:S(2)}, u32[]{:S(2)}) collective-permute-start(bf16[4,8,4096]{2,1,0:T(8,128)(2,1)S(1)} %stack.21.refs_0_), channel_id=1, source_target_pairs={{32,0},{12,4},{40,8},{20,12},{48,16},{28,20},{56,24},{4,28},{64,32... | collective-permute-start | bytes 786440 | tf_op jit(solution)/shard_map/ppermute | solution.py:44
  13.7 1.3 %collective-permute-start.5 = (bf16[4,8,4096]{2,1,0:T(8,128)(2,1)S(1)}, bf16[4,8,4096]{2,1,0:T(8,128)(2,1)S(1)}, u32[]{:S(2)}, u32[]{:S(2)}) collective-permute-start(bf16[4,8,4096]{2,1,0:T(8,128)(2,1)S(1)} %stack.21.refs_0_), channel_id=1, source_target_pairs={{96,0},{28,4},{104,8},{4,12},{112,16},{12,20},{120,24},{20,28},{0,... | collective-permute-start | bytes 786440 | tf_op jit(solution)/shard_map/ppermute | solution.py:44
  14.9 8.1 %split_ahead.3.refs_8_ = bf16[4,2,2048,256]{3,2,1,0:T(8,128)(2,1)} custom-call(bf16[8,2048,2,256]{3,2,1,0:T(2,128)(2,1)} %refs_9_.1, bf16[4,2,2048,256]{3,2,1,0:T(8,128)(2,1)} %split_ahead.2.refs_0_), custom_call_target="tpu_custom_call", output_to_operand_aliasing={{}: (1, {})} | custom-call | bytes 25165824 | tf_op jit(solution)/shard_map/split_ahead/pallas_call | solution.py:161
  23.0 1.1 collective-permute-done.5.refs_3_
  26.7 28.2 %attend.1 = (bf16[16,16,2176]{2,1,0:T(8,128)(2,1)S(1)}, bf16[16,16,2176]{2,1,0:T(8,128)(2,1)S(1)}) custom-call(s32[4]{0:T(128)S(1)} %pad_add_fusion.info, s32[8]{0:T(128)S(1)} %subtract_clamp_fusion.valid, bf16[4,8,4096]{2,1,0:T(8,128)(2,1)S(1)} %stack.21.refs_0_, bf16[4,8,4096]{2,1,0:T(8,128)(2,1)S(1)} %collective-permute-done.3.refs_1_, ...), custom_call_target="tpu_custom_call" | custom-call | flops 8589934592 | bytes 16777216 | tf_op jit(solution)/shard_map/attend/pallas_call | solution.py:279
  55.3 2.6 %collective-permute-done.10.got = bf16[16,16,2176]{2,1,0:T(8,128)(2,1)S(1)} collective-permute-done((bf16[16,16,2176]{2,1,0:T(8,128)(2,1)S(1)}, bf16[16,16,2176]{2,1,0:T(8,128)(2,1)S(1)}, u32[]{:S(2)}, u32[]{:S(2)}) %collective-permute-start.10) | collective-permute-done | bytes 1114144 | tf_op jit(solution)/shard_map/ppermute | solution.py:48
  57.9 1.7 %merge_twins.1 = (bf16[4,16,2176]{2,1,0:T(8,128)(2,1)S(1)}, bf16[4,16,2176]{2,1,0:T(8,128)(2,1)S(1)}, bf16[4,16,2176]{2,1,0:T(8,128)(2,1)S(1)}, bf16[4,16,2176]{2,1,0:T(8,128)(2,1)S(1)}) custom-call(s32[4]{0:T(128)S(1)} %pad_add_fusion.info, bf16[16,16,2176]{2,1,0:T(8,128)(2,1)S(1)} %get-tuple-element.35.mine, ...), custom_call_target="tpu_custom_call" | custom-call | tf_op jit(solution)/shard_map/merge_twins/pallas_call | solution.py:363
  59.6 1.2 %collective-permute-start.11 = (bf16[4,16,2176]{2,1,0:T(8,128)(2,1)S(1)}, bf16[4,16,2176]{2,1,0:T(8,128)(2,1)S(1)}, u32[]{:S(2)}, u32[]{:S(2)}) collective-permute-start(bf16[4,16,2176]{2,1,0:T(8,128)(2,1)S(1)} %get-tuple-element.38), channel_id=1, source_target_pairs={{32,0},{12,4},{40,8},{20,12},{48,16},{28,20},{56,24},{4,28},{64,32... | collective-permute-start | bytes 835592 | tf_op jit(solution)/shard_map/ppermute | solution.py:44
  60.8 9.0 %collective-permute-start.12 = (bf16[4,16,2176]{2,1,0:T(8,128)(2,1)S(1)}, bf16[4,16,2176]{2,1,0:T(8,128)(2,1)S(1)}, u32[]{:S(2)}, u32[]{:S(2)}) collective-permute-start(bf16[4,16,2176]{2,1,0:T(8,128)(2,1)S(1)} %get-tuple-element.39), channel_id=1, source_target_pairs={{64,0},{20,4},{72,8},{28,12},{80,16},{4,20},{88,24},{12,28},{96,32... | collective-permute-start | bytes 835592 | tf_op jit(solution)/shard_map/ppermute | solution.py:44
  69.9 1.3 %collective-permute-start.13 = (bf16[4,16,2176]{2,1,0:T(8,128)(2,1)S(1)}, bf16[4,16,2176]{2,1,0:T(8,128)(2,1)S(1)}, u32[]{:S(2)}, u32[]{:S(2)}) collective-permute-start(bf16[4,16,2176]{2,1,0:T(8,128)(2,1)S(1)} %get-tuple-element.40), channel_id=1, source_target_pairs={{96,0},{28,4},{104,8},{4,12},{112,16},{12,20},{120,24},{20,28},{0,... | collective-permute-start | bytes 835592 | tf_op jit(solution)/shard_map/ppermute | solution.py:44
  71.2 3.2 %collective-permute-done.12.refs_2_ = bf16[4,16,2176]{2,1,0:T(8,128)(2,1)S(1)} collective-permute-done((bf16[4,16,2176]{2,1,0:T(8,128)(2,1)S(1)}, bf16[4,16,2176]{2,1,0:T(8,128)(2,1)S(1)}, u32[]{:S(2)}, u32[]{:S(2)}) %collective-permute-start.12) | collective-permute-done | bytes 278560 | tf_op jit(solution)/shard_map/ppermute | solution.py:44
  74.4 3.2 %collective-permute-done.13.refs_3_ = bf16[4,16,2176]{2,1,0:T(8,128)(2,1)S(1)} collective-permute-done((bf16[4,16,2176]{2,1,0:T(8,128)(2,1)S(1)}, bf16[4,16,2176]{2,1,0:T(8,128)(2,1)S(1)}, u32[]{:S(2)}, u32[]{:S(2)}) %collective-permute-start.13) | collective-permute-done | bytes 278560 | tf_op jit(solution)/shard_map/ppermute | solution.py:44
  78.3 2.5 %collective-permute-start.14 = (bf16[4,16,2176]{2,1,0:T(8,128)(2,1)S(1)}, bf16[4,16,2176]{2,1,0:T(8,128)(2,1)S(1)}, u32[]{:S(2)}, u32[]{:S(2)}) collective-permute-start(bf16[4,16,2176]{2,1,0:T(8,128)(2,1)S(1)} %merge_four.1.refs_0_), channel_id=1, source_target_pairs={{8,0},{36,4},{16,8},{44,12},{24,16},{52,20},{0,24},{60,28},{40,32}... | collective-permute-start | bytes 835592 | tf_op jit(solution)/shard_map/ppermute | solution.py:39
  80.8 1.6 %collective-permute-start.15 = (bf16[4,16,2176]{2,1,0:T(8,128)(2,1)S(1)}, bf16[4,16,2176]{2,1,0:T(8,128)(2,1)S(1)}, u32[]{:S(2)}, u32[]{:S(2)}) collective-permute-start(bf16[4,16,2176]{2,1,0:T(8,128)(2,1)S(1)} %merge_four.1.refs_0_), channel_id=1, source_target_pairs={{16,0},{68,4},{24,8},{76,12},{0,16},{84,20},{8,24},{92,28},{48,32}... | collective-permute-start | bytes 835592 | tf_op jit(solution)/shard_map/ppermute | solution.py:39
  82.4 5.5 %collective-permute-done.14.refs_1_ = bf16[4,16,2176]{2,1,0:T(8,128)(2,1)S(1)} collective-permute-done((bf16[4,16,2176]{2,1,0:T(8,128)(2,1)S(1)}, bf16[4,16,2176]{2,1,0:T(8,128)(2,1)S(1)}, u32[]{:S(2)}, u32[]{:S(2)}) %collective-permute-start.14) | collective-permute-done | bytes 278560 | tf_op jit(solution)/shard_map/ppermute | solution.py:39
  87.9 1.1 collective-permute-done.15.refs_2_
  89.0 2.9 %collective-permute-done.16.refs_3_ = bf16[4,16,2176]{2,1,0:T(8,128)(2,1)S(1)} collective-permute-done((bf16[4,16,2176]{2,1,0:T(8,128)(2,1)S(1)}, bf16[4,16,2176]{2,1,0:T(8,128)(2,1)S(1)}, u32[]{:S(2)}, u32[]{:S(2)}) %collective-permute-start.16) | collective-permute-done | bytes 278560 | tf_op jit(solution)/shard_map/ppermute | solution.py:39
  93.1 3.4 %collective-permute-start.18 = (bf16[4,16,2048]{2,1,0:T(8,128)(2,1)S(1)}, bf16[4,16,2048]{2,1,0:T(8,128)(2,1)S(1)}, u32[]{:S(2)}, u32[]{:S(2)}) collective-permute-start(bf16[4,16,2048]{2,1,0:T(8,128)(2,1)S(1)} %merge_final.1.refs_0_), channel_id=1, source_target_pairs={{64,0},{20,4},{72,8},{28,12},{80,16},{4,20},{88,24},{12,28},{96,32... | collective-permute-start | bytes 786440 | tf_op jit(solution)/shard_map/ppermute | solution.py:44
  96.5 2.5 %collective-permute-done.17.refs_1_ = bf16[4,16,2048]{2,1,0:T(8,128)(2,1)S(1)} collective-permute-done((bf16[4,16,2048]{2,1,0:T(8,128)(2,1)S(1)}, bf16[4,16,2048]{2,1,0:T(8,128)(2,1)S(1)}, u32[]{:S(2)}, u32[]{:S(2)}) %collective-permute-start.17) | collective-permute-done | bytes 262176 | tf_op jit(solution)/shard_map/ppermute | solution.py:44
  99.0 2.0 %collective-permute-done.18.refs_2_ = bf16[4,16,2048]{2,1,0:T(8,128)(2,1)S(1)} collective-permute-done((bf16[4,16,2048]{2,1,0:T(8,128)(2,1)S(1)}, bf16[4,16,2048]{2,1,0:T(8,128)(2,1)S(1)}, u32[]{:S(2)}, u32[]{:S(2)}) %collective-permute-start.18) | collective-permute-done | bytes 262176 | tf_op jit(solution)/shard_map/ppermute | solution.py:44
  101.0 3.1 %collective-permute-done.19.refs_3_ = bf16[4,16,2048]{2,1,0:T(8,128)(2,1)S(1)} collective-permute-done((bf16[4,16,2048]{2,1,0:T(8,128)(2,1)S(1)}, bf16[4,16,2048]{2,1,0:T(8,128)(2,1)S(1)}, u32[]{:S(2)}, u32[]{:S(2)}) %collective-permute-start.19) | collective-permute-done | bytes 262176 | tf_op jit(solution)/shard_map/ppermute | solution.py:44
  104.1 1.5 %collective-permute-done.23.refs_7_ = bf16[4,16,2048]{2,1,0:T(8,128)(2,1)S(1)} collective-permute-done((bf16[4,16,2048]{2,1,0:T(8,128)(2,1)S(1)}, bf16[4,16,2048]{2,1,0:T(8,128)(2,1)S(1)}, u32[]{:S(2)}, u32[]{:S(2)}) %collective-permute-start.23) | collective-permute-done | bytes 262176 | tf_op jit(solution)/shard_map/ppermute | solution.py:48
  105.7 2.1 %project.1 = (f32[64,512]{1,0:T(8,128)S(1)}, bf16[64,512]{1,0:T(8,128)(2,1)S(1)}, bf16[64,512]{1,0:T(8,128)(2,1)S(1)}, bf16[64,512]{1,0:T(8,128)(2,1)S(1)}) custom-call(s32[4]{0:T(128)S(1)} %pad_add_fusion.info, bf16[4,16,2048]{2,1,0:T(8,128)(2,1)S(1)} %merge_final.1.refs_0_, bf16[4,16,2048]{2,1,0:T(8,128)(2,1)S(1)} %collective-permute-done.17.refs_1_, ...), custom_call_target="tpu_custom_call" | custom-call | flops 1073741824 | bytes 4194304 | tf_op jit(solution)/shard_map/project/pallas_call | solution.py:447
  107.8 1.7 %collective-permute-start.24 = (bf16[64,512]{1,0:T(8,128)(2,1)S(1)}, bf16[64,512]{1,0:T(8,128)(2,1)S(1)}, u32[]{:S(2)}, u32[]{:S(2)}) collective-permute-start(bf16[64,512]{1,0:T(8,128)(2,1)S(1)} %get-tuple-element.42), channel_id=1, source_target_pairs={{3,0},{0,1},{1,2},{2,3},{7,4},{4,5},{5,6},{6,7},{11,8},{8,9},{9,10... | collective-permute-start | bytes 196616 | tf_op jit(solution)/shard_map/ppermute | solution.py:52
  109.4 2.9 %collective-permute-start.25 = (bf16[64,512]{1,0:T(8,128)(2,1)S(1)}, bf16[64,512]{1,0:T(8,128)(2,1)S(1)}, u32[]{:S(2)}, u32[]{:S(2)}) collective-permute-start(bf16[64,512]{1,0:T(8,128)(2,1)S(1)} %get-tuple-element.43), channel_id=1, source_target_pairs={{2,0},{3,1},{0,2},{1,3},{6,4},{7,5},{4,6},{5,7},{10,8},{11,9},{8,1... | collective-permute-start | bytes 196616 | tf_op jit(solution)/shard_map/ppermute | solution.py:52
  112.3 1.3 %collective-permute-start.26 = (bf16[64,512]{1,0:T(8,128)(2,1)S(1)}, bf16[64,512]{1,0:T(8,128)(2,1)S(1)}, u32[]{:S(2)}, u32[]{:S(2)}) collective-permute-start(bf16[64,512]{1,0:T(8,128)(2,1)S(1)} %get-tuple-element.44), channel_id=1, source_target_pairs={{1,0},{2,1},{3,2},{0,3},{5,4},{6,5},{7,6},{4,7},{9,8},{10,9},{11,1... | collective-permute-start | bytes 196616 | tf_op jit(solution)/shard_map/ppermute | solution.py:52
  113.7 2.2 %collective-permute-done.25 = bf16[64,512]{1,0:T(8,128)(2,1)S(1)} collective-permute-done((bf16[64,512]{1,0:T(8,128)(2,1)S(1)}, bf16[64,512]{1,0:T(8,128)(2,1)S(1)}, u32[]{:S(2)}, u32[]{:S(2)}) %collective-permute-start.25) | collective-permute-done | bytes 65568 | tf_op jit(solution)/shard_map/ppermute | solution.py:52
  115.8 0.8 collective-permute-done.26
  (43 shorter events, 6.8 us)
Async XLA Ops:
  0.0 4.5 %copy-start = (bf16[8,32,2,256]{3,2,1,0:T(2,128)(2,1)S(1)}, bf16[8,32,2,256]{3,2,1,0:T(2,128)(2,1)}, u32[]{:S(2)}) copy-start(bf16[8,32,2,256]{3,2,1,0:T(2,128)(2,1)} %param.7) | copy-start | bytes 786436
  0.0 8.7 %collective-permute-start = (bf16[8,4096]{1,0:T(8,128)(2,1)}, bf16[8,4096]{1,0:T(8,128)(2,1)S(1)}, u32[]{:S(2)}, u32[]{:S(2)}) collective-permute-start(bf16[8,4096]{1,0:T(8,128)(2,1)} %refs_0_.1), channel_id=1, source_target_pairs={{8,0},{36,4},{16,8},{44,12},{24,16},{52,20},{0,24},{60,28},{40,32}... | collective-permute-start | bytes 196616 | tf_op jit(solution)/shard_map/ppermute | solution.py:39
  2.8 6.0 %collective-permute-start.1 = (bf16[8,4096]{1,0:T(8,128)(2,1)}, bf16[8,4096]{1,0:T(8,128)(2,1)S(1)}, u32[]{:S(2)}, u32[]{:S(2)}) collective-permute-start(bf16[8,4096]{1,0:T(8,128)(2,1)} %refs_0_.1), channel_id=1, source_target_pairs={{16,0},{68,4},{24,8},{76,12},{0,16},{84,20},{8,24},{92,28},{48,32}... | collective-permute-start | bytes 196616 | tf_op jit(solution)/shard_map/ppermute | solution.py:39
  3.6 5.9 %collective-permute-start.2 = (bf16[8,4096]{1,0:T(8,128)(2,1)}, bf16[8,4096]{1,0:T(8,128)(2,1)S(1)}, u32[]{:S(2)}, u32[]{:S(2)}) collective-permute-start(bf16[8,4096]{1,0:T(8,128)(2,1)} %refs_0_.1), channel_id=1, source_target_pairs={{24,0},{100,4},{0,8},{108,12},{8,16},{116,20},{16,24},{124,28},{56... | collective-permute-start | bytes 196616 | tf_op jit(solution)/shard_map/ppermute | solution.py:39
  4.6 4.0 %copy-start.3 = (s32[8]{0:T(128)S(1)}, s32[8]{0:T(128)}, u32[]{:S(2)}) copy-start(s32[8]{0:T(128)} %param.8) | copy-start | bytes 100
  4.6 4.9 %copy-start.2 = (bf16[8,4096]{1,0:T(8,128)(2,1)S(1)}, bf16[8,4096]{1,0:T(8,128)(2,1)}, u32[]{:S(2)}) copy-start(bf16[8,4096]{1,0:T(8,128)(2,1)} %refs_0_.1) | copy-start | bytes 196612
  9.6 13.4 %collective-permute-start.3 = (bf16[4,8,4096]{2,1,0:T(8,128)(2,1)S(1)}, bf16[4,8,4096]{2,1,0:T(8,128)(2,1)S(1)}, u32[]{:S(2)}, u32[]{:S(2)}) collective-permute-start(bf16[4,8,4096]{2,1,0:T(8,128)(2,1)S(1)} %stack.21.refs_0_), channel_id=1, source_target_pairs={{32,0},{12,4},{40,8},{20,12},{48,16},{28,20},{56,24},{4,28},{64,32... | collective-permute-start | bytes 786440 | tf_op jit(solution)/shard_map/ppermute | solution.py:44
  13.7 9.3 %collective-permute-start.4 = (bf16[4,8,4096]{2,1,0:T(8,128)(2,1)S(1)}, bf16[4,8,4096]{2,1,0:T(8,128)(2,1)S(1)}, u32[]{:S(2)}, u32[]{:S(2)}) collective-permute-start(bf16[4,8,4096]{2,1,0:T(8,128)(2,1)S(1)} %stack.21.refs_0_), channel_id=1, source_target_pairs={{64,0},{20,4},{72,8},{28,12},{80,16},{4,20},{88,24},{12,28},{96,32... | collective-permute-start | bytes 786440 | tf_op jit(solution)/shard_map/ppermute | solution.py:44
  13.7 10.4 %collective-permute-start.5 = (bf16[4,8,4096]{2,1,0:T(8,128)(2,1)S(1)}, bf16[4,8,4096]{2,1,0:T(8,128)(2,1)S(1)}, u32[]{:S(2)}, u32[]{:S(2)}) collective-permute-start(bf16[4,8,4096]{2,1,0:T(8,128)(2,1)S(1)} %stack.21.refs_0_), channel_id=1, source_target_pairs={{96,0},{28,4},{104,8},{4,12},{112,16},{12,20},{120,24},{20,28},{0,... | collective-permute-start | bytes 786440 | tf_op jit(solution)/shard_map/ppermute | solution.py:44
  24.1 1.5 %collective-permute-start.6 = (bf16[4,8,4096]{2,1,0:T(8,128)(2,1)S(1)}, bf16[4,8,4096]{2,1,0:T(8,128)(2,1)S(1)}, u32[]{:S(2)}, u32[]{:S(2)}) collective-permute-start(bf16[4,8,4096]{2,1,0:T(8,128)(2,1)S(1)} %stack.21.refs_0_), channel_id=1, source_target_pairs={{4,0},{0,4},{12,8},{8,12},{20,16},{16,20},{28,24},{24,28},{36,32},... | collective-permute-start | bytes 786440 | tf_op jit(solution)/shard_map/ppermute | solution.py:48
  24.1 1.9 %collective-permute-start.7 = (bf16[4,8,4096]{2,1,0:T(8,128)(2,1)S(1)}, bf16[4,8,4096]{2,1,0:T(8,128)(2,1)S(1)}, u32[]{:S(2)}, u32[]{:S(2)}) collective-permute-start(bf16[4,8,4096]{2,1,0:T(8,128)(2,1)S(1)} %collective-permute-done.3.refs_1_), channel_id=1, source_target_pairs={{4,0},{0,4},{12,8},{8,12},{20,16},{16,20},{28,24},{24,28},{36,32},... | collective-permute-start | bytes 786440 | tf_op jit(solution)/shard_map/ppermute | solution.py:48
  24.6 1.8 %collective-permute-start.8 = (bf16[4,8,4096]{2,1,0:T(8,128)(2,1)S(1)}, bf16[4,8,4096]{2,1,0:T(8,128)(2,1)S(1)}, u32[]{:S(2)}, u32[]{:S(2)}) collective-permute-start(bf16[4,8,4096]{2,1,0:T(8,128)(2,1)S(1)} %collective-permute-done.4.refs_2_), channel_id=1, source_target_pairs={{4,0},{0,4},{12,8},{8,12},{20,16},{16,20},{28,24},{24,28},{36,32},... | collective-permute-start | bytes 786440 | tf_op jit(solution)/shard_map/ppermute | solution.py:48
  24.6 2.1 %collective-permute-start.9 = (bf16[4,8,4096]{2,1,0:T(8,128)(2,1)S(1)}, bf16[4,8,4096]{2,1,0:T(8,128)(2,1)S(1)}, u32[]{:S(2)}, u32[]{:S(2)}) collective-permute-start(bf16[4,8,4096]{2,1,0:T(8,128)(2,1)S(1)} %collective-permute-done.5.refs_3_), channel_id=1, source_target_pairs={{4,0},{0,4},{12,8},{8,12},{20,16},{16,20},{28,24},{24,28},{36,32},... | collective-permute-start | bytes 786440 | tf_op jit(solution)/shard_map/ppermute | solution.py:48
  54.9 50.8 %copy-start.1 = (bf16[4096,512]{1,0:T(8,128)(2,1)S(1)}, bf16[4096,512]{1,0:T(8,128)(2,1)}, u32[]{:S(2)}) copy-start(bf16[4096,512]{1,0:T(8,128)(2,1)} %refs_8_.1) | copy-start | bytes 12582916
  54.9 3.1 %collective-permute-start.10 = (bf16[16,16,2176]{2,1,0:T(8,128)(2,1)S(1)}, bf16[16,16,2176]{2,1,0:T(8,128)(2,1)S(1)}, u32[]{:S(2)}, u32[]{:S(2)}) collective-permute-start(bf16[16,16,2176]{2,1,0:T(8,128)(2,1)S(1)} %get-tuple-element.36), channel_id=1, source_target_pairs={{4,0},{0,4},{12,8},{8,12},{20,16},{16,20},{28,24},{24,28},{36,32},... | collective-permute-start | bytes 3342344 | tf_op jit(solution)/shard_map/ppermute | solution.py:48
  59.6 11.6 %collective-permute-start.11 = (bf16[4,16,2176]{2,1,0:T(8,128)(2,1)S(1)}, bf16[4,16,2176]{2,1,0:T(8,128)(2,1)S(1)}, u32[]{:S(2)}, u32[]{:S(2)}) collective-permute-start(bf16[4,16,2176]{2,1,0:T(8,128)(2,1)S(1)} %get-tuple-element.38), channel_id=1, source_target_pairs={{32,0},{12,4},{40,8},{20,12},{48,16},{28,20},{56,24},{4,28},{64,32... | collective-permute-start | bytes 835592 | tf_op jit(solution)/shard_map/ppermute | solution.py:44
  60.8 13.6 %collective-permute-start.12 = (bf16[4,16,2176]{2,1,0:T(8,128)(2,1)S(1)}, bf16[4,16,2176]{2,1,0:T(8,128)(2,1)S(1)}, u32[]{:S(2)}, u32[]{:S(2)}) collective-permute-start(bf16[4,16,2176]{2,1,0:T(8,128)(2,1)S(1)} %get-tuple-element.39), channel_id=1, source_target_pairs={{64,0},{20,4},{72,8},{28,12},{80,16},{4,20},{88,24},{12,28},{96,32... | collective-permute-start | bytes 835592 | tf_op jit(solution)/shard_map/ppermute | solution.py:44
  69.9 7.8 %collective-permute-start.13 = (bf16[4,16,2176]{2,1,0:T(8,128)(2,1)S(1)}, bf16[4,16,2176]{2,1,0:T(8,128)(2,1)S(1)}, u32[]{:S(2)}, u32[]{:S(2)}) collective-permute-start(bf16[4,16,2176]{2,1,0:T(8,128)(2,1)S(1)} %get-tuple-element.40), channel_id=1, source_target_pairs={{96,0},{28,4},{104,8},{4,12},{112,16},{12,20},{120,24},{20,28},{0,... | collective-permute-start | bytes 835592 | tf_op jit(solution)/shard_map/ppermute | solution.py:44
  78.3 9.6 %collective-permute-start.14 = (bf16[4,16,2176]{2,1,0:T(8,128)(2,1)S(1)}, bf16[4,16,2176]{2,1,0:T(8,128)(2,1)S(1)}, u32[]{:S(2)}, u32[]{:S(2)}) collective-permute-start(bf16[4,16,2176]{2,1,0:T(8,128)(2,1)S(1)} %merge_four.1.refs_0_), channel_id=1, source_target_pairs={{8,0},{36,4},{16,8},{44,12},{24,16},{52,20},{0,24},{60,28},{40,32}... | collective-permute-start | bytes 835592 | tf_op jit(solution)/shard_map/ppermute | solution.py:39
  80.8 8.2 %collective-permute-start.15 = (bf16[4,16,2176]{2,1,0:T(8,128)(2,1)S(1)}, bf16[4,16,2176]{2,1,0:T(8,128)(2,1)S(1)}, u32[]{:S(2)}, u32[]{:S(2)}) collective-permute-start(bf16[4,16,2176]{2,1,0:T(8,128)(2,1)S(1)} %merge_four.1.refs_0_), channel_id=1, source_target_pairs={{16,0},{68,4},{24,8},{76,12},{0,16},{84,20},{8,24},{92,28},{48,32}... | collective-permute-start | bytes 835592 | tf_op jit(solution)/shard_map/ppermute | solution.py:39
  82.4 9.5 %collective-permute-start.16 = (bf16[4,16,2176]{2,1,0:T(8,128)(2,1)S(1)}, bf16[4,16,2176]{2,1,0:T(8,128)(2,1)S(1)}, u32[]{:S(2)}, u32[]{:S(2)}) collective-permute-start(bf16[4,16,2176]{2,1,0:T(8,128)(2,1)S(1)} %merge_four.1.refs_0_), channel_id=1, source_target_pairs={{24,0},{100,4},{0,8},{108,12},{8,16},{116,20},{16,24},{124,28},{56... | collective-permute-start | bytes 835592 | tf_op jit(solution)/shard_map/ppermute | solution.py:39
  92.6 6.4 %collective-permute-start.17 = (bf16[4,16,2048]{2,1,0:T(8,128)(2,1)S(1)}, bf16[4,16,2048]{2,1,0:T(8,128)(2,1)S(1)}, u32[]{:S(2)}, u32[]{:S(2)}) collective-permute-start(bf16[4,16,2048]{2,1,0:T(8,128)(2,1)S(1)} %merge_final.1.refs_0_), channel_id=1, source_target_pairs={{32,0},{12,4},{40,8},{20,12},{48,16},{28,20},{56,24},{4,28},{64,32... | collective-permute-start | bytes 786440 | tf_op jit(solution)/shard_map/ppermute | solution.py:44
  93.1 7.9 %collective-permute-start.18 = (bf16[4,16,2048]{2,1,0:T(8,128)(2,1)S(1)}, bf16[4,16,2048]{2,1,0:T(8,128)(2,1)S(1)}, u32[]{:S(2)}, u32[]{:S(2)}) collective-permute-start(bf16[4,16,2048]{2,1,0:T(8,128)(2,1)S(1)} %merge_final.1.refs_0_), channel_id=1, source_target_pairs={{64,0},{20,4},{72,8},{28,12},{80,16},{4,20},{88,24},{12,28},{96,32... | collective-permute-start | bytes 786440 | tf_op jit(solution)/shard_map/ppermute | solution.py:44
  96.5 7.6 %collective-permute-start.19 = (bf16[4,16,2048]{2,1,0:T(8,128)(2,1)S(1)}, bf16[4,16,2048]{2,1,0:T(8,128)(2,1)S(1)}, u32[]{:S(2)}, u32[]{:S(2)}) collective-permute-start(bf16[4,16,2048]{2,1,0:T(8,128)(2,1)S(1)} %merge_final.1.refs_0_), channel_id=1, source_target_pairs={{96,0},{28,4},{104,8},{4,12},{112,16},{12,20},{120,24},{20,28},{0,... | collective-permute-start | bytes 786440 | tf_op jit(solution)/shard_map/ppermute | solution.py:44
  96.5 7.6 %collective-permute-start.20 = (bf16[4,16,2048]{2,1,0:T(8,128)(2,1)S(1)}, bf16[4,16,2048]{2,1,0:T(8,128)(2,1)S(1)}, u32[]{:S(2)}, u32[]{:S(2)}) collective-permute-start(bf16[4,16,2048]{2,1,0:T(8,128)(2,1)S(1)} %merge_final.1.refs_0_), channel_id=1, source_target_pairs={{4,0},{0,4},{12,8},{8,12},{20,16},{16,20},{28,24},{24,28},{36,32},... | collective-permute-start | bytes 786440 | tf_op jit(solution)/shard_map/ppermute | solution.py:48
  99.0 5.1 %collective-permute-start.21 = (bf16[4,16,2048]{2,1,0:T(8,128)(2,1)S(1)}, bf16[4,16,2048]{2,1,0:T(8,128)(2,1)S(1)}, u32[]{:S(2)}, u32[]{:S(2)}) collective-permute-start(bf16[4,16,2048]{2,1,0:T(8,128)(2,1)S(1)} %collective-permute-done.17.refs_1_), channel_id=1, source_target_pairs={{4,0},{0,4},{12,8},{8,12},{20,16},{16,20},{28,24},{24,28},{36,32},... | collective-permute-start | bytes 786440 | tf_op jit(solution)/shard_map/ppermute | solution.py:48
  101.0 3.1 %collective-permute-start.22 = (bf16[4,16,2048]{2,1,0:T(8,128)(2,1)S(1)}, bf16[4,16,2048]{2,1,0:T(8,128)(2,1)S(1)}, u32[]{:S(2)}, u32[]{:S(2)}) collective-permute-start(bf16[4,16,2048]{2,1,0:T(8,128)(2,1)S(1)} %collective-permute-done.18.refs_2_), channel_id=1, source_target_pairs={{4,0},{0,4},{12,8},{8,12},{20,16},{16,20},{28,24},{24,28},{36,32},... | collective-permute-start | bytes 786440 | tf_op jit(solution)/shard_map/ppermute | solution.py:48
  104.1 1.5 %collective-permute-start.23 = (bf16[4,16,2048]{2,1,0:T(8,128)(2,1)S(1)}, bf16[4,16,2048]{2,1,0:T(8,128)(2,1)S(1)}, u32[]{:S(2)}, u32[]{:S(2)}) collective-permute-start(bf16[4,16,2048]{2,1,0:T(8,128)(2,1)S(1)} %collective-permute-done.19.refs_3_), channel_id=1, source_target_pairs={{4,0},{0,4},{12,8},{8,12},{20,16},{16,20},{28,24},{24,28},{36,32},... | collective-permute-start | bytes 786440 | tf_op jit(solution)/shard_map/ppermute | solution.py:48
  107.8 5.9 %collective-permute-start.24 = (bf16[64,512]{1,0:T(8,128)(2,1)S(1)}, bf16[64,512]{1,0:T(8,128)(2,1)S(1)}, u32[]{:S(2)}, u32[]{:S(2)}) collective-permute-start(bf16[64,512]{1,0:T(8,128)(2,1)S(1)} %get-tuple-element.42), channel_id=1, source_target_pairs={{3,0},{0,1},{1,2},{2,3},{7,4},{4,5},{5,6},{6,7},{11,8},{8,9},{9,10... | collective-permute-start | bytes 196616 | tf_op jit(solution)/shard_map/ppermute | solution.py:52
  109.4 6.4 %collective-permute-start.25 = (bf16[64,512]{1,0:T(8,128)(2,1)S(1)}, bf16[64,512]{1,0:T(8,128)(2,1)S(1)}, u32[]{:S(2)}, u32[]{:S(2)}) collective-permute-start(bf16[64,512]{1,0:T(8,128)(2,1)S(1)} %get-tuple-element.43), channel_id=1, source_target_pairs={{2,0},{3,1},{0,2},{1,3},{6,4},{7,5},{4,6},{5,7},{10,8},{11,9},{8,1... | collective-permute-start | bytes 196616 | tf_op jit(solution)/shard_map/ppermute | solution.py:52
  112.3 4.3 %collective-permute-start.26 = (bf16[64,512]{1,0:T(8,128)(2,1)S(1)}, bf16[64,512]{1,0:T(8,128)(2,1)S(1)}, u32[]{:S(2)}, u32[]{:S(2)}) collective-permute-start(bf16[64,512]{1,0:T(8,128)(2,1)S(1)} %get-tuple-element.44), channel_id=1, source_target_pairs={{1,0},{2,1},{3,2},{0,3},{5,4},{6,5},{7,6},{4,7},{9,8},{10,9},{11,1... | collective-permute-start | bytes 196616 | tf_op jit(solution)/shard_map/ppermute | solution.py:52

commit v5 on v4

--- a/solution.py
+++ b/solution.py
@@ -228,38 +228,35 @@
         put_partial(out, 2 * r + half, top, *sum_up(w, keys[side, r, head, :, HD:]))
 
     full = jnp.logical_and(first >= slot, second >= slot)
-
-    @pl.when(full)
-    def _():
-        s = scores(*where[0])
+    empty = jnp.logical_and(first <= 0, second <= 0)
+
+    def run(biases):
+        def masked(block):
+            s = scores(*block)
+            return s if biases is None else s + biases[block[0]]
+
+        s = masked(where[0])
         for i, block in enumerate(where):
-            later = scores(*where[i + 1]) if i + 1 < len(where) else None
+            later = masked(where[i + 1]) if i + 1 < len(where) else None
             finish(*block, s)
             s = later
 
-    @pl.when(jnp.logical_not(full))
-    def _():
-        @pl.loop(0, 2)
-        def _(r):
-            count = valid[2 * step + r]
-
-            @pl.when(count > 0)
-            def _():
-                for head, out in ((1 - core, sent), (core, mine)):
-
-                    @pl.loop(0, 2)
-                    def _(half, head=head, out=out):
-                        s = scores(r, head, out, half)
-                        position = lax.broadcasted_iota(jnp.int32, s.shape, 1)
-                        finish(r, head, out, half, jnp.where(position < count, s, EMPTY))
-
-            @pl.when(count <= 0)
-            def _():
-                none = pack_stats(jnp.full((ROWS, GROUP), EMPTY, F32), jnp.zeros((ROWS, GROUP), F32))
-                for out in (sent, mine):
-                    for half in range(2):
-                        out[2 * r + half, :, :FEATS] = jnp.zeros((ROWS, FEATS), BF16)
-                        out[2 * r + half, :, FEATS:] = none
+    @pl.when(full)
+    def _():
+        run(None)
+
+    @pl.when(jnp.logical_not(jnp.logical_or(full, empty)))
+    def _():
+        position = lax.broadcasted_iota(jnp.int32, (1, slot), 1)
+        run([jnp.where(position < count, 0.0, EMPTY) for count in (first, second)])
+
+    @pl.when(empty)
+    def _():
+        none = pack_stats(jnp.full((ROWS, GROUP), EMPTY, F32), jnp.zeros((ROWS, GROUP), F32))
+        for out in (sent, mine):
+            for i in range(out.shape[0]):
+                out[i, :, :FEATS] = jnp.zeros((ROWS, FEATS), BF16)
+                out[i, :, FEATS:] = none
 
     z, x = info[0], info[1]
 

time: 117 us -> 110 us (0.940)
  starting transfers between devices: 36.9 us -> 27.5 us
  waiting for transfers between devices: 34.1 us -> 35.8 us
    ppermute x9, starting transfers between devices: 20.9 us -> 12.7 us  [from_second(): return lax.ppermute(value, 'ctx', pairs)]
    ppermute x9, waiting for transfers between devices: 15.1 us -> 16.5 us  [from_second(): return lax.ppermute(value, 'ctx', pairs)]
  transfers between devices with their start and end apart: 27 -> 27, of which waited for: 19 -> 20; matrix products, arithmetic and copies ran while one was open for 0% -> 0% of each run, Pallas kernels for 10% -> 11%
where the time goes in v5:
time: 110 us
  Pallas kernels  45.7 us (42%)
  waiting for transfers between devices  35.8 us (33%)
  starting transfers between devices  27.5 us (25%)
    pallas_call x1, Pallas kernels, attend(): pl.pallas_call(attend_kernel, out_shape=[blocks, blocks], grid_spec=pltpu...  28.5 us
    ppermute x9, waiting for transfers between devices, from_second(): return lax.ppermute(value, 'ctx', pairs)  16.5 us
    ppermute x9, starting transfers between devices, from_second(): return lax.ppermute(value, 'ctx', pairs)  12.7 us
    pallas_call x2, Pallas kernels, split_ahead(): pl.pallas_call(ahead_kernel, grid=(count,), in_specs=[pl.BlockSpec((1, pe...  12 us
    ppermute x6, waiting for transfers between devices, from_first(): return lax.ppermute(value, 'ctx', pairs)  10.6 us
    ppermute x6, starting transfers between devices, from_first(): return lax.ppermute(value, 'ctx', pairs)  7.62 us
    ppermute x3, starting transfers between devices, from_plane(): lax.ppermute(value, 'kvh', [((s + step) % SIDE, s) for s in range(SIDE)])  5.9 us
    ppermute x9, waiting for transfers between devices, from_twin(): lax.ppermute(value, 'ctx', [(at(z, x, 1 - c), at(z, x, c)) for z, x, c in...  5.77 us
  transfers between devices with their start and end apart: 27, of which 20 were waited for; matrix products, arithmetic and copies ran while one was open for 0% of the time, Pallas kernels for 11%

profile of v5, /device:TPU:0, one launch (start us, length us, event | category | flops | bytes accessed | tf_op | source)
XLA Modules:
  0.0 109.9 jit_solution(15278172347906158097)
XLA Ops:
  0.0 2.8 %collective-permute-start = (bf16[8,4096]{1,0:T(8,128)(2,1)}, bf16[8,4096]{1,0:T(8,128)(2,1)S(1)}, u32[]{:S(2)}, u32[]{:S(2)}) collective-permute-start(bf16[8,4096]{1,0:T(8,128)(2,1)} %refs_0_.1), channel_id=1, source_target_pairs={{8,0},{36,4},{16,8},{44,12},{24,16},{52,20},{0,24},{60,28},{40,32}... | collective-permute-start | bytes 196616 | tf_op jit(solution)/shard_map/ppermute | solution.py:39
  2.8 0.8 collective-permute-start.1
  3.6 0.9 collective-permute-start.2
  4.6 4.0 %split_ahead.2.refs_0_ = bf16[4,2,2048,256]{3,2,1,0:T(8,128)(2,1)} custom-call(bf16[8,2048,2,256]{3,2,1,0:T(2,128)(2,1)} %refs_9_.1), custom_call_target="tpu_custom_call" | custom-call | bytes 8388608 | tf_op jit(solution)/shard_map/split_ahead/pallas_call | solution.py:161
  9.6 4.1 %collective-permute-start.3 = (bf16[4,8,4096]{2,1,0:T(8,128)(2,1)S(1)}, bf16[4,8,4096]{2,1,0:T(8,128)(2,1)S(1)}, u32[]{:S(2)}, u32[]{:S(2)}) collective-permute-start(bf16[4,8,4096]{2,1,0:T(8,128)(2,1)S(1)} %stack.21.refs_0_), channel_id=1, source_target_pairs={{32,0},{12,4},{40,8},{20,12},{48,16},{28,20},{56,24},{4,28},{64,32... | collective-permute-start | bytes 786440 | tf_op jit(solution)/shard_map/ppermute | solution.py:44
  13.7 1.3 %collective-permute-start.5 = (bf16[4,8,4096]{2,1,0:T(8,128)(2,1)S(1)}, bf16[4,8,4096]{2,1,0:T(8,128)(2,1)S(1)}, u32[]{:S(2)}, u32[]{:S(2)}) collective-permute-start(bf16[4,8,4096]{2,1,0:T(8,128)(2,1)S(1)} %stack.21.refs_0_), channel_id=1, source_target_pairs={{96,0},{28,4},{104,8},{4,12},{112,16},{12,20},{120,24},{20,28},{0,... | collective-permute-start | bytes 786440 | tf_op jit(solution)/shard_map/ppermute | solution.py:44
  14.9 8.1 %split_ahead.3.refs_8_ = bf16[4,2,2048,256]{3,2,1,0:T(8,128)(2,1)} custom-call(bf16[8,2048,2,256]{3,2,1,0:T(2,128)(2,1)} %refs_9_.1, bf16[4,2,2048,256]{3,2,1,0:T(8,128)(2,1)} %split_ahead.2.refs_0_), custom_call_target="tpu_custom_call", output_to_operand_aliasing={{}: (1, {})} | custom-call | bytes 25165824 | tf_op jit(solution)/shard_map/split_ahead/pallas_call | solution.py:161
  23.0 1.1 collective-permute-done.5.refs_3_
  26.7 28.5 %attend.1 = (bf16[16,16,2176]{2,1,0:T(8,128)(2,1)S(1)}, bf16[16,16,2176]{2,1,0:T(8,128)(2,1)S(1)}) custom-call(s32[4]{0:T(128)S(1)} %pad_add_fusion.info, s32[8]{0:T(128)S(1)} %subtract_clamp_fusion.valid, bf16[4,8,4096]{2,1,0:T(8,128)(2,1)S(1)} %stack.21.refs_0_, bf16[4,8,4096]{2,1,0:T(8,128)(2,1)S(1)} %collective-permute-done.3.refs_1_, ...), custom_call_target="tpu_custom_call" | custom-call | flops 8589934592 | bytes 16777216 | tf_op jit(solution)/shard_map/attend/pallas_call | solution.py:276
  55.5 2.6 %collective-permute-done.10.got = bf16[16,16,2176]{2,1,0:T(8,128)(2,1)S(1)} collective-permute-done((bf16[16,16,2176]{2,1,0:T(8,128)(2,1)S(1)}, bf16[16,16,2176]{2,1,0:T(8,128)(2,1)S(1)}, u32[]{:S(2)}, u32[]{:S(2)}) %collective-permute-start.10) | collective-permute-done | bytes 1114144 | tf_op jit(solution)/shard_map/ppermute | solution.py:48
  58.1 1.7 %merge_twins.1 = (bf16[4,16,2176]{2,1,0:T(8,128)(2,1)S(1)}, bf16[4,16,2176]{2,1,0:T(8,128)(2,1)S(1)}, bf16[4,16,2176]{2,1,0:T(8,128)(2,1)S(1)}, bf16[4,16,2176]{2,1,0:T(8,128)(2,1)S(1)}) custom-call(s32[4]{0:T(128)S(1)} %pad_add_fusion.info, bf16[16,16,2176]{2,1,0:T(8,128)(2,1)S(1)} %get-tuple-element.35.mine, ...), custom_call_target="tpu_custom_call" | custom-call | tf_op jit(solution)/shard_map/merge_twins/pallas_call | solution.py:360
  59.9 3.3 %collective-permute-start.12 = (bf16[4,16,2176]{2,1,0:T(8,128)(2,1)S(1)}, bf16[4,16,2176]{2,1,0:T(8,128)(2,1)S(1)}, u32[]{:S(2)}, u32[]{:S(2)}) collective-permute-start(bf16[4,16,2176]{2,1,0:T(8,128)(2,1)S(1)} %get-tuple-element.39), channel_id=1, source_target_pairs={{64,0},{20,4},{72,8},{28,12},{80,16},{4,20},{88,24},{12,28},{96,32... | collective-permute-start | bytes 835592 | tf_op jit(solution)/shard_map/ppermute | solution.py:44
  63.2 3.2 %collective-permute-done.11.refs_1_ = bf16[4,16,2176]{2,1,0:T(8,128)(2,1)S(1)} collective-permute-done((bf16[4,16,2176]{2,1,0:T(8,128)(2,1)S(1)}, bf16[4,16,2176]{2,1,0:T(8,128)(2,1)S(1)}, u32[]{:S(2)}, u32[]{:S(2)}) %collective-permute-start.11) | collective-permute-done | bytes 278560 | tf_op jit(solution)/shard_map/ppermute | solution.py:44
  66.4 1.6 %collective-permute-done.12.refs_2_ = bf16[4,16,2176]{2,1,0:T(8,128)(2,1)S(1)} collective-permute-done((bf16[4,16,2176]{2,1,0:T(8,128)(2,1)S(1)}, bf16[4,16,2176]{2,1,0:T(8,128)(2,1)S(1)}, u32[]{:S(2)}, u32[]{:S(2)}) %collective-permute-start.12) | collective-permute-done | bytes 278560 | tf_op jit(solution)/shard_map/ppermute | solution.py:44
  68.0 3.0 %collective-permute-done.13.refs_3_ = bf16[4,16,2176]{2,1,0:T(8,128)(2,1)S(1)} collective-permute-done((bf16[4,16,2176]{2,1,0:T(8,128)(2,1)S(1)}, bf16[4,16,2176]{2,1,0:T(8,128)(2,1)S(1)}, u32[]{:S(2)}, u32[]{:S(2)}) %collective-permute-start.13) | collective-permute-done | bytes 278560 | tf_op jit(solution)/shard_map/ppermute | solution.py:44
  71.7 1.8 %collective-permute-start.14 = (bf16[4,16,2176]{2,1,0:T(8,128)(2,1)S(1)}, bf16[4,16,2176]{2,1,0:T(8,128)(2,1)S(1)}, u32[]{:S(2)}, u32[]{:S(2)}) collective-permute-start(bf16[4,16,2176]{2,1,0:T(8,128)(2,1)S(1)} %merge_four.1.refs_0_), channel_id=1, source_target_pairs={{8,0},{36,4},{16,8},{44,12},{24,16},{52,20},{0,24},{60,28},{40,32}... | collective-permute-start | bytes 835592 | tf_op jit(solution)/shard_map/ppermute | solution.py:39
  73.5 1.3 %collective-permute-start.15 = (bf16[4,16,2176]{2,1,0:T(8,128)(2,1)S(1)}, bf16[4,16,2176]{2,1,0:T(8,128)(2,1)S(1)}, u32[]{:S(2)}, u32[]{:S(2)}) collective-permute-start(bf16[4,16,2176]{2,1,0:T(8,128)(2,1)S(1)} %merge_four.1.refs_0_), channel_id=1, source_target_pairs={{16,0},{68,4},{24,8},{76,12},{0,16},{84,20},{8,24},{92,28},{48,32}... | collective-permute-start | bytes 835592 | tf_op jit(solution)/shard_map/ppermute | solution.py:39
  74.8 5.8 %collective-permute-done.14.refs_1_ = bf16[4,16,2176]{2,1,0:T(8,128)(2,1)S(1)} collective-permute-done((bf16[4,16,2176]{2,1,0:T(8,128)(2,1)S(1)}, bf16[4,16,2176]{2,1,0:T(8,128)(2,1)S(1)}, u32[]{:S(2)}, u32[]{:S(2)}) %collective-permute-start.14) | collective-permute-done | bytes 278560 | tf_op jit(solution)/shard_map/ppermute | solution.py:39
  80.6 1.1 collective-permute-done.15.refs_2_
  81.7 2.9 %collective-permute-done.16.refs_3_ = bf16[4,16,2176]{2,1,0:T(8,128)(2,1)S(1)} collective-permute-done((bf16[4,16,2176]{2,1,0:T(8,128)(2,1)S(1)}, bf16[4,16,2176]{2,1,0:T(8,128)(2,1)S(1)}, u32[]{:S(2)}, u32[]{:S(2)}) %collective-permute-start.16) | collective-permute-done | bytes 278560 | tf_op jit(solution)/shard_map/ppermute | solution.py:39
  85.2 0.9 collective-permute-start.17
  86.1 3.1 %collective-permute-start.18 = (bf16[4,16,2048]{2,1,0:T(8,128)(2,1)S(1)}, bf16[4,16,2048]{2,1,0:T(8,128)(2,1)S(1)}, u32[]{:S(2)}, u32[]{:S(2)}) collective-permute-start(bf16[4,16,2048]{2,1,0:T(8,128)(2,1)S(1)} %merge_final.1.refs_0_), channel_id=1, source_target_pairs={{64,0},{20,4},{72,8},{28,12},{80,16},{4,20},{88,24},{12,28},{96,32... | collective-permute-start | bytes 786440 | tf_op jit(solution)/shard_map/ppermute | solution.py:44
  89.2 2.5 %collective-permute-done.17.refs_1_ = bf16[4,16,2048]{2,1,0:T(8,128)(2,1)S(1)} collective-permute-done((bf16[4,16,2048]{2,1,0:T(8,128)(2,1)S(1)}, bf16[4,16,2048]{2,1,0:T(8,128)(2,1)S(1)}, u32[]{:S(2)}, u32[]{:S(2)}) %collective-permute-start.17) | collective-permute-done | bytes 262176 | tf_op jit(solution)/shard_map/ppermute | solution.py:44
  91.7 2.3 %collective-permute-done.18.refs_2_ = bf16[4,16,2048]{2,1,0:T(8,128)(2,1)S(1)} collective-permute-done((bf16[4,16,2048]{2,1,0:T(8,128)(2,1)S(1)}, bf16[4,16,2048]{2,1,0:T(8,128)(2,1)S(1)}, u32[]{:S(2)}, u32[]{:S(2)}) %collective-permute-start.18) | collective-permute-done | bytes 262176 | tf_op jit(solution)/shard_map/ppermute | solution.py:44
  94.0 2.8 %collective-permute-done.19.refs_3_ = bf16[4,16,2048]{2,1,0:T(8,128)(2,1)S(1)} collective-permute-done((bf16[4,16,2048]{2,1,0:T(8,128)(2,1)S(1)}, bf16[4,16,2048]{2,1,0:T(8,128)(2,1)S(1)}, u32[]{:S(2)}, u32[]{:S(2)}) %collective-permute-start.19) | collective-permute-done | bytes 262176 | tf_op jit(solution)/shard_map/ppermute | solution.py:44
  96.9 1.5 %collective-permute-done.23.refs_7_ = bf16[4,16,2048]{2,1,0:T(8,128)(2,1)S(1)} collective-permute-done((bf16[4,16,2048]{2,1,0:T(8,128)(2,1)S(1)}, bf16[4,16,2048]{2,1,0:T(8,128)(2,1)S(1)}, u32[]{:S(2)}, u32[]{:S(2)}) %collective-permute-start.23) | collective-permute-done | bytes 262176 | tf_op jit(solution)/shard_map/ppermute | solution.py:48
  98.4 2.1 %project.1 = (f32[64,512]{1,0:T(8,128)S(1)}, bf16[64,512]{1,0:T(8,128)(2,1)S(1)}, bf16[64,512]{1,0:T(8,128)(2,1)S(1)}, bf16[64,512]{1,0:T(8,128)(2,1)S(1)}) custom-call(s32[4]{0:T(128)S(1)} %pad_add_fusion.info, bf16[4,16,2048]{2,1,0:T(8,128)(2,1)S(1)} %merge_final.1.refs_0_, bf16[4,16,2048]{2,1,0:T(8,128)(2,1)S(1)} %collective-permute-done.17.refs_1_, ...), custom_call_target="tpu_custom_call" | custom-call | flops 1073741824 | bytes 4194304 | tf_op jit(solution)/shard_map/project/pallas_call | solution.py:444
  100.5 1.6 %collective-permute-start.24 = (bf16[64,512]{1,0:T(8,128)(2,1)S(1)}, bf16[64,512]{1,0:T(8,128)(2,1)S(1)}, u32[]{:S(2)}, u32[]{:S(2)}) collective-permute-start(bf16[64,512]{1,0:T(8,128)(2,1)S(1)} %get-tuple-element.42), channel_id=1, source_target_pairs={{3,0},{0,1},{1,2},{2,3},{7,4},{4,5},{5,6},{6,7},{11,8},{8,9},{9,10... | collective-permute-start | bytes 196616 | tf_op jit(solution)/shard_map/ppermute | solution.py:52
  102.1 2.9 %collective-permute-start.25 = (bf16[64,512]{1,0:T(8,128)(2,1)S(1)}, bf16[64,512]{1,0:T(8,128)(2,1)S(1)}, u32[]{:S(2)}, u32[]{:S(2)}) collective-permute-start(bf16[64,512]{1,0:T(8,128)(2,1)S(1)} %get-tuple-element.43), channel_id=1, source_target_pairs={{2,0},{3,1},{0,2},{1,3},{6,4},{7,5},{4,6},{5,7},{10,8},{11,9},{8,1... | collective-permute-start | bytes 196616 | tf_op jit(solution)/shard_map/ppermute | solution.py:52
  105.0 1.3 %collective-permute-start.26 = (bf16[64,512]{1,0:T(8,128)(2,1)S(1)}, bf16[64,512]{1,0:T(8,128)(2,1)S(1)}, u32[]{:S(2)}, u32[]{:S(2)}) collective-permute-start(bf16[64,512]{1,0:T(8,128)(2,1)S(1)} %get-tuple-element.44), channel_id=1, source_target_pairs={{1,0},{2,1},{3,2},{0,3},{5,4},{6,5},{7,6},{4,7},{9,8},{10,9},{11,1... | collective-permute-start | bytes 196616 | tf_op jit(solution)/shard_map/ppermute | solution.py:52
  106.4 2.2 %collective-permute-done.25 = bf16[64,512]{1,0:T(8,128)(2,1)S(1)} collective-permute-done((bf16[64,512]{1,0:T(8,128)(2,1)S(1)}, bf16[64,512]{1,0:T(8,128)(2,1)S(1)}, u32[]{:S(2)}, u32[]{:S(2)}) %collective-permute-start.25) | collective-permute-done | bytes 65568 | tf_op jit(solution)/shard_map/ppermute | solution.py:52
  108.5 0.8 collective-permute-done.26
  (43 shorter events, 6.1 us)
Async XLA Ops:
  0.0 4.5 %copy-start = (bf16[8,32,2,256]{3,2,1,0:T(2,128)(2,1)S(1)}, bf16[8,32,2,256]{3,2,1,0:T(2,128)(2,1)}, u32[]{:S(2)}) copy-start(bf16[8,32,2,256]{3,2,1,0:T(2,128)(2,1)} %param.7) | copy-start | bytes 786436
  0.0 8.7 %collective-permute-start = (bf16[8,4096]{1,0:T(8,128)(2,1)}, bf16[8,4096]{1,0:T(8,128)(2,1)S(1)}, u32[]{:S(2)}, u32[]{:S(2)}) collective-permute-start(bf16[8,4096]{1,0:T(8,128)(2,1)} %refs_0_.1), channel_id=1, source_target_pairs={{8,0},{36,4},{16,8},{44,12},{24,16},{52,20},{0,24},{60,28},{40,32}... | collective-permute-start | bytes 196616 | tf_op jit(solution)/shard_map/ppermute | solution.py:39
  2.8 6.0 %collective-permute-start.1 = (bf16[8,4096]{1,0:T(8,128)(2,1)}, bf16[8,4096]{1,0:T(8,128)(2,1)S(1)}, u32[]{:S(2)}, u32[]{:S(2)}) collective-permute-start(bf16[8,4096]{1,0:T(8,128)(2,1)} %refs_0_.1), channel_id=1, source_target_pairs={{16,0},{68,4},{24,8},{76,12},{0,16},{84,20},{8,24},{92,28},{48,32}... | collective-permute-start | bytes 196616 | tf_op jit(solution)/shard_map/ppermute | solution.py:39
  3.6 5.9 %collective-permute-start.2 = (bf16[8,4096]{1,0:T(8,128)(2,1)}, bf16[8,4096]{1,0:T(8,128)(2,1)S(1)}, u32[]{:S(2)}, u32[]{:S(2)}) collective-permute-start(bf16[8,4096]{1,0:T(8,128)(2,1)} %refs_0_.1), channel_id=1, source_target_pairs={{24,0},{100,4},{0,8},{108,12},{8,16},{116,20},{16,24},{124,28},{56... | collective-permute-start | bytes 196616 | tf_op jit(solution)/shard_map/ppermute | solution.py:39
  4.6 4.0 %copy-start.3 = (s32[8]{0:T(128)S(1)}, s32[8]{0:T(128)}, u32[]{:S(2)}) copy-start(s32[8]{0:T(128)} %param.8) | copy-start | bytes 100
  4.6 4.9 %copy-start.2 = (bf16[8,4096]{1,0:T(8,128)(2,1)S(1)}, bf16[8,4096]{1,0:T(8,128)(2,1)}, u32[]{:S(2)}) copy-start(bf16[8,4096]{1,0:T(8,128)(2,1)} %refs_0_.1) | copy-start | bytes 196612
  9.6 13.4 %collective-permute-start.3 = (bf16[4,8,4096]{2,1,0:T(8,128)(2,1)S(1)}, bf16[4,8,4096]{2,1,0:T(8,128)(2,1)S(1)}, u32[]{:S(2)}, u32[]{:S(2)}) collective-permute-start(bf16[4,8,4096]{2,1,0:T(8,128)(2,1)S(1)} %stack.21.refs_0_), channel_id=1, source_target_pairs={{32,0},{12,4},{40,8},{20,12},{48,16},{28,20},{56,24},{4,28},{64,32... | collective-permute-start | bytes 786440 | tf_op jit(solution)/shard_map/ppermute | solution.py:44
  13.7 9.3 %collective-permute-start.4 = (bf16[4,8,4096]{2,1,0:T(8,128)(2,1)S(1)}, bf16[4,8,4096]{2,1,0:T(8,128)(2,1)S(1)}, u32[]{:S(2)}, u32[]{:S(2)}) collective-permute-start(bf16[4,8,4096]{2,1,0:T(8,128)(2,1)S(1)} %stack.21.refs_0_), channel_id=1, source_target_pairs={{64,0},{20,4},{72,8},{28,12},{80,16},{4,20},{88,24},{12,28},{96,32... | collective-permute-start | bytes 786440 | tf_op jit(solution)/shard_map/ppermute | solution.py:44
  13.7 10.4 %collective-permute-start.5 = (bf16[4,8,4096]{2,1,0:T(8,128)(2,1)S(1)}, bf16[4,8,4096]{2,1,0:T(8,128)(2,1)S(1)}, u32[]{:S(2)}, u32[]{:S(2)}) collective-permute-start(bf16[4,8,4096]{2,1,0:T(8,128)(2,1)S(1)} %stack.21.refs_0_), channel_id=1, source_target_pairs={{96,0},{28,4},{104,8},{4,12},{112,16},{12,20},{120,24},{20,28},{0,... | collective-permute-start | bytes 786440 | tf_op jit(solution)/shard_map/ppermute | solution.py:44
  24.1 1.5 %collective-permute-start.6 = (bf16[4,8,4096]{2,1,0:T(8,128)(2,1)S(1)}, bf16[4,8,4096]{2,1,0:T(8,128)(2,1)S(1)}, u32[]{:S(2)}, u32[]{:S(2)}) collective-permute-start(bf16[4,8,4096]{2,1,0:T(8,128)(2,1)S(1)} %stack.21.refs_0_), channel_id=1, source_target_pairs={{4,0},{0,4},{12,8},{8,12},{20,16},{16,20},{28,24},{24,28},{36,32},... | collective-permute-start | bytes 786440 | tf_op jit(solution)/shard_map/ppermute | solution.py:48
  24.1 1.9 %collective-permute-start.7 = (bf16[4,8,4096]{2,1,0:T(8,128)(2,1)S(1)}, bf16[4,8,4096]{2,1,0:T(8,128)(2,1)S(1)}, u32[]{:S(2)}, u32[]{:S(2)}) collective-permute-start(bf16[4,8,4096]{2,1,0:T(8,128)(2,1)S(1)} %collective-permute-done.3.refs_1_), channel_id=1, source_target_pairs={{4,0},{0,4},{12,8},{8,12},{20,16},{16,20},{28,24},{24,28},{36,32},... | collective-permute-start | bytes 786440 | tf_op jit(solution)/shard_map/ppermute | solution.py:48
  24.6 1.8 %collective-permute-start.8 = (bf16[4,8,4096]{2,1,0:T(8,128)(2,1)S(1)}, bf16[4,8,4096]{2,1,0:T(8,128)(2,1)S(1)}, u32[]{:S(2)}, u32[]{:S(2)}) collective-permute-start(bf16[4,8,4096]{2,1,0:T(8,128)(2,1)S(1)} %collective-permute-done.4.refs_2_), channel_id=1, source_target_pairs={{4,0},{0,4},{12,8},{8,12},{20,16},{16,20},{28,24},{24,28},{36,32},... | collective-permute-start | bytes 786440 | tf_op jit(solution)/shard_map/ppermute | solution.py:48
  24.6 2.1 %collective-permute-start.9 = (bf16[4,8,4096]{2,1,0:T(8,128)(2,1)S(1)}, bf16[4,8,4096]{2,1,0:T(8,128)(2,1)S(1)}, u32[]{:S(2)}, u32[]{:S(2)}) collective-permute-start(bf16[4,8,4096]{2,1,0:T(8,128)(2,1)S(1)} %collective-permute-done.5.refs_3_), channel_id=1, source_target_pairs={{4,0},{0,4},{12,8},{8,12},{20,16},{16,20},{28,24},{24,28},{36,32},... | collective-permute-start | bytes 786440 | tf_op jit(solution)/shard_map/ppermute | solution.py:48
  55.2 43.1 %copy-start.1 = (bf16[4096,512]{1,0:T(8,128)(2,1)S(1)}, bf16[4096,512]{1,0:T(8,128)(2,1)}, u32[]{:S(2)}) copy-start(bf16[4096,512]{1,0:T(8,128)(2,1)} %refs_8_.1) | copy-start | bytes 12582916
  55.3 2.8 %collective-permute-start.10 = (bf16[16,16,2176]{2,1,0:T(8,128)(2,1)S(1)}, bf16[16,16,2176]{2,1,0:T(8,128)(2,1)S(1)}, u32[]{:S(2)}, u32[]{:S(2)}) collective-permute-start(bf16[16,16,2176]{2,1,0:T(8,128)(2,1)S(1)} %get-tuple-element.36), channel_id=1, source_target_pairs={{4,0},{0,4},{12,8},{8,12},{20,16},{16,20},{28,24},{24,28},{36,32},... | collective-permute-start | bytes 3342344 | tf_op jit(solution)/shard_map/ppermute | solution.py:48
  59.8 6.6 %collective-permute-start.11 = (bf16[4,16,2176]{2,1,0:T(8,128)(2,1)S(1)}, bf16[4,16,2176]{2,1,0:T(8,128)(2,1)S(1)}, u32[]{:S(2)}, u32[]{:S(2)}) collective-permute-start(bf16[4,16,2176]{2,1,0:T(8,128)(2,1)S(1)} %get-tuple-element.38), channel_id=1, source_target_pairs={{32,0},{12,4},{40,8},{20,12},{48,16},{28,20},{56,24},{4,28},{64,32... | collective-permute-start | bytes 835592 | tf_op jit(solution)/shard_map/ppermute | solution.py:44
  59.9 8.1 %collective-permute-start.12 = (bf16[4,16,2176]{2,1,0:T(8,128)(2,1)S(1)}, bf16[4,16,2176]{2,1,0:T(8,128)(2,1)S(1)}, u32[]{:S(2)}, u32[]{:S(2)}) collective-permute-start(bf16[4,16,2176]{2,1,0:T(8,128)(2,1)S(1)} %get-tuple-element.39), channel_id=1, source_target_pairs={{64,0},{20,4},{72,8},{28,12},{80,16},{4,20},{88,24},{12,28},{96,32... | collective-permute-start | bytes 835592 | tf_op jit(solution)/shard_map/ppermute | solution.py:44
  63.2 7.8 %collective-permute-start.13 = (bf16[4,16,2176]{2,1,0:T(8,128)(2,1)S(1)}, bf16[4,16,2176]{2,1,0:T(8,128)(2,1)S(1)}, u32[]{:S(2)}, u32[]{:S(2)}) collective-permute-start(bf16[4,16,2176]{2,1,0:T(8,128)(2,1)S(1)} %get-tuple-element.40), channel_id=1, source_target_pairs={{96,0},{28,4},{104,8},{4,12},{112,16},{12,20},{120,24},{20,28},{0,... | collective-permute-start | bytes 835592 | tf_op jit(solution)/shard_map/ppermute | solution.py:44
  71.7 8.9 %collective-permute-start.14 = (bf16[4,16,2176]{2,1,0:T(8,128)(2,1)S(1)}, bf16[4,16,2176]{2,1,0:T(8,128)(2,1)S(1)}, u32[]{:S(2)}, u32[]{:S(2)}) collective-permute-start(bf16[4,16,2176]{2,1,0:T(8,128)(2,1)S(1)} %merge_four.1.refs_0_), channel_id=1, source_target_pairs={{8,0},{36,4},{16,8},{44,12},{24,16},{52,20},{0,24},{60,28},{40,32}... | collective-permute-start | bytes 835592 | tf_op jit(solution)/shard_map/ppermute | solution.py:39
  73.5 8.2 %collective-permute-start.15 = (bf16[4,16,2176]{2,1,0:T(8,128)(2,1)S(1)}, bf16[4,16,2176]{2,1,0:T(8,128)(2,1)S(1)}, u32[]{:S(2)}, u32[]{:S(2)}) collective-permute-start(bf16[4,16,2176]{2,1,0:T(8,128)(2,1)S(1)} %merge_four.1.refs_0_), channel_id=1, source_target_pairs={{16,0},{68,4},{24,8},{76,12},{0,16},{84,20},{8,24},{92,28},{48,32}... | collective-permute-start | bytes 835592 | tf_op jit(solution)/shard_map/ppermute | solution.py:39
  74.8 9.8 %collective-permute-start.16 = (bf16[4,16,2176]{2,1,0:T(8,128)(2,1)S(1)}, bf16[4,16,2176]{2,1,0:T(8,128)(2,1)S(1)}, u32[]{:S(2)}, u32[]{:S(2)}) collective-permute-start(bf16[4,16,2176]{2,1,0:T(8,128)(2,1)S(1)} %merge_four.1.refs_0_), channel_id=1, source_target_pairs={{24,0},{100,4},{0,8},{108,12},{8,16},{116,20},{16,24},{124,28},{56... | collective-permute-start | bytes 835592 | tf_op jit(solution)/shard_map/ppermute | solution.py:39
  85.2 6.4 %collective-permute-start.17 = (bf16[4,16,2048]{2,1,0:T(8,128)(2,1)S(1)}, bf16[4,16,2048]{2,1,0:T(8,128)(2,1)S(1)}, u32[]{:S(2)}, u32[]{:S(2)}) collective-permute-start(bf16[4,16,2048]{2,1,0:T(8,128)(2,1)S(1)} %merge_final.1.refs_0_), channel_id=1, source_target_pairs={{32,0},{12,4},{40,8},{20,12},{48,16},{28,20},{56,24},{4,28},{64,32... | collective-permute-start | bytes 786440 | tf_op jit(solution)/shard_map/ppermute | solution.py:44
  86.1 7.9 %collective-permute-start.18 = (bf16[4,16,2048]{2,1,0:T(8,128)(2,1)S(1)}, bf16[4,16,2048]{2,1,0:T(8,128)(2,1)S(1)}, u32[]{:S(2)}, u32[]{:S(2)}) collective-permute-start(bf16[4,16,2048]{2,1,0:T(8,128)(2,1)S(1)} %merge_final.1.refs_0_), channel_id=1, source_target_pairs={{64,0},{20,4},{72,8},{28,12},{80,16},{4,20},{88,24},{12,28},{96,32... | collective-permute-start | bytes 786440 | tf_op jit(solution)/shard_map/ppermute | solution.py:44
  89.2 7.6 %collective-permute-start.19 = (bf16[4,16,2048]{2,1,0:T(8,128)(2,1)S(1)}, bf16[4,16,2048]{2,1,0:T(8,128)(2,1)S(1)}, u32[]{:S(2)}, u32[]{:S(2)}) collective-permute-start(bf16[4,16,2048]{2,1,0:T(8,128)(2,1)S(1)} %merge_final.1.refs_0_), channel_id=1, source_target_pairs={{96,0},{28,4},{104,8},{4,12},{112,16},{12,20},{120,24},{20,28},{0,... | collective-permute-start | bytes 786440 | tf_op jit(solution)/shard_map/ppermute | solution.py:44
  89.2 7.6 %collective-permute-start.20 = (bf16[4,16,2048]{2,1,0:T(8,128)(2,1)S(1)}, bf16[4,16,2048]{2,1,0:T(8,128)(2,1)S(1)}, u32[]{:S(2)}, u32[]{:S(2)}) collective-permute-start(bf16[4,16,2048]{2,1,0:T(8,128)(2,1)S(1)} %merge_final.1.refs_0_), channel_id=1, source_target_pairs={{4,0},{0,4},{12,8},{8,12},{20,16},{16,20},{28,24},{24,28},{36,32},... | collective-permute-start | bytes 786440 | tf_op jit(solution)/shard_map/ppermute | solution.py:48
  91.7 5.2 %collective-permute-start.21 = (bf16[4,16,2048]{2,1,0:T(8,128)(2,1)S(1)}, bf16[4,16,2048]{2,1,0:T(8,128)(2,1)S(1)}, u32[]{:S(2)}, u32[]{:S(2)}) collective-permute-start(bf16[4,16,2048]{2,1,0:T(8,128)(2,1)S(1)} %collective-permute-done.17.refs_1_), channel_id=1, source_target_pairs={{4,0},{0,4},{12,8},{8,12},{20,16},{16,20},{28,24},{24,28},{36,32},... | collective-permute-start | bytes 786440 | tf_op jit(solution)/shard_map/ppermute | solution.py:48
  94.0 2.8 %collective-permute-start.22 = (bf16[4,16,2048]{2,1,0:T(8,128)(2,1)S(1)}, bf16[4,16,2048]{2,1,0:T(8,128)(2,1)S(1)}, u32[]{:S(2)}, u32[]{:S(2)}) collective-permute-start(bf16[4,16,2048]{2,1,0:T(8,128)(2,1)S(1)} %collective-permute-done.18.refs_2_), channel_id=1, source_target_pairs={{4,0},{0,4},{12,8},{8,12},{20,16},{16,20},{28,24},{24,28},{36,32},... | collective-permute-start | bytes 786440 | tf_op jit(solution)/shard_map/ppermute | solution.py:48
  96.8 1.5 %collective-permute-start.23 = (bf16[4,16,2048]{2,1,0:T(8,128)(2,1)S(1)}, bf16[4,16,2048]{2,1,0:T(8,128)(2,1)S(1)}, u32[]{:S(2)}, u32[]{:S(2)}) collective-permute-start(bf16[4,16,2048]{2,1,0:T(8,128)(2,1)S(1)} %collective-permute-done.19.refs_3_), channel_id=1, source_target_pairs={{4,0},{0,4},{12,8},{8,12},{20,16},{16,20},{28,24},{24,28},{36,32},... | collective-permute-start | bytes 786440 | tf_op jit(solution)/shard_map/ppermute | solution.py:48
  100.5 5.9 %collective-permute-start.24 = (bf16[64,512]{1,0:T(8,128)(2,1)S(1)}, bf16[64,512]{1,0:T(8,128)(2,1)S(1)}, u32[]{:S(2)}, u32[]{:S(2)}) collective-permute-start(bf16[64,512]{1,0:T(8,128)(2,1)S(1)} %get-tuple-element.42), channel_id=1, source_target_pairs={{3,0},{0,1},{1,2},{2,3},{7,4},{4,5},{5,6},{6,7},{11,8},{8,9},{9,10... | collective-permute-start | bytes 196616 | tf_op jit(solution)/shard_map/ppermute | solution.py:52
  102.1 6.4 %collective-permute-start.25 = (bf16[64,512]{1,0:T(8,128)(2,1)S(1)}, bf16[64,512]{1,0:T(8,128)(2,1)S(1)}, u32[]{:S(2)}, u32[]{:S(2)}) collective-permute-start(bf16[64,512]{1,0:T(8,128)(2,1)S(1)} %get-tuple-element.43), channel_id=1, source_target_pairs={{2,0},{3,1},{0,2},{1,3},{6,4},{7,5},{4,6},{5,7},{10,8},{11,9},{8,1... | collective-permute-start | bytes 196616 | tf_op jit(solution)/shard_map/ppermute | solution.py:52
  105.0 4.3 %collective-permute-start.26 = (bf16[64,512]{1,0:T(8,128)(2,1)S(1)}, bf16[64,512]{1,0:T(8,128)(2,1)S(1)}, u32[]{:S(2)}, u32[]{:S(2)}) collective-permute-start(bf16[64,512]{1,0:T(8,128)(2,1)S(1)} %get-tuple-element.44), channel_id=1, source_target_pairs={{1,0},{2,1},{3,2},{0,3},{5,4},{6,5},{7,6},{4,7},{9,8},{10,9},{11,1... | collective-permute-start | bytes 196616 | tf_op jit(solution)/shard_map/ppermute | solution.py:52

commit v6 on v5

--- a/solution.py
+++ b/solution.py
@@ -70,6 +70,11 @@
         compiler_params=pltpu.CompilerParams(vmem_limit_bytes=8 * MIB),
         name="stack",
     )(*parts)
+
+
+def from_all(move, value_for):
+    got = {step: move(value_for(step), step) for step in (2, 1, 3)}
+    return [got[step] for step in (1, 2, 3)]
 
 
 def dot_nt(a, b):
@@ -464,19 +469,19 @@
     request = 2 * z + x // 2
     new = lax.dynamic_slice(new_kv, (request, 0, core, 0), (1, NEW, 1, 2 * HD)).reshape(1, NEW, 2 * HD)
     ahead = split_ahead(cache, None, 0, 1)
-    line = stack([queries] + [from_first(queries, s) for s in (1, 2, 3)])
+    line = stack([queries] + from_all(from_first, lambda _: queries))
     info, valid, new, line, ahead = lax.optimization_barrier((info, valid, new, line, ahead))
-    own = [line] + [from_second(line, s) for s in (1, 2, 3)]
+    own = [line] + from_all(from_second, lambda _: line)
     ahead = split_ahead(cache, ahead, 1, AHEAD - 1)
     *own, ahead = lax.optimization_barrier((*own, ahead))
     other = [from_twin(part) for part in own]
 
     sent, mine = attend(info, valid, own, other, ahead, cache, new)
     parts = merge_twins(info, mine, from_twin(sent))
-    zs = merge_four([parts[0]] + [from_second(parts[SIDE - s], s) for s in (1, 2, 3)])
-    rows = merge_final([zs] + [from_first(zs, s) for s in (1, 2, 3)])
-
-    own = [rows] + [from_second(rows, s) for s in (1, 2, 3)]
+    zs = merge_four([parts[0]] + from_all(from_second, lambda s: parts[SIDE - s]))
+    rows = merge_final([zs] + from_all(from_first, lambda _: zs))
+
+    own = [rows] + from_all(from_second, lambda _: rows)
     other = [from_twin(part) for part in own]
     keep, *sends = project(info, own, other, out_weight)
     total = keep

time: 110 us -> 110 us (level)
  no operation moved by 1% of the time
where the time goes in v6:
time: 110 us
  Pallas kernels  45.7 us (42%)
  waiting for transfers between devices  35.8 us (33%)
  starting transfers between devices  27.5 us (25%)
    pallas_call x1, Pallas kernels, attend(): pl.pallas_call(attend_kernel, out_shape=[blocks, blocks], grid_spec=pltpu...  28.5 us
    ppermute x9, waiting for transfers between devices, from_second(): return lax.ppermute(value, 'ctx', pairs)  16.5 us
    ppermute x9, starting transfers between devices, from_second(): return lax.ppermute(value, 'ctx', pairs)  12.7 us
    pallas_call x2, Pallas kernels, split_ahead(): pl.pallas_call(ahead_kernel, grid=(count,), in_specs=[pl.BlockSpec((1, pe...  12 us
    ppermute x6, waiting for transfers between devices, from_first(): return lax.ppermute(value, 'ctx', pairs)  10.6 us
    ppermute x6, starting transfers between devices, from_first(): return lax.ppermute(value, 'ctx', pairs)  7.62 us
    ppermute x3, starting transfers between devices, from_plane(): lax.ppermute(value, 'kvh', [((s + step) % SIDE, s) for s in range(SIDE)])  5.9 us
    ppermute x9, waiting for transfers between devices, from_twin(): lax.ppermute(value, 'ctx', [(at(z, x, 1 - c), at(z, x, c)) for z, x, c in...  5.77 us
  transfers between devices with their start and end apart: 27, of which 20 were waited for; matrix products, arithmetic and copies ran while one was open for 0% of the time, Pallas kernels for 11%

profile of v6, /device:TPU:0, one launch (start us, length us, event | category | flops | bytes accessed | tf_op | source)
XLA Modules:
  0.0 109.9 jit_solution(15278172347906158097)
XLA Ops:
  0.0 2.8 %collective-permute-start = (bf16[8,4096]{1,0:T(8,128)(2,1)}, bf16[8,4096]{1,0:T(8,128)(2,1)S(1)}, u32[]{:S(2)}, u32[]{:S(2)}) collective-permute-start(bf16[8,4096]{1,0:T(8,128)(2,1)} %refs_0_.1), channel_id=1, source_target_pairs={{8,0},{36,4},{16,8},{44,12},{24,16},{52,20},{0,24},{60,28},{40,32}... | collective-permute-start | bytes 196616 | tf_op jit(solution)/shard_map/ppermute | solution.py:39
  2.8 0.8 collective-permute-start.1
  3.6 0.9 collective-permute-start.2
  4.6 4.0 %split_ahead.2.refs_0_ = bf16[4,2,2048,256]{3,2,1,0:T(8,128)(2,1)} custom-call(bf16[8,2048,2,256]{3,2,1,0:T(2,128)(2,1)} %refs_9_.1), custom_call_target="tpu_custom_call" | custom-call | bytes 8388608 | tf_op jit(solution)/shard_map/split_ahead/pallas_call | solution.py:166
  9.6 4.1 %collective-permute-start.3 = (bf16[4,8,4096]{2,1,0:T(8,128)(2,1)S(1)}, bf16[4,8,4096]{2,1,0:T(8,128)(2,1)S(1)}, u32[]{:S(2)}, u32[]{:S(2)}) collective-permute-start(bf16[4,8,4096]{2,1,0:T(8,128)(2,1)S(1)} %stack.21.refs_0_), channel_id=1, source_target_pairs={{32,0},{12,4},{40,8},{20,12},{48,16},{28,20},{56,24},{4,28},{64,32... | collective-permute-start | bytes 786440 | tf_op jit(solution)/shard_map/ppermute | solution.py:44
  13.7 1.3 %collective-permute-start.5 = (bf16[4,8,4096]{2,1,0:T(8,128)(2,1)S(1)}, bf16[4,8,4096]{2,1,0:T(8,128)(2,1)S(1)}, u32[]{:S(2)}, u32[]{:S(2)}) collective-permute-start(bf16[4,8,4096]{2,1,0:T(8,128)(2,1)S(1)} %stack.21.refs_0_), channel_id=1, source_target_pairs={{96,0},{28,4},{104,8},{4,12},{112,16},{12,20},{120,24},{20,28},{0,... | collective-permute-start | bytes 786440 | tf_op jit(solution)/shard_map/ppermute | solution.py:44
  14.9 8.1 %split_ahead.3.refs_8_ = bf16[4,2,2048,256]{3,2,1,0:T(8,128)(2,1)} custom-call(bf16[8,2048,2,256]{3,2,1,0:T(2,128)(2,1)} %refs_9_.1, bf16[4,2,2048,256]{3,2,1,0:T(8,128)(2,1)} %split_ahead.2.refs_0_), custom_call_target="tpu_custom_call", output_to_operand_aliasing={{}: (1, {})} | custom-call | bytes 25165824 | tf_op jit(solution)/shard_map/split_ahead/pallas_call | solution.py:166
  23.0 1.1 collective-permute-done.5.refs_3_
  26.7 28.5 %attend.1 = (bf16[16,16,2176]{2,1,0:T(8,128)(2,1)S(1)}, bf16[16,16,2176]{2,1,0:T(8,128)(2,1)S(1)}) custom-call(s32[4]{0:T(128)S(1)} %pad_add_fusion.info, s32[8]{0:T(128)S(1)} %subtract_clamp_fusion.valid, bf16[4,8,4096]{2,1,0:T(8,128)(2,1)S(1)} %stack.21.refs_0_, bf16[4,8,4096]{2,1,0:T(8,128)(2,1)S(1)} %collective-permute-done.3.refs_1_, ...), custom_call_target="tpu_custom_call" | custom-call | flops 8589934592 | bytes 16777216 | tf_op jit(solution)/shard_map/attend/pallas_call | solution.py:281
  55.5 2.6 %collective-permute-done.10.got = bf16[16,16,2176]{2,1,0:T(8,128)(2,1)S(1)} collective-permute-done((bf16[16,16,2176]{2,1,0:T(8,128)(2,1)S(1)}, bf16[16,16,2176]{2,1,0:T(8,128)(2,1)S(1)}, u32[]{:S(2)}, u32[]{:S(2)}) %collective-permute-start.10) | collective-permute-done | bytes 1114144 | tf_op jit(solution)/shard_map/ppermute | solution.py:48
  58.1 1.7 %merge_twins.1 = (bf16[4,16,2176]{2,1,0:T(8,128)(2,1)S(1)}, bf16[4,16,2176]{2,1,0:T(8,128)(2,1)S(1)}, bf16[4,16,2176]{2,1,0:T(8,128)(2,1)S(1)}, bf16[4,16,2176]{2,1,0:T(8,128)(2,1)S(1)}) custom-call(s32[4]{0:T(128)S(1)} %pad_add_fusion.info, bf16[16,16,2176]{2,1,0:T(8,128)(2,1)S(1)} %get-tuple-element.35.mine, ...), custom_call_target="tpu_custom_call" | custom-call | tf_op jit(solution)/shard_map/merge_twins/pallas_call | solution.py:365
  59.9 3.3 %collective-permute-start.12 = (bf16[4,16,2176]{2,1,0:T(8,128)(2,1)S(1)}, bf16[4,16,2176]{2,1,0:T(8,128)(2,1)S(1)}, u32[]{:S(2)}, u32[]{:S(2)}) collective-permute-start(bf16[4,16,2176]{2,1,0:T(8,128)(2,1)S(1)} %get-tuple-element.39), channel_id=1, source_target_pairs={{64,0},{20,4},{72,8},{28,12},{80,16},{4,20},{88,24},{12,28},{96,32... | collective-permute-start | bytes 835592 | tf_op jit(solution)/shard_map/ppermute | solution.py:44
  63.2 3.2 %collective-permute-done.11.refs_1_ = bf16[4,16,2176]{2,1,0:T(8,128)(2,1)S(1)} collective-permute-done((bf16[4,16,2176]{2,1,0:T(8,128)(2,1)S(1)}, bf16[4,16,2176]{2,1,0:T(8,128)(2,1)S(1)}, u32[]{:S(2)}, u32[]{:S(2)}) %collective-permute-start.11) | collective-permute-done | bytes 278560 | tf_op jit(solution)/shard_map/ppermute | solution.py:44
  66.4 1.6 %collective-permute-done.12.refs_2_ = bf16[4,16,2176]{2,1,0:T(8,128)(2,1)S(1)} collective-permute-done((bf16[4,16,2176]{2,1,0:T(8,128)(2,1)S(1)}, bf16[4,16,2176]{2,1,0:T(8,128)(2,1)S(1)}, u32[]{:S(2)}, u32[]{:S(2)}) %collective-permute-start.12) | collective-permute-done | bytes 278560 | tf_op jit(solution)/shard_map/ppermute | solution.py:44
  68.0 3.0 %collective-permute-done.13.refs_3_ = bf16[4,16,2176]{2,1,0:T(8,128)(2,1)S(1)} collective-permute-done((bf16[4,16,2176]{2,1,0:T(8,128)(2,1)S(1)}, bf16[4,16,2176]{2,1,0:T(8,128)(2,1)S(1)}, u32[]{:S(2)}, u32[]{:S(2)}) %collective-permute-start.13) | collective-permute-done | bytes 278560 | tf_op jit(solution)/shard_map/ppermute | solution.py:44
  71.7 1.8 %collective-permute-start.14 = (bf16[4,16,2176]{2,1,0:T(8,128)(2,1)S(1)}, bf16[4,16,2176]{2,1,0:T(8,128)(2,1)S(1)}, u32[]{:S(2)}, u32[]{:S(2)}) collective-permute-start(bf16[4,16,2176]{2,1,0:T(8,128)(2,1)S(1)} %merge_four.1.refs_0_), channel_id=1, source_target_pairs={{8,0},{36,4},{16,8},{44,12},{24,16},{52,20},{0,24},{60,28},{40,32}... | collective-permute-start | bytes 835592 | tf_op jit(solution)/shard_map/ppermute | solution.py:39
  73.5 1.3 %collective-permute-start.15 = (bf16[4,16,2176]{2,1,0:T(8,128)(2,1)S(1)}, bf16[4,16,2176]{2,1,0:T(8,128)(2,1)S(1)}, u32[]{:S(2)}, u32[]{:S(2)}) collective-permute-start(bf16[4,16,2176]{2,1,0:T(8,128)(2,1)S(1)} %merge_four.1.refs_0_), channel_id=1, source_target_pairs={{16,0},{68,4},{24,8},{76,12},{0,16},{84,20},{8,24},{92,28},{48,32}... | collective-permute-start | bytes 835592 | tf_op jit(solution)/shard_map/ppermute | solution.py:39
  74.8 5.8 %collective-permute-done.14.refs_1_ = bf16[4,16,2176]{2,1,0:T(8,128)(2,1)S(1)} collective-permute-done((bf16[4,16,2176]{2,1,0:T(8,128)(2,1)S(1)}, bf16[4,16,2176]{2,1,0:T(8,128)(2,1)S(1)}, u32[]{:S(2)}, u32[]{:S(2)}) %collective-permute-start.14) | collective-permute-done | bytes 278560 | tf_op jit(solution)/shard_map/ppermute | solution.py:39
  80.6 1.1 collective-permute-done.15.refs_2_
  81.7 2.9 %collective-permute-done.16.refs_3_ = bf16[4,16,2176]{2,1,0:T(8,128)(2,1)S(1)} collective-permute-done((bf16[4,16,2176]{2,1,0:T(8,128)(2,1)S(1)}, bf16[4,16,2176]{2,1,0:T(8,128)(2,1)S(1)}, u32[]{:S(2)}, u32[]{:S(2)}) %collective-permute-start.16) | collective-permute-done | bytes 278560 | tf_op jit(solution)/shard_map/ppermute | solution.py:39
  85.2 0.9 collective-permute-start.17
  86.1 3.0 %collective-permute-start.18 = (bf16[4,16,2048]{2,1,0:T(8,128)(2,1)S(1)}, bf16[4,16,2048]{2,1,0:T(8,128)(2,1)S(1)}, u32[]{:S(2)}, u32[]{:S(2)}) collective-permute-start(bf16[4,16,2048]{2,1,0:T(8,128)(2,1)S(1)} %merge_final.1.refs_0_), channel_id=1, source_target_pairs={{64,0},{20,4},{72,8},{28,12},{80,16},{4,20},{88,24},{12,28},{96,32... | collective-permute-start | bytes 786440 | tf_op jit(solution)/shard_map/ppermute | solution.py:44
  89.2 2.5 %collective-permute-done.17.refs_1_ = bf16[4,16,2048]{2,1,0:T(8,128)(2,1)S(1)} collective-permute-done((bf16[4,16,2048]{2,1,0:T(8,128)(2,1)S(1)}, bf16[4,16,2048]{2,1,0:T(8,128)(2,1)S(1)}, u32[]{:S(2)}, u32[]{:S(2)}) %collective-permute-start.17) | collective-permute-done | bytes 262176 | tf_op jit(solution)/shard_map/ppermute | solution.py:44
  91.7 2.3 %collective-permute-done.18.refs_2_ = bf16[4,16,2048]{2,1,0:T(8,128)(2,1)S(1)} collective-permute-done((bf16[4,16,2048]{2,1,0:T(8,128)(2,1)S(1)}, bf16[4,16,2048]{2,1,0:T(8,128)(2,1)S(1)}, u32[]{:S(2)}, u32[]{:S(2)}) %collective-permute-start.18) | collective-permute-done | bytes 262176 | tf_op jit(solution)/shard_map/ppermute | solution.py:44
  94.0 2.8 %collective-permute-done.19.refs_3_ = bf16[4,16,2048]{2,1,0:T(8,128)(2,1)S(1)} collective-permute-done((bf16[4,16,2048]{2,1,0:T(8,128)(2,1)S(1)}, bf16[4,16,2048]{2,1,0:T(8,128)(2,1)S(1)}, u32[]{:S(2)}, u32[]{:S(2)}) %collective-permute-start.19) | collective-permute-done | bytes 262176 | tf_op jit(solution)/shard_map/ppermute | solution.py:44
  96.9 1.5 %collective-permute-done.23.refs_7_ = bf16[4,16,2048]{2,1,0:T(8,128)(2,1)S(1)} collective-permute-done((bf16[4,16,2048]{2,1,0:T(8,128)(2,1)S(1)}, bf16[4,16,2048]{2,1,0:T(8,128)(2,1)S(1)}, u32[]{:S(2)}, u32[]{:S(2)}) %collective-permute-start.23) | collective-permute-done | bytes 262176 | tf_op jit(solution)/shard_map/ppermute | solution.py:48
  98.4 2.1 %project.1 = (f32[64,512]{1,0:T(8,128)S(1)}, bf16[64,512]{1,0:T(8,128)(2,1)S(1)}, bf16[64,512]{1,0:T(8,128)(2,1)S(1)}, bf16[64,512]{1,0:T(8,128)(2,1)S(1)}) custom-call(s32[4]{0:T(128)S(1)} %pad_add_fusion.info, bf16[4,16,2048]{2,1,0:T(8,128)(2,1)S(1)} %merge_final.1.refs_0_, bf16[4,16,2048]{2,1,0:T(8,128)(2,1)S(1)} %collective-permute-done.17.refs_1_, ...), custom_call_target="tpu_custom_call" | custom-call | flops 1073741824 | bytes 4194304 | tf_op jit(solution)/shard_map/project/pallas_call | solution.py:449
  100.5 1.6 %collective-permute-start.24 = (bf16[64,512]{1,0:T(8,128)(2,1)S(1)}, bf16[64,512]{1,0:T(8,128)(2,1)S(1)}, u32[]{:S(2)}, u32[]{:S(2)}) collective-permute-start(bf16[64,512]{1,0:T(8,128)(2,1)S(1)} %get-tuple-element.42), channel_id=1, source_target_pairs={{3,0},{0,1},{1,2},{2,3},{7,4},{4,5},{5,6},{6,7},{11,8},{8,9},{9,10... | collective-permute-start | bytes 196616 | tf_op jit(solution)/shard_map/ppermute | solution.py:52
  102.1 2.9 %collective-permute-start.25 = (bf16[64,512]{1,0:T(8,128)(2,1)S(1)}, bf16[64,512]{1,0:T(8,128)(2,1)S(1)}, u32[]{:S(2)}, u32[]{:S(2)}) collective-permute-start(bf16[64,512]{1,0:T(8,128)(2,1)S(1)} %get-tuple-element.43), channel_id=1, source_target_pairs={{2,0},{3,1},{0,2},{1,3},{6,4},{7,5},{4,6},{5,7},{10,8},{11,9},{8,1... | collective-permute-start | bytes 196616 | tf_op jit(solution)/shard_map/ppermute | solution.py:52
  105.0 1.3 %collective-permute-start.26 = (bf16[64,512]{1,0:T(8,128)(2,1)S(1)}, bf16[64,512]{1,0:T(8,128)(2,1)S(1)}, u32[]{:S(2)}, u32[]{:S(2)}) collective-permute-start(bf16[64,512]{1,0:T(8,128)(2,1)S(1)} %get-tuple-element.44), channel_id=1, source_target_pairs={{1,0},{2,1},{3,2},{0,3},{5,4},{6,5},{7,6},{4,7},{9,8},{10,9},{11,1... | collective-permute-start | bytes 196616 | tf_op jit(solution)/shard_map/ppermute | solution.py:52
  106.4 2.2 %collective-permute-done.25 = bf16[64,512]{1,0:T(8,128)(2,1)S(1)} collective-permute-done((bf16[64,512]{1,0:T(8,128)(2,1)S(1)}, bf16[64,512]{1,0:T(8,128)(2,1)S(1)}, u32[]{:S(2)}, u32[]{:S(2)}) %collective-permute-start.25) | collective-permute-done | bytes 65568 | tf_op jit(solution)/shard_map/ppermute | solution.py:52
  108.5 0.8 collective-permute-done.26
  (43 shorter events, 6.1 us)
Async XLA Ops:
  0.0 4.5 %copy-start = (bf16[8,32,2,256]{3,2,1,0:T(2,128)(2,1)S(1)}, bf16[8,32,2,256]{3,2,1,0:T(2,128)(2,1)}, u32[]{:S(2)}) copy-start(bf16[8,32,2,256]{3,2,1,0:T(2,128)(2,1)} %param.7) | copy-start | bytes 786436
  0.0 8.7 %collective-permute-start = (bf16[8,4096]{1,0:T(8,128)(2,1)}, bf16[8,4096]{1,0:T(8,128)(2,1)S(1)}, u32[]{:S(2)}, u32[]{:S(2)}) collective-permute-start(bf16[8,4096]{1,0:T(8,128)(2,1)} %refs_0_.1), channel_id=1, source_target_pairs={{8,0},{36,4},{16,8},{44,12},{24,16},{52,20},{0,24},{60,28},{40,32}... | collective-permute-start | bytes 196616 | tf_op jit(solution)/shard_map/ppermute | solution.py:39
  2.8 6.0 %collective-permute-start.1 = (bf16[8,4096]{1,0:T(8,128)(2,1)}, bf16[8,4096]{1,0:T(8,128)(2,1)S(1)}, u32[]{:S(2)}, u32[]{:S(2)}) collective-permute-start(bf16[8,4096]{1,0:T(8,128)(2,1)} %refs_0_.1), channel_id=1, source_target_pairs={{16,0},{68,4},{24,8},{76,12},{0,16},{84,20},{8,24},{92,28},{48,32}... | collective-permute-start | bytes 196616 | tf_op jit(solution)/shard_map/ppermute | solution.py:39
  3.6 5.9 %collective-permute-start.2 = (bf16[8,4096]{1,0:T(8,128)(2,1)}, bf16[8,4096]{1,0:T(8,128)(2,1)S(1)}, u32[]{:S(2)}, u32[]{:S(2)}) collective-permute-start(bf16[8,4096]{1,0:T(8,128)(2,1)} %refs_0_.1), channel_id=1, source_target_pairs={{24,0},{100,4},{0,8},{108,12},{8,16},{116,20},{16,24},{124,28},{56... | collective-permute-start | bytes 196616 | tf_op jit(solution)/shard_map/ppermute | solution.py:39
  4.6 4.0 %copy-start.3 = (s32[8]{0:T(128)S(1)}, s32[8]{0:T(128)}, u32[]{:S(2)}) copy-start(s32[8]{0:T(128)} %param.8) | copy-start | bytes 100
  4.6 4.9 %copy-start.2 = (bf16[8,4096]{1,0:T(8,128)(2,1)S(1)}, bf16[8,4096]{1,0:T(8,128)(2,1)}, u32[]{:S(2)}) copy-start(bf16[8,4096]{1,0:T(8,128)(2,1)} %refs_0_.1) | copy-start | bytes 196612
  9.6 13.4 %collective-permute-start.3 = (bf16[4,8,4096]{2,1,0:T(8,128)(2,1)S(1)}, bf16[4,8,4096]{2,1,0:T(8,128)(2,1)S(1)}, u32[]{:S(2)}, u32[]{:S(2)}) collective-permute-start(bf16[4,8,4096]{2,1,0:T(8,128)(2,1)S(1)} %stack.21.refs_0_), channel_id=1, source_target_pairs={{32,0},{12,4},{40,8},{20,12},{48,16},{28,20},{56,24},{4,28},{64,32... | collective-permute-start | bytes 786440 | tf_op jit(solution)/shard_map/ppermute | solution.py:44
  13.7 9.3 %collective-permute-start.4 = (bf16[4,8,4096]{2,1,0:T(8,128)(2,1)S(1)}, bf16[4,8,4096]{2,1,0:T(8,128)(2,1)S(1)}, u32[]{:S(2)}, u32[]{:S(2)}) collective-permute-start(bf16[4,8,4096]{2,1,0:T(8,128)(2,1)S(1)} %stack.21.refs_0_), channel_id=1, source_target_pairs={{64,0},{20,4},{72,8},{28,12},{80,16},{4,20},{88,24},{12,28},{96,32... | collective-permute-start | bytes 786440 | tf_op jit(solution)/shard_map/ppermute | solution.py:44
  13.7 10.4 %collective-permute-start.5 = (bf16[4,8,4096]{2,1,0:T(8,128)(2,1)S(1)}, bf16[4,8,4096]{2,1,0:T(8,128)(2,1)S(1)}, u32[]{:S(2)}, u32[]{:S(2)}) collective-permute-start(bf16[4,8,4096]{2,1,0:T(8,128)(2,1)S(1)} %stack.21.refs_0_), channel_id=1, source_target_pairs={{96,0},{28,4},{104,8},{4,12},{112,16},{12,20},{120,24},{20,28},{0,... | collective-permute-start | bytes 786440 | tf_op jit(solution)/shard_map/ppermute | solution.py:44
  24.1 1.5 %collective-permute-start.6 = (bf16[4,8,4096]{2,1,0:T(8,128)(2,1)S(1)}, bf16[4,8,4096]{2,1,0:T(8,128)(2,1)S(1)}, u32[]{:S(2)}, u32[]{:S(2)}) collective-permute-start(bf16[4,8,4096]{2,1,0:T(8,128)(2,1)S(1)} %stack.21.refs_0_), channel_id=1, source_target_pairs={{4,0},{0,4},{12,8},{8,12},{20,16},{16,20},{28,24},{24,28},{36,32},... | collective-permute-start | bytes 786440 | tf_op jit(solution)/shard_map/ppermute | solution.py:48
  24.1 1.9 %collective-permute-start.7 = (bf16[4,8,4096]{2,1,0:T(8,128)(2,1)S(1)}, bf16[4,8,4096]{2,1,0:T(8,128)(2,1)S(1)}, u32[]{:S(2)}, u32[]{:S(2)}) collective-permute-start(bf16[4,8,4096]{2,1,0:T(8,128)(2,1)S(1)} %collective-permute-done.3.refs_1_), channel_id=1, source_target_pairs={{4,0},{0,4},{12,8},{8,12},{20,16},{16,20},{28,24},{24,28},{36,32},... | collective-permute-start | bytes 786440 | tf_op jit(solution)/shard_map/ppermute | solution.py:48
  24.6 1.8 %collective-permute-start.8 = (bf16[4,8,4096]{2,1,0:T(8,128)(2,1)S(1)}, bf16[4,8,4096]{2,1,0:T(8,128)(2,1)S(1)}, u32[]{:S(2)}, u32[]{:S(2)}) collective-permute-start(bf16[4,8,4096]{2,1,0:T(8,128)(2,1)S(1)} %collective-permute-done.4.refs_2_), channel_id=1, source_target_pairs={{4,0},{0,4},{12,8},{8,12},{20,16},{16,20},{28,24},{24,28},{36,32},... | collective-permute-start | bytes 786440 | tf_op jit(solution)/shard_map/ppermute | solution.py:48
  24.6 2.1 %collective-permute-start.9 = (bf16[4,8,4096]{2,1,0:T(8,128)(2,1)S(1)}, bf16[4,8,4096]{2,1,0:T(8,128)(2,1)S(1)}, u32[]{:S(2)}, u32[]{:S(2)}) collective-permute-start(bf16[4,8,4096]{2,1,0:T(8,128)(2,1)S(1)} %collective-permute-done.5.refs_3_), channel_id=1, source_target_pairs={{4,0},{0,4},{12,8},{8,12},{20,16},{16,20},{28,24},{24,28},{36,32},... | collective-permute-start | bytes 786440 | tf_op jit(solution)/shard_map/ppermute | solution.py:48
  55.2 43.1 %copy-start.1 = (bf16[4096,512]{1,0:T(8,128)(2,1)S(1)}, bf16[4096,512]{1,0:T(8,128)(2,1)}, u32[]{:S(2)}) copy-start(bf16[4096,512]{1,0:T(8,128)(2,1)} %refs_8_.1) | copy-start | bytes 12582916
  55.3 2.8 %collective-permute-start.10 = (bf16[16,16,2176]{2,1,0:T(8,128)(2,1)S(1)}, bf16[16,16,2176]{2,1,0:T(8,128)(2,1)S(1)}, u32[]{:S(2)}, u32[]{:S(2)}) collective-permute-start(bf16[16,16,2176]{2,1,0:T(8,128)(2,1)S(1)} %get-tuple-element.36), channel_id=1, source_target_pairs={{4,0},{0,4},{12,8},{8,12},{20,16},{16,20},{28,24},{24,28},{36,32},... | collective-permute-start | bytes 3342344 | tf_op jit(solution)/shard_map/ppermute | solution.py:48
  59.8 6.6 %collective-permute-start.11 = (bf16[4,16,2176]{2,1,0:T(8,128)(2,1)S(1)}, bf16[4,16,2176]{2,1,0:T(8,128)(2,1)S(1)}, u32[]{:S(2)}, u32[]{:S(2)}) collective-permute-start(bf16[4,16,2176]{2,1,0:T(8,128)(2,1)S(1)} %get-tuple-element.38), channel_id=1, source_target_pairs={{32,0},{12,4},{40,8},{20,12},{48,16},{28,20},{56,24},{4,28},{64,32... | collective-permute-start | bytes 835592 | tf_op jit(solution)/shard_map/ppermute | solution.py:44
  59.9 8.1 %collective-permute-start.12 = (bf16[4,16,2176]{2,1,0:T(8,128)(2,1)S(1)}, bf16[4,16,2176]{2,1,0:T(8,128)(2,1)S(1)}, u32[]{:S(2)}, u32[]{:S(2)}) collective-permute-start(bf16[4,16,2176]{2,1,0:T(8,128)(2,1)S(1)} %get-tuple-element.39), channel_id=1, source_target_pairs={{64,0},{20,4},{72,8},{28,12},{80,16},{4,20},{88,24},{12,28},{96,32... | collective-permute-start | bytes 835592 | tf_op jit(solution)/shard_map/ppermute | solution.py:44
  63.2 7.8 %collective-permute-start.13 = (bf16[4,16,2176]{2,1,0:T(8,128)(2,1)S(1)}, bf16[4,16,2176]{2,1,0:T(8,128)(2,1)S(1)}, u32[]{:S(2)}, u32[]{:S(2)}) collective-permute-start(bf16[4,16,2176]{2,1,0:T(8,128)(2,1)S(1)} %get-tuple-element.40), channel_id=1, source_target_pairs={{96,0},{28,4},{104,8},{4,12},{112,16},{12,20},{120,24},{20,28},{0,... | collective-permute-start | bytes 835592 | tf_op jit(solution)/shard_map/ppermute | solution.py:44
  71.7 8.9 %collective-permute-start.14 = (bf16[4,16,2176]{2,1,0:T(8,128)(2,1)S(1)}, bf16[4,16,2176]{2,1,0:T(8,128)(2,1)S(1)}, u32[]{:S(2)}, u32[]{:S(2)}) collective-permute-start(bf16[4,16,2176]{2,1,0:T(8,128)(2,1)S(1)} %merge_four.1.refs_0_), channel_id=1, source_target_pairs={{8,0},{36,4},{16,8},{44,12},{24,16},{52,20},{0,24},{60,28},{40,32}... | collective-permute-start | bytes 835592 | tf_op jit(solution)/shard_map/ppermute | solution.py:39
  73.5 8.2 %collective-permute-start.15 = (bf16[4,16,2176]{2,1,0:T(8,128)(2,1)S(1)}, bf16[4,16,2176]{2,1,0:T(8,128)(2,1)S(1)}, u32[]{:S(2)}, u32[]{:S(2)}) collective-permute-start(bf16[4,16,2176]{2,1,0:T(8,128)(2,1)S(1)} %merge_four.1.refs_0_), channel_id=1, source_target_pairs={{16,0},{68,4},{24,8},{76,12},{0,16},{84,20},{8,24},{92,28},{48,32}... | collective-permute-start | bytes 835592 | tf_op jit(solution)/shard_map/ppermute | solution.py:39
  74.8 9.8 %collective-permute-start.16 = (bf16[4,16,2176]{2,1,0:T(8,128)(2,1)S(1)}, bf16[4,16,2176]{2,1,0:T(8,128)(2,1)S(1)}, u32[]{:S(2)}, u32[]{:S(2)}) collective-permute-start(bf16[4,16,2176]{2,1,0:T(8,128)(2,1)S(1)} %merge_four.1.refs_0_), channel_id=1, source_target_pairs={{24,0},{100,4},{0,8},{108,12},{8,16},{116,20},{16,24},{124,28},{56... | collective-permute-start | bytes 835592 | tf_op jit(solution)/shard_map/ppermute | solution.py:39
  85.2 6.4 %collective-permute-start.17 = (bf16[4,16,2048]{2,1,0:T(8,128)(2,1)S(1)}, bf16[4,16,2048]{2,1,0:T(8,128)(2,1)S(1)}, u32[]{:S(2)}, u32[]{:S(2)}) collective-permute-start(bf16[4,16,2048]{2,1,0:T(8,128)(2,1)S(1)} %merge_final.1.refs_0_), channel_id=1, source_target_pairs={{32,0},{12,4},{40,8},{20,12},{48,16},{28,20},{56,24},{4,28},{64,32... | collective-permute-start | bytes 786440 | tf_op jit(solution)/shard_map/ppermute | solution.py:44
  86.1 7.9 %collective-permute-start.18 = (bf16[4,16,2048]{2,1,0:T(8,128)(2,1)S(1)}, bf16[4,16,2048]{2,1,0:T(8,128)(2,1)S(1)}, u32[]{:S(2)}, u32[]{:S(2)}) collective-permute-start(bf16[4,16,2048]{2,1,0:T(8,128)(2,1)S(1)} %merge_final.1.refs_0_), channel_id=1, source_target_pairs={{64,0},{20,4},{72,8},{28,12},{80,16},{4,20},{88,24},{12,28},{96,32... | collective-permute-start | bytes 786440 | tf_op jit(solution)/shard_map/ppermute | solution.py:44
  89.2 7.6 %collective-permute-start.19 = (bf16[4,16,2048]{2,1,0:T(8,128)(2,1)S(1)}, bf16[4,16,2048]{2,1,0:T(8,128)(2,1)S(1)}, u32[]{:S(2)}, u32[]{:S(2)}) collective-permute-start(bf16[4,16,2048]{2,1,0:T(8,128)(2,1)S(1)} %merge_final.1.refs_0_), channel_id=1, source_target_pairs={{96,0},{28,4},{104,8},{4,12},{112,16},{12,20},{120,24},{20,28},{0,... | collective-permute-start | bytes 786440 | tf_op jit(solution)/shard_map/ppermute | solution.py:44
  89.2 7.6 %collective-permute-start.20 = (bf16[4,16,2048]{2,1,0:T(8,128)(2,1)S(1)}, bf16[4,16,2048]{2,1,0:T(8,128)(2,1)S(1)}, u32[]{:S(2)}, u32[]{:S(2)}) collective-permute-start(bf16[4,16,2048]{2,1,0:T(8,128)(2,1)S(1)} %merge_final.1.refs_0_), channel_id=1, source_target_pairs={{4,0},{0,4},{12,8},{8,12},{20,16},{16,20},{28,24},{24,28},{36,32},... | collective-permute-start | bytes 786440 | tf_op jit(solution)/shard_map/ppermute | solution.py:48
  91.7 5.2 %collective-permute-start.21 = (bf16[4,16,2048]{2,1,0:T(8,128)(2,1)S(1)}, bf16[4,16,2048]{2,1,0:T(8,128)(2,1)S(1)}, u32[]{:S(2)}, u32[]{:S(2)}) collective-permute-start(bf16[4,16,2048]{2,1,0:T(8,128)(2,1)S(1)} %collective-permute-done.17.refs_1_), channel_id=1, source_target_pairs={{4,0},{0,4},{12,8},{8,12},{20,16},{16,20},{28,24},{24,28},{36,32},... | collective-permute-start | bytes 786440 | tf_op jit(solution)/shard_map/ppermute | solution.py:48
  94.0 2.8 %collective-permute-start.22 = (bf16[4,16,2048]{2,1,0:T(8,128)(2,1)S(1)}, bf16[4,16,2048]{2,1,0:T(8,128)(2,1)S(1)}, u32[]{:S(2)}, u32[]{:S(2)}) collective-permute-start(bf16[4,16,2048]{2,1,0:T(8,128)(2,1)S(1)} %collective-permute-done.18.refs_2_), channel_id=1, source_target_pairs={{4,0},{0,4},{12,8},{8,12},{20,16},{16,20},{28,24},{24,28},{36,32},... | collective-permute-start | bytes 786440 | tf_op jit(solution)/shard_map/ppermute | solution.py:48
  96.8 1.5 %collective-permute-start.23 = (bf16[4,16,2048]{2,1,0:T(8,128)(2,1)S(1)}, bf16[4,16,2048]{2,1,0:T(8,128)(2,1)S(1)}, u32[]{:S(2)}, u32[]{:S(2)}) collective-permute-start(bf16[4,16,2048]{2,1,0:T(8,128)(2,1)S(1)} %collective-permute-done.19.refs_3_), channel_id=1, source_target_pairs={{4,0},{0,4},{12,8},{8,12},{20,16},{16,20},{28,24},{24,28},{36,32},... | collective-permute-start | bytes 786440 | tf_op jit(solution)/shard_map/ppermute | solution.py:48
  100.5 5.9 %collective-permute-start.24 = (bf16[64,512]{1,0:T(8,128)(2,1)S(1)}, bf16[64,512]{1,0:T(8,128)(2,1)S(1)}, u32[]{:S(2)}, u32[]{:S(2)}) collective-permute-start(bf16[64,512]{1,0:T(8,128)(2,1)S(1)} %get-tuple-element.42), channel_id=1, source_target_pairs={{3,0},{0,1},{1,2},{2,3},{7,4},{4,5},{5,6},{6,7},{11,8},{8,9},{9,10... | collective-permute-start | bytes 196616 | tf_op jit(solution)/shard_map/ppermute | solution.py:52
  102.1 6.4 %collective-permute-start.25 = (bf16[64,512]{1,0:T(8,128)(2,1)S(1)}, bf16[64,512]{1,0:T(8,128)(2,1)S(1)}, u32[]{:S(2)}, u32[]{:S(2)}) collective-permute-start(bf16[64,512]{1,0:T(8,128)(2,1)S(1)} %get-tuple-element.43), channel_id=1, source_target_pairs={{2,0},{3,1},{0,2},{1,3},{6,4},{7,5},{4,6},{5,7},{10,8},{11,9},{8,1... | collective-permute-start | bytes 196616 | tf_op jit(solution)/shard_map/ppermute | solution.py:52
  105.0 4.3 %collective-permute-start.26 = (bf16[64,512]{1,0:T(8,128)(2,1)S(1)}, bf16[64,512]{1,0:T(8,128)(2,1)S(1)}, u32[]{:S(2)}, u32[]{:S(2)}) collective-permute-start(bf16[64,512]{1,0:T(8,128)(2,1)S(1)} %get-tuple-element.44), channel_id=1, source_target_pairs={{1,0},{2,1},{3,2},{0,3},{5,4},{6,5},{7,6},{4,7},{9,8},{10,9},{11,1... | collective-permute-start | bytes 196616 | tf_op jit(solution)/shard_map/ppermute | solution.py:52
